TPU v7x, 32 devices: a whole 2x2x4 slice. The times are simulated.
32 devices in a mesh: groups: 2 (over x), agent: 8 (over z, y), tm: 2 (over core).
Axes of the slice: x: 2, y: 2, z: 4, core: 2. Of those that a mesh axis runs over, the one named last changes fastest.
Arguments:
- embedded: bfloat16 [64, 1024, 512], P(('groups', 'tm'), 'agent'), parts along dimension 0, may hold values from -6 to 6
- block_lists: int32 [16, 32, 2], P(('groups', 'agent'), 'tm'), parts along dimension 0, may hold values from 0 to 7, all different within a row; in each aligned block of 16 rows (0 to 15, 16 to 31, ..., all dimensions but the last counted through in order) at most 8 rows name the same one
- done_flags: int32 [64, 1024], P(('groups', 'tm'), 'agent'), parts along dimension 0, may hold values 0 or 1
- rewards: float32 [64, 1024], P(('groups', 'tm'), 'agent'), parts along dimension 0, may hold values from -1.2 to 1.2
- bootstrap: float32 [2048], P(('groups', 'agent')), parts along dimension 0, may hold values from -6 to 6
- agent_proj: bfloat16 [512, 1536], replicated, may hold values from -2 to 2
- agent_merge: bfloat16 [512, 512], replicated, may hold values from -0.75 to 0.75
- time_proj: bfloat16 [512, 1536], replicated, may hold values from -2 to 2
- time_merge: bfloat16 [512, 512], replicated, may hold values from -0.75 to 0.75
- value_weight: float32 [512], replicated, may hold values from -0.25 to 0.25
Outputs:
- values: float32 [64, 1024], P(('groups', 'tm'), 'agent'), parts along dimension 0
- advantages: float32 [64, 1024], P(('groups', 'tm'), 'agent'), parts along dimension 0
There are 2 independent parts, one for each index of `groups`. A program takes and returns all parts, laid end to end along the dimension named above; an argument that names none is the same for every part. Nothing has to cross between parts.
Inputs may be any that keep to these rules, and one draw needn't show every extreme that they name: `block_lists`: each row names 2 different agent blocks. Within the 16 rows of one block along the second dimension no agent block is named more than 8 times, and some agent block is named exactly 8 times.
All inputs are finite; a program needn't handle non-finite values. No bound on the sum of `done_flags` on one device may be relied on, other than what follows from the above.
Results may differ from a plain program's by a relative error of at most 0.0085.
Values may be sent and summed in bfloat16 or wider, within the bound.
No kernel may reach another device: no remote copies, remote signals or barrier semaphores. Data moves between devices by JAX's collectives and lax.ppermute only.
A program may use at most 128 MiB of HBM per device.

v0:
```python
import math

import jax
import jax.numpy as jnp
from jax import lax
from jax.sharding import PartitionSpec as P

HEADS = 8
WINDOW = 16


discount = 0.9997
trace_decay = 0.995
epsilon = 1e-06


def from_behind(value, axis, by):
    devices = lax.axis_size(axis)
    pairs = [(i, i + by) for i in range(devices) if 0 <= i + by < devices]
    return lax.ppermute(value, axis, pairs)


def entering(value, axis, join, neutral):
    count, mine = (lax.axis_size(axis), lax.axis_index(axis))
    pieces = jax.tree.map(lambda part: lax.all_gather(part, axis), value)
    pieces = jax.tree.map(lambda part: part[::-1], pieces)
    mine = count - 1 - mine
    running = jax.tree.map(
        lambda part, zero: jnp.full_like(part, 0) + jnp.asarray(zero, part.dtype), value, neutral
    )

    def hop(position, running):
        longer = join(running, jax.tree.map(lambda part: part[position], pieces))
        return jax.tree.map(lambda new, old: jnp.where(position < mine, new, old), longer, running)

    return lax.fori_loop(0, count - 1, hop, running)


def rms_norm(values):
    return values * lax.rsqrt(jnp.mean(values * values, axis=-1, keepdims=True) + epsilon)


def softmax_rows(scores):
    shifted = scores - jnp.max(scores, axis=-1, keepdims=True)
    exponent = jnp.exp(shifted)
    return exponent / jnp.sum(exponent, axis=-1, keepdims=True)


def suffix_pass(changes, factors, inject):
    agents_here = changes.shape[1]

    def backward(running, inputs):
        change, factor, injected = inputs
        advance = change + factor * running[0]
        through = factor * running[1]
        from_value = injected + factor * running[2]
        return ((advance, through, from_value), (advance, through, from_value))

    start_state = (
        jnp.zeros((agents_here,), jnp.float32),
        jnp.ones((agents_here,), jnp.float32),
        jnp.zeros((agents_here,), jnp.float32),
    )
    final_state, outputs = lax.scan(backward, start_state, (changes, factors, inject), reverse=True)
    return outputs


def compose_split(earlier, later):
    return (later[0] + later[1] * earlier[0], later[1] * earlier[1])


def body(
    embedded,
    block_lists,
    done_flags,
    rewards,
    bootstrap,
    agent_proj,
    agent_merge,
    time_proj,
    time_merge,
    value_weight,
):
    steps_here, agents_here, model_width = embedded.shape
    list_length = block_lists.shape[2]
    head_size = model_width // HEADS
    window = WINDOW
    score_scale = head_size ** (-0.5)
    tokens = steps_here * agents_here
    blocks_count = lax.axis_size("agent")
    capacity = max(2, (2 * steps_here * list_length + blocks_count - 1) // blocks_count)
    residual = embedded.astype(jnp.float32).reshape(tokens, model_width)
    normed = rms_norm(residual).astype(jnp.bfloat16)
    projected = jnp.dot(normed, agent_proj, preferred_element_type=jnp.float32).astype(jnp.bfloat16)
    projected = projected.reshape(steps_here, agents_here, 3 * model_width)
    queries = projected[:, :, :model_width]
    keyvals = projected[:, :, model_width:]
    listed_peers = block_lists[0].reshape(-1)
    row_count = listed_peers.shape[0]
    row_steps = jnp.arange(row_count, dtype=jnp.int32) // list_length
    peer_hits = (
        listed_peers[:, None] == jnp.arange(blocks_count, dtype=jnp.int32)[None, :]
    ).astype(jnp.int32)
    earlier = jnp.cumsum(peer_hits, axis=0) - peer_hits
    slot_index = jnp.sum(earlier * peer_hits, axis=1)
    slot_hits = (slot_index[:, None] == jnp.arange(capacity, dtype=jnp.int32)[None, :]).astype(
        jnp.int32
    )
    requests = (
        jnp.einsum(
            "rp,rc->pc",
            peer_hits * (row_steps[:, None] + 1),
            slot_hits,
            preferred_element_type=jnp.int32,
        )
        - 1
    )
    wanted = lax.all_to_all(requests, "agent", split_axis=0, concat_axis=0, tiled=True)
    chosen = jnp.maximum(wanted, 0).reshape(-1)
    positions = listed_peers * capacity + slot_index
    outgoing = normed.reshape(steps_here, agents_here, model_width)[chosen]
    outgoing = outgoing.reshape(blocks_count, capacity, agents_here, model_width)
    arrived = lax.all_to_all(outgoing, "agent", split_axis=0, concat_axis=0, tiled=True)
    listed_rows = arrived.reshape(blocks_count * capacity, agents_here, model_width)[positions]
    listed = jnp.dot(
        listed_rows.reshape(-1, model_width),
        agent_proj[:, model_width:],
        preferred_element_type=jnp.float32,
    ).astype(jnp.bfloat16)
    listed = listed.reshape(steps_here, list_length * agents_here, 2 * model_width)
    step_group = math.gcd(steps_here, max(1, 512 // agents_here))
    group_count = steps_here // step_group
    all_keys = jnp.concatenate([keyvals, listed], axis=1).reshape(
        group_count, step_group, -1, 2, HEADS, head_size
    )
    query_heads = queries.reshape(group_count, step_group, agents_here, HEADS, head_size)

    def agent_group(inputs):
        query_part, key_part = inputs
        scores = (
            jnp.einsum(
                "tqhe,tkhe->thqk", query_part, key_part[:, :, 0], preferred_element_type=jnp.float32
            )
            * score_scale
        )
        attention = softmax_rows(scores).astype(jnp.bfloat16)
        return jnp.einsum(
            "thqk,tkhe->tqhe", attention, key_part[:, :, 1], preferred_element_type=jnp.float32
        ).astype(jnp.bfloat16)

    attended = lax.map(agent_group, (query_heads, all_keys))
    residual = residual + jnp.dot(
        attended.reshape(tokens, model_width), agent_merge, preferred_element_type=jnp.float32
    )
    normed = rms_norm(residual).astype(jnp.bfloat16)
    projected = jnp.dot(normed, time_proj, preferred_element_type=jnp.float32).astype(jnp.bfloat16)
    projected = projected.reshape(steps_here, agents_here, 3 * model_width)
    time_keys = projected[:, :, model_width:]
    rim_keys = from_behind(time_keys, "tm", 1)
    padded = jnp.concatenate([rim_keys, time_keys], axis=0)
    block_count = steps_here // window
    previous = padded[:steps_here].reshape(block_count, window, agents_here, 2, HEADS, head_size)
    current = padded[window:].reshape(block_count, window, agents_here, 2, HEADS, head_size)
    key_blocks = jnp.concatenate([previous, current], axis=1)
    query_blocks = projected[:, :, :model_width].reshape(
        block_count, window, agents_here, HEADS, head_size
    )
    offset = lax.axis_index("tm") * steps_here
    block_starts = offset + jnp.arange(block_count, dtype=jnp.int32) * window
    query_step = block_starts[:, None] + jnp.arange(window, dtype=jnp.int32)[None, :]
    key_step = block_starts[:, None] - window + jnp.arange(2 * window, dtype=jnp.int32)[None, :]
    allowed = (
        (key_step[:, None, :] <= query_step[:, :, None])
        & (key_step[:, None, :] > query_step[:, :, None] - window)
        & (key_step[:, None, :] >= 0)
    )
    scores = (
        jnp.einsum(
            "bqahe,bkahe->bahqk",
            query_blocks,
            key_blocks[:, :, :, 0],
            preferred_element_type=jnp.float32,
        )
        * score_scale
    )
    scores = jnp.where(allowed[:, None, None], scores, -1e30)
    attention = softmax_rows(scores).astype(jnp.bfloat16)
    attended = jnp.einsum(
        "bahqk,bkahe->bqahe", attention, key_blocks[:, :, :, 1], preferred_element_type=jnp.float32
    ).astype(jnp.bfloat16)
    residual = residual + jnp.dot(
        attended.reshape(tokens, model_width), time_merge, preferred_element_type=jnp.float32
    )
    values = jnp.sum(rms_norm(residual) * value_weight, axis=-1).reshape(steps_here, agents_here)
    living = 1.0 - done_flags.astype(jnp.float32)
    factors = discount * trace_decay * living
    last_block = lax.axis_index("tm") == lax.axis_size("tm") - 1
    arriving = from_behind(values[0], "tm", -1)
    following_last = jnp.where(last_block, bootstrap, arriving)
    following = jnp.concatenate([values[1:], following_last[None, :]], axis=0)
    changes = rewards + discount * living * following - values
    inject = jnp.zeros((steps_here, agents_here), jnp.float32)
    local_adv, gains_adv, gains_val = suffix_pass(changes, factors, inject)
    element = (local_adv[0], gains_adv[0])
    identity = (jnp.zeros((agents_here,), jnp.float32), jnp.ones((agents_here,), jnp.float32))
    carried = entering(element, "tm", compose_split, identity)
    advantages = local_adv + gains_adv * carried[0][None, :]
    return (values, advantages)


def solution(mesh):
    placed = (
        P(("groups", "tm"), "agent", None),
        P(("groups", "agent"), "tm", None),
        P(("groups", "tm"), "agent"),
        P(("groups", "tm"), "agent"),
        P(("groups", "agent")),
        P(),
        P(),
        P(),
        P(),
        P(),
    )
    return jax.shard_map(
        body,
        mesh=mesh,
        in_specs=placed,
        out_specs=(P(("groups", "tm"), "agent"), P(("groups", "tm"), "agent")),
        check_vma=False,
    )
```

profile of v0, /device:TPU:0, one launch (start us, length us, event | category | flops | bytes accessed | tf_op | source)
XLA Modules:
  0.0 488.0 jit_solution(13060431496737885862)
XLA Ops:
  2.8 7.3 %all-to-all-start = ((s32[8,1,8]{2,1,0:T(1,128)}), s32[8,1,8]{2,1,0:T(1,128)S(1)}, u32[]{:S(2)}, u32[]{:S(2)}) async-start(s32[8,1,8]{2,1,0:T(1,128)} %bitcast.11), calls=%async_computation | async-start | bytes 8192 | tf_op jit(solution)/shard_map/all_to_all | solution.py:118
  16.6 7.0 %gather_fusion = bf16[64,128,512]{2,1,0:T(8,128)(2,1)} fusion(bf16[16,128,512]{2,1,0:T(8,128)(2,1)} %multiply_convert_fusion.1, s32[1024]{0:T(1024)S(1)} %pad_clamp_fusion.1), kind=kCustom, calls=%fused_computation | custom fusion | bytes 16777472 | tf_op jit(solution)/shard_map/gather | solution.py:121
  23.6 5.3 %all-to-all-start.1 = ((bf16[8,8,128,512]{3,2,1,0:T(8,128)(2,1)}), bf16[8,8,128,512]{3,2,1,0:T(8,128)(2,1)}, u32[]{:S(2)}, u32[]{:S(2)}) async-start(bf16[8,8,128,512]{3,2,1,0:T(8,128)(2,1)} %bitcast.112), calls=%async_computation.1 | async-start | bytes 16777216 | tf_op jit(solution)/shard_map/all_to_all | solution.py:123
  28.9 4.2 copy.48
  33.1 5.9 %convolution_convert_fusion.2 = bf16[2048,1536]{1,0:T(8,128)(2,1)S(1)} fusion(bf16[512,1536]{1,0:T(8,128)(2,1)S(1)} %copy-done.14, f32[2048,512]{0,1:T(8,128)} %copy.48, f32[2048]{0:T(1024)S(1)} %get-tuple-element.245), kind=kOutput, calls=%fused_computation.45 | convolution fusion | flops 3226468352 | bytes 12066816 | tf_op jit(solution)/shard_map/dot_general | solution.py:94
  43.2 6.4 %copy.52 = bf16[16,128,1024]{1,2,0:T(8,128)(2,1)} copy(bf16[16,128,1024]{2,1,0:T(8,128)(2,1)} %slice.75) | data formatting | bytes 8388608
  49.6 7.7 %copy.38 = bf16[4,4,128,2,8,64]{2,1,0,5,4,3:T(4,128)(2,1)} copy(bf16[4,4,128,2,8,64]{2,5,4,3,1,0:T(8,128)(2,1)} %bitcast.115) | data formatting | bytes 8388608 | tf_op jit(solution)/shard_map/concatenate | solution.py:133
  57.3 3.9 copy.39
  61.3 150.1 %all-to-all-done.1 = bf16[8,8,128,512]{3,2,1,0:T(8,128)(2,1)} async-done(((bf16[8,8,128,512]{3,2,1,0:T(8,128)(2,1)}), bf16[8,8,128,512]{3,2,1,0:T(8,128)(2,1)}, u32[]{:S(2)}, u32[]{:S(2)}) %all-to-all-start.1) | async-done | bytes 8388640 | tf_op jit(solution)/shard_map/all_to_all | solution.py:123
  211.4 6.2 %gather_fusion.1 = bf16[32,128,512]{2,1,0:T(8,128)(2,1)} fusion(bf16[64,128,512]{2,1,0:T(8,128)(2,1)} %bitcast.13, s32[1024]{0:T(1024)S(1)} %pad_clamp_fusion), kind=kCustom, calls=%fused_computation.1 | custom fusion | bytes 8388736 | tf_op jit(solution)/shard_map/gather | solution.py:124
  217.5 9.0 %convolution_convert_fusion.1 = bf16[4096,1024]{1,0:T(8,128)(2,1)} fusion(bf16[4096,512]{1,0:T(8,128)(2,1)} %bitcast.123, bf16[512,1536]{1,0:T(8,128)(2,1)S(1)} %copy-done.14), kind=kOutput, calls=%fused_computation.44 | convolution fusion | flops 4299161600 | bytes 13631488 | tf_op jit(solution)/shard_map/dot_general | solution.py:125
  226.5 11.3 %copy.37 = bf16[4096,1024]{0,1:T(8,128)(2,1)} copy(bf16[4096,1024]{1,0:T(8,128)(2,1)} %convolution_convert_fusion.1) | data formatting | bytes 16777216 | tf_op jit(solution)/shard_map/convert_element_type | solution.py:129
  237.8 14.6 %concatenate.15 = bf16[4,4,256,2,8,64]{2,1,0,5,4,3:T(4,128)(2,1)} reshape(bf16[4096,1024]{0,1:T(8,128)(2,1)} %copy.37) | data formatting | bytes 16777216 | tf_op jit(solution)/shard_map/concatenate | solution.py:133
  252.4 9.5 %pad_maximum_fusion = bf16[4,4,384,2,8,64]{2,1,0,5,4,3:T(4,128)(2,1)} fusion(bf16[4,4,256,2,8,64]{2,1,0,5,4,3:T(4,128)(2,1)} %concatenate.15, bf16[4,4,128,2,8,64]{2,1,0,5,4,3:T(4,128)(2,1)} %copy.38), kind=kLoop, calls=%fused_computation.32 | loop fusion | flops 25165824 | bytes 25165824 | tf_op jit(solution)/shard_map/concatenate | solution.py:133
  261.9 104.3 %while.36 = (s32[]{:T(128)}, bf16[4,4,128,8,64]{2,1,0,4,3:T(4,128)(2,1)}, bf16[4,4,384,2,8,64]{2,1,0,5,4,3:T(4,128)(2,1)}, bf16[4,4,128,8,64]{2,4,3,1,0:T(8,128)(2,1)}, s32[]{:T(128)}) while((s32[]{:T(128)}, bf16[4,4,128,8,64]{2,1,0,4,3:T(4,128)(2,1)}, bf16[4,4,384,2,8,64]{2,1,0,5,4,3:T(4,128)(2,1)}, bf16[4,4,128,8,64]{2,4,3,1,0:T(8,128)(2,1)}, ...), condition=%wide.region_6.7_spmd, body=%wide.region_3.6_spmd.sunk | while | flops 417075968 | bytes 80774264 | solution.py:151
  274.5 12.5 %fusion.83 = bf16[1,4,128,8,64]{2,4,3,1,0:T(8,128)(2,1)S(1)} fusion(f32[4,8,128]{2,1,0:T(8,128)S(1)} %fusion.82, bf16[4,384,2,8,64]{1,4,3,0,2:T(8,128)(2,1)} %bitcast.111, f32[4,8,128,384]{3,2,1,0:T(8,128)} %copy-done.2), kind=kOutput, calls=%fused_computation.14.clone.1 | convolution fusion | flops 209457536 | bytes 14696448 | tf_op jit(solution)/shard_map/while/body/eval_jaxpr/thqk,tkhe->tqhe/dot_general | solution.py:147
  300.4 12.5 %fusion.83 = bf16[1,4,128,8,64]{2,4,3,1,0:T(8,128)(2,1)S(1)} fusion(f32[4,8,128]{2,1,0:T(8,128)S(1)} %fusion.82, bf16[4,384,2,8,64]{1,4,3,0,2:T(8,128)(2,1)} %bitcast.111, f32[4,8,128,384]{3,2,1,0:T(8,128)} %copy-done.2), kind=kOutput, calls=%fused_computation.14.clone.1 | convolution fusion | flops 209457536 | bytes 14696448 | tf_op jit(solution)/shard_map/while/body/eval_jaxpr/thqk,tkhe->tqhe/dot_general | solution.py:147
  326.4 12.5 %fusion.83 = bf16[1,4,128,8,64]{2,4,3,1,0:T(8,128)(2,1)S(1)} fusion(f32[4,8,128]{2,1,0:T(8,128)S(1)} %fusion.82, bf16[4,384,2,8,64]{1,4,3,0,2:T(8,128)(2,1)} %bitcast.111, f32[4,8,128,384]{3,2,1,0:T(8,128)} %copy-done.2), kind=kOutput, calls=%fused_computation.14.clone.1 | convolution fusion | flops 209457536 | bytes 14696448 | tf_op jit(solution)/shard_map/while/body/eval_jaxpr/thqk,tkhe->tqhe/dot_general | solution.py:147
  352.4 12.5 %fusion.83 = bf16[1,4,128,8,64]{2,4,3,1,0:T(8,128)(2,1)S(1)} fusion(f32[4,8,128]{2,1,0:T(8,128)S(1)} %fusion.82, bf16[4,384,2,8,64]{1,4,3,0,2:T(8,128)(2,1)} %bitcast.111, f32[4,8,128,384]{3,2,1,0:T(8,128)} %copy-done.2), kind=kOutput, calls=%fused_computation.14.clone.1 | convolution fusion | flops 209457536 | bytes 14696448 | tf_op jit(solution)/shard_map/while/body/eval_jaxpr/thqk,tkhe->tqhe/dot_general | solution.py:147
  366.2 4.5 reshape.335
  370.7 4.2 multiply_reduce_fusion.3
  375.0 3.9 convolution_convert_fusion
  384.1 6.4 %copy.54 = bf16[16,128,1024]{1,2,0:T(8,128)(2,1)} copy(bf16[16,128,1024]{2,1,0:T(8,128)(2,1)} %slice.78) | data formatting | bytes 8388608
  396.9 13.0 %copy.44 = bf16[1,16,128,2,8,64]{5,1,4,2,3,0:T(8,128)(2,1)} copy(bf16[1,16,128,2,8,64]{2,5,4,3,1,0:T(8,128)(2,1)} %bitcast.114) | data formatting | bytes 8388608 | tf_op jit(solution)/shard_map/reshape | solution.py:163
  409.9 3.9 copy.53
  413.8 7.5 %copy.46 = bf16[16,128,8,64]{3,0,2,1:T(8,128)(2,1)} copy(bf16[16,128,8,64]{1,3,2,0:T(8,128)(2,1)} %bitcast.118) | data formatting | bytes 4194304 | tf_op jit(solution)/shard_map/reshape.8
  421.3 13.0 %copy.43 = bf16[1,16,128,2,8,64]{5,1,4,2,3,0:T(8,128)(2,1)} copy(bf16[1,16,128,2,8,64]{2,5,4,3,1,0:T(8,128)(2,1)} %bitcast.19) | data formatting | bytes 8388608 | tf_op jit(solution)/shard_map/reshape | solution.py:162
  434.3 12.3 %fusion.26 = f32[128,8,16,32]{3,2,1,0:T(8,128)} fusion(bf16[16,128,8,64]{3,0,2,1:T(8,128)(2,1)} %copy.46, bf16[1,16,128,2,8,64]{5,1,4,2,3,0:T(8,128)(2,1)} %copy.43, bf16[1,16,128,2,8,64]{5,1,4,2,3,0:T(8,128)(2,1)} %copy.44), kind=kOutput, calls=%fused_computation.35 | convolution fusion | flops 75497472 | bytes 12582912 | tf_op jit(solution)/shard_map/bqahe,bkahe->bahqk/dot_general | solution.py:178
  446.6 11.8 %fusion.65 = (f32[128,8,16]{2,1,0:T(8,128)S(1)}, f32[128,8,16,32]{3,2,1,0:T(8,128)}) fusion(f32[128,8,16,32]{3,2,1,0:T(8,128)} %fusion.26, pred[16,32]{1,0:T(8,128)(4,1)S(1)} %and_and_fusion), kind=kOutput, calls=%fused_computation.118 | output fusion | flops 3145759 | bytes 4260352 | tf_op jit(solution)/shard_map/sub | solution.py:44
  458.4 7.3 %convert_bitcast_fusion = bf16[1,16,128,8,64]{4,1,3,2,0:T(8,128)(2,1)} fusion(bf16[1,16,128,2,8,64]{5,1,4,2,3,0:T(8,128)(2,1)} %copy.44, bf16[1,16,128,2,8,64]{5,1,4,2,3,0:T(8,128)(2,1)S(1)} %copy-done.4, f32[128,8,16,32]{3,2,1,0:T(8,128)} %get-tuple-element.250, f32[128,8,16]{2,1,0:T(8,128)S(1)} %get-tuple-element.249), kind=kOutput, calls=%fused_computation.49 | convolution fusion | flops 77594624 | bytes 12648448 | tf_op jit(solution)/shard_map/bahqk,bkahe->bqahe/dot_general | solution.py:188
  465.7 8.1 %copy.47 = bf16[1,16,128,8,64]{2,1,4,3,0:T(8,128)(2,1)} copy(bf16[1,16,128,8,64]{4,1,3,2,0:T(8,128)(2,1)} %convert_bitcast_fusion) | data formatting | bytes 4194304 | tf_op jit(solution)/shard_map/convert_element_type | solution.py:190
  473.8 4.3 multiply_reduce_fusion.2
  (160 shorter events, 89.0 us)
Async XLA Ops:
  0.6 374.4 %copy-start = (bf16[512,1536]{1,0:T(8,128)(2,1)S(1)}, bf16[512,1536]{1,0:T(8,128)(2,1)}, u32[]{:S(2)}) copy-start(bf16[512,1536]{1,0:T(8,128)(2,1)} %param.21) | copy-start | bytes 4718596
  2.8 13.7 %all-to-all-start = ((s32[8,1,8]{2,1,0:T(1,128)}), s32[8,1,8]{2,1,0:T(1,128)S(1)}, u32[]{:S(2)}, u32[]{:S(2)}) async-start(s32[8,1,8]{2,1,0:T(1,128)} %bitcast.11), calls=%async_computation | async-start | bytes 8192 | tf_op jit(solution)/shard_map/all_to_all | solution.py:118
  23.6 187.8 %all-to-all-start.1 = ((bf16[8,8,128,512]{3,2,1,0:T(8,128)(2,1)}), bf16[8,8,128,512]{3,2,1,0:T(8,128)(2,1)}, u32[]{:S(2)}, u32[]{:S(2)}) async-start(bf16[8,8,128,512]{3,2,1,0:T(8,128)(2,1)} %bitcast.112), calls=%async_computation.1 | async-start | bytes 16777216 | tf_op jit(solution)/shard_map/all_to_all | solution.py:123
  28.8 4.3 copy-start.14
  41.5 1.5 copy-start.11
  266.1 1.7 copy-start.1
  269.8 2.6 copy-start.2
  292.0 1.7 copy-start.1
  295.7 2.6 copy-start.2
  317.9 1.7 copy-start.1
  321.7 2.6 copy-start.2
  344.0 1.7 copy-start.1
  347.7 2.6 copy-start.2
  366.2 4.5 copy-start.6
  375.0 4.0 copy-start.3
  378.9 2.7 copy-start.5
  390.5 30.8 %collective-permute-start = (bf16[16,128,1024]{1,2,0:T(8,128)(2,1)}, bf16[16,128,1024]{1,2,0:T(8,128)(2,1)}, u32[]{:S(2)}, u32[]{:S(2)}) collective-permute-start(bf16[16,128,1024]{1,2,0:T(8,128)(2,1)} %copy.54), channel_id=1, source_target_pairs={{0,1},{2,3},{4,5},{6,7},{8,9},{10,11},{12,13},{14,15},{16,17},{18,... | collective-permute-start | bytes 12582920 | tf_op jit(solution)/shard_map/ppermute | solution.py:20
  446.6 11.8 %copy-start.4 = (bf16[1,16,128,2,8,64]{5,1,4,2,3,0:T(8,128)(2,1)S(1)}, bf16[1,16,128,2,8,64]{5,1,4,2,3,0:T(8,128)(2,1)}, u32[]{:S(2)}) copy-start(bf16[1,16,128,2,8,64]{5,1,4,2,3,0:T(8,128)(2,1)} %copy.43) | copy-start | bytes 12582916
  465.7 8.1 %copy-start.7 = (bf16[512,512]{1,0:T(8,128)(2,1)S(1)}, bf16[512,512]{1,0:T(8,128)(2,1)}, u32[]{:S(2)}) copy-start(bf16[512,512]{1,0:T(8,128)(2,1)} %param.22) | copy-start | bytes 1572868
  473.8 4.4 copy-start.12
  478.1 3.6 copy-start.13
  478.2 3.6 copy-start.9
  478.2 3.6 copy-start.10
  478.7 9.1 %copy-start.8 = (f32[2048]{0:T(1024)}, f32[2048]{0:T(1024)S(1)}, u32[]{:S(2)}) copy-start(f32[2048]{0:T(1024)S(1)} %multiply_reduce_fusion.1) | copy-start | bytes 24580
  478.7 3.0 collective-permute-start.1
where the time goes:
time: 493 us; the launch traced here: 488 us
  local copies, waits for them, and re-layouts  169 us (34%)
  waiting for transfers between devices  153 us (31%)
  matrix products  106 us (22%)
  other arithmetic  37.1 us (8%)
  starting transfers between devices  17 us (3%)
    all_to_all x1, waiting for transfers between devices, body(): lax.all_to_all(outgoing, 'agent', split_axis=0, concat_axis=0, tiled=True)  150 us
    dot_general x4, matrix products, agent_group(): jnp.einsum('thqk,tkhe->tqhe', attention, key_part[:, :, 1], preferred_ele...  50 us
    concatenate x2, local copies, waits for them, and re-layouts, body(): jnp.concatenate([keyvals, listed], axis=1)  22.3 us
    unnamed x32, local copies, waits for them, and re-layouts  20.3 us
    sub x5, other arithmetic, softmax_rows(): shifted = scores - jnp.max(scores, axis=-1, keepdims=True)  20.2 us
    while x16, local copies, waits for them, and re-layouts  17.2 us
    dynamic_slice x8, local copies, waits for them, and re-layouts, body(): attended = lax.map(agent_group, (query_heads, all_keys))  14.9 us
    reshape x1, local copies, waits for them, and re-layouts, body(): padded[:steps_here]  13 us
  transfers between devices with their start and end apart: 4, of which 3 were waited for; matrix products, arithmetic and copies ran while one was open for 13% of the time, Pallas kernels for 0%

commit v1 on v0

v1 whole, which is shorter than its diff:
```python
import functools

import jax
import jax.numpy as jnp
from jax import lax
from jax.experimental import pallas as pl
from jax.experimental.pallas import tpu as pltpu
from jax.sharding import PartitionSpec as P

HEADS = 8
WINDOW = 16
discount = 0.9997
trace_decay = 0.995
epsilon = 1e-06
bf16 = jnp.bfloat16
f32 = jnp.float32
VMEM_LIMIT = 48 * 1024 * 1024


def rms(values):
    return values * lax.rsqrt(jnp.mean(values * values, axis=-1, keepdims=True) + epsilon)


def dot(a, b):
    return jnp.dot(a, b, preferred_element_type=f32)


def dot_t(a, b):
    return lax.dot_general(a, b, (((1,), (1,)), ((), ())), preferred_element_type=f32)


def attend(queries, keys, values, head_size, bias):
    rows, width = queries.shape
    scale = head_size ** (-0.5)
    pair = 2 * head_size
    lane = lax.broadcasted_iota(jnp.int32, (rows, pair), 1)
    first = lane < head_size
    ones = jnp.ones((keys.shape[0], pair), bf16)
    mixed = []
    for at in range(0, width, pair):
        both = queries[:, at : at + pair]
        none = jnp.zeros_like(both)
        stacked = jnp.concatenate(
            [jnp.where(first, both, none), jnp.where(first, none, both)], axis=0
        )
        scores = dot_t(stacked, keys[:, at : at + pair]) * scale
        if bias is not None:
            scores = scores + bias
        weights = jnp.exp(scores - jnp.max(scores, axis=-1, keepdims=True)).astype(bf16)
        summed = dot(weights, jnp.concatenate([values[:, at : at + pair], ones], axis=1))
        result = summed[:, :pair] / summed[:, pair:]
        mixed.append(jnp.where(first, result[:rows], result[rows:]).astype(bf16))
    return jnp.concatenate(mixed, axis=1)


def agent_kernel(list_length, head_size, where_ref, *refs):
    own_ref, listed_refs = refs[0], refs[1 : 1 + list_length]
    proj_ref, merge_ref, residual_ref, normed_ref = refs[1 + list_length :]
    width = own_ref.shape[-1]
    own = own_ref[0].astype(f32)
    rows = [rms(own).astype(bf16)]
    for listed in listed_refs:
        rows.append(rms(listed[0].astype(f32)).astype(bf16))
    queries = dot(rows[0], proj_ref[:, :width]).astype(bf16)
    keyvals = dot(jnp.concatenate(rows, axis=0), proj_ref[:, width:]).astype(bf16)
    mixed = attend(queries, keyvals[:, :width], keyvals[:, width:], head_size, None)
    residual = own + dot(mixed, merge_ref[...])
    residual_ref[0] = residual
    normed_ref[0] = rms(residual).astype(bf16)


def agent_stage(embedded, pool, where, first_step, steps, proj, merge):
    _, agents, width = embedded.shape
    list_length = where.shape[0] // steps
    piece = (1, agents, width)

    def listed_spec(j):
        return pl.BlockSpec(piece, lambda i, w: (w[i * list_length + j], 0, 0))

    whole = lambda i, w: (0, 0)
    return pl.pallas_call(
        functools.partial(agent_kernel, list_length, width // HEADS),
        grid_spec=pltpu.PrefetchScalarGridSpec(
            num_scalar_prefetch=1,
            grid=(steps,),
            in_specs=[pl.BlockSpec(piece, lambda i, w: (first_step + i, 0, 0))]
            + [listed_spec(j) for j in range(list_length)]
            + [pl.BlockSpec(proj.shape, whole), pl.BlockSpec(merge.shape, whole)],
            out_specs=[pl.BlockSpec(piece, lambda i, w: (i, 0, 0))] * 2,
        ),
        out_shape=[
            jax.ShapeDtypeStruct((steps, agents, width), f32),
            jax.ShapeDtypeStruct((steps, agents, width), bf16),
        ],
        compiler_params=pltpu.CompilerParams(vmem_limit_bytes=VMEM_LIMIT),
        name="agent_stage",
    )(where, embedded, *([pool] * list_length), proj, merge)


def suffix(values, rewards, done, next_value, next_advantage):
    steps = values.shape[0]
    living = 1.0 - done.astype(f32)
    running, following, rows = next_advantage, next_value, [None] * steps
    for step in range(steps - 1, -1, -1):
        alive = living[step : step + 1]
        value = values[step : step + 1]
        change = rewards[step : step + 1] + discount * alive * following - value
        running = change + discount * trace_decay * alive * running
        rows[step] = running
        following = value
    return rows


def time_kernel(parts, steps, tile, head_size, offset_ref, *refs):
    refs = list(refs)
    residual_refs = [refs.pop(0) for _ in range(parts)]
    rim_refs = [refs.pop(0) for _ in range(parts)]
    proj_ref, merge_ref, weight_ref, done_ref, rewards_ref, boot_ref = refs[:6]
    values_ref, edge_ref, bias_ref = refs[6:]
    width = proj_ref.shape[0]
    turn = pl.program_id(0)
    group = 8
    rows = steps * group
    agents = values_ref.shape[1]

    @pl.when(turn == 0)
    def _():
        r = lax.broadcasted_iota(jnp.int32, (2 * rows, 2 * rows), 0) % rows
        c = lax.broadcasted_iota(jnp.int32, (2 * rows, 2 * rows), 1)
        query_step = r // group
        key_step = c // group - steps
        allowed = (
            (r % group == c % group)
            & (key_step <= query_step)
            & (key_step > query_step - WINDOW)
            & (key_step + offset_ref[0] >= 0)
        )
        bias_ref[...] = jnp.where(allowed, 0.0, -1e30)
        values_ref[...] = jnp.zeros_like(values_ref)

    def pieces(part_refs):
        whole = jnp.concatenate([ref[...].astype(f32) for ref in part_refs], axis=0)
        return [
            whole[:, at : at + group].reshape(rows, width) for at in range(0, tile, group)
        ]

    residuals = pieces(residual_refs)
    current = jnp.concatenate([rms(r).astype(bf16) for r in residuals], axis=0)
    behind = jnp.concatenate([r.astype(bf16) for r in pieces(rim_refs)], axis=0)
    projected = dot(current, proj_ref[...]).astype(bf16)
    before = dot(behind, proj_ref[:, width:]).astype(bf16)
    bias = bias_ref[...]
    mixed = []
    for at in range(0, tile * steps, rows):
        mine, past = projected[at : at + rows], before[at : at + rows]
        keys = jnp.concatenate([past[:, :width], mine[:, width : 2 * width]], axis=0)
        held = jnp.concatenate([past[:, width:], mine[:, 2 * width :]], axis=0)
        mixed.append(attend(mine[:, :width], keys, held, head_size, bias))
    merged = dot(jnp.concatenate(mixed, axis=0), merge_ref[...])
    lane = lax.broadcasted_iota(jnp.int32, (steps, group, agents), 2)
    place = lax.broadcasted_iota(jnp.int32, (steps, group, agents), 1)
    total = values_ref[...]
    for n, residual in enumerate(residuals):
        final = rms(residual + merged[n * rows : (n + 1) * rows])
        value = jnp.sum(final * weight_ref[...], axis=-1, keepdims=True)
        spot = lane == place + (turn * tile + n * group)
        total = total + jnp.sum(
            jnp.where(spot, value.reshape(steps, group, 1), 0.0), axis=1
        )
    values_ref[...] = total

    @pl.when(turn == pl.num_programs(0) - 1)
    def _():
        found = values_ref[...]
        boot = boot_ref[...]
        advantages = suffix(found, rewards_ref[...], done_ref[...], boot, jnp.zeros_like(boot))
        edge_ref[...] = jnp.concatenate([found[:1], advantages[0]], axis=0)


def time_stage(residuals, rims, offset, proj, merge, weight, done, rewards, boot):
    part_steps = [r.shape[0] for r in residuals]
    steps = sum(part_steps)
    _, agents, width = residuals[0].shape
    tile = 16
    whole = lambda i, o: (0, 0)

    def blocks(arrays):
        return [
            pl.BlockSpec((array.shape[0], tile, width), lambda i, o: (0, i, 0))
            for array in arrays
        ]

    rows = 16 * steps
    fixed = [proj, merge, weight, done, rewards, boot]
    return pl.pallas_call(
        functools.partial(time_kernel, len(residuals), steps, tile, width // HEADS),
        grid_spec=pltpu.PrefetchScalarGridSpec(
            num_scalar_prefetch=1,
            grid=(agents // tile,),
            in_specs=blocks(residuals)
            + blocks(rims)
            + [pl.BlockSpec(array.shape, whole) for array in fixed],
            out_specs=[
                pl.BlockSpec((steps, agents), whole),
                pl.BlockSpec((2, agents), whole),
            ],
            scratch_shapes=[pltpu.VMEM((rows, rows), f32)],
        ),
        out_shape=[
            jax.ShapeDtypeStruct((steps, agents), f32),
            jax.ShapeDtypeStruct((2, agents), f32),
        ],
        compiler_params=pltpu.CompilerParams(vmem_limit_bytes=VMEM_LIMIT),
        name="time_stage",
    )(offset, *residuals, *rims, *fixed)


def advantage_kernel(last_ref, values_ref, rewards_ref, done_ref, boot_ref, edge_ref, out_ref, mine_ref):
    last = last_ref[0] > 0
    arriving = edge_ref[...]
    boot = boot_ref[...]
    found = values_ref[...]
    next_value = jnp.where(last, boot, arriving[:1])
    next_advantage = jnp.where(last, 0.0, arriving[1:2])
    rows = suffix(found, rewards_ref[...], done_ref[...], next_value, next_advantage)
    out_ref[...] = jnp.concatenate(rows, axis=0)
    mine_ref[...] = jnp.concatenate([found[:1], rows[0]], axis=0)


def advantage_stage(last, values, rewards, done, boot, edge):
    return pl.pallas_call(
        advantage_kernel,
        in_specs=[pl.BlockSpec(memory_space=pltpu.SMEM)]
        + [pl.BlockSpec(memory_space=pltpu.VMEM)] * 5,
        out_specs=[pl.BlockSpec(memory_space=pltpu.VMEM)] * 2,
        out_shape=[
            jax.ShapeDtypeStruct(values.shape, f32),
            jax.ShapeDtypeStruct(edge.shape, f32),
        ],
        name="advantage_stage",
    )(last, values, rewards, done, boot, edge)


def exchange_slots(embedded, lists, capacity):
    steps, agents, width = embedded.shape
    blocks = lax.axis_size("agent")
    list_length = lists.shape[1]
    named = lists.reshape(-1)
    row_steps = jnp.arange(named.shape[0], dtype=jnp.int32) // list_length
    hits = (named[:, None] == jnp.arange(blocks, dtype=jnp.int32)[None, :]).astype(jnp.int32)
    slot = jnp.sum((jnp.cumsum(hits, axis=0) - hits) * hits, axis=1)
    slot_hits = (slot[:, None] == jnp.arange(capacity, dtype=jnp.int32)[None, :]).astype(jnp.int32)
    requests = jnp.sum(
        (hits * row_steps[:, None])[:, :, None] * slot_hits[:, None, :], axis=0
    )
    wanted = lax.all_to_all(requests, "agent", split_axis=0, concat_axis=0, tiled=True)
    outgoing = embedded[wanted.reshape(-1)].reshape(blocks, capacity, agents, width)
    arrived = lax.all_to_all(outgoing, "agent", split_axis=0, concat_axis=0, tiled=True)
    return arrived.reshape(blocks * capacity, agents, width), named * capacity + slot


def body(
    embedded,
    block_lists,
    done_flags,
    rewards,
    bootstrap,
    agent_proj,
    agent_merge,
    time_proj,
    time_merge,
    value_weight,
):
    steps, agents, width = embedded.shape
    list_length = block_lists.shape[2]
    blocks = lax.axis_size("agent")
    lists = block_lists[0]
    capacity = max(2, (2 * steps * list_length + blocks - 1) // blocks)
    residuals, normed = [], []
    if steps <= 2 * capacity:
        chunk = max(1, steps // 4)
        pools = [
            lax.all_gather(embedded[at : at + chunk], "agent", axis=0, tiled=True)
            for at in range(0, steps, chunk)
        ]
        for n, pool in enumerate(pools):
            mine = lists[n * chunk : (n + 1) * chunk]
            where = mine * chunk + jnp.arange(chunk, dtype=jnp.int32)[:, None]
            first, second = agent_stage(
                embedded, pool, where.reshape(-1), n * chunk, chunk, agent_proj, agent_merge
            )
            residuals.append(first)
            normed.append(second)
    else:
        pool, where = exchange_slots(embedded, lists, capacity)
        first, second = agent_stage(embedded, pool, where, 0, steps, agent_proj, agent_merge)
        residuals.append(first)
        normed.append(second)

    spans = lax.axis_size("tm")
    forward = [(i, i + 1) for i in range(spans - 1)]
    backward = [(i + 1, i) for i in range(spans - 1)]
    rims = [lax.ppermute(part, "tm", forward) for part in normed]
    index = lax.axis_index("tm")
    offset = (index * steps).astype(jnp.int32).reshape(1)
    boot = bootstrap.reshape(1, agents)
    values, edge = time_stage(
        residuals,
        rims,
        offset,
        time_proj,
        time_merge,
        value_weight.reshape(1, width),
        done_flags,
        rewards,
        boot,
    )
    last = (index == spans - 1).astype(jnp.int32).reshape(1)
    for _ in range(max(1, spans - 1)):
        arriving = lax.ppermute(edge, "tm", backward)
        advantages, edge = advantage_stage(last, values, rewards, done_flags, boot, arriving)
    return (values, advantages)


def solution(mesh):
    placed = (
        P(("groups", "tm"), "agent", None),
        P(("groups", "agent"), "tm", None),
        P(("groups", "tm"), "agent"),
        P(("groups", "tm"), "agent"),
        P(("groups", "agent")),
        P(),
        P(),
        P(),
        P(),
        P(),
    )
    return jax.shard_map(
        body,
        mesh=mesh,
        in_specs=placed,
        out_specs=(P(("groups", "tm"), "agent"), P(("groups", "tm"), "agent")),
        check_vma=False,
    )
```

time: 493 us -> 358 us (0.73)
  local copies, waits for them, and re-layouts: 169 us -> 17.6 us
  matrix products: 106 us -> 0 us
  waiting for transfers between devices: 153 us -> 256 us
  Pallas kernels: 0 us -> 61.3 us
  other arithmetic: 37.1 us -> 0.08 us
  between operations: 1.11 us -> 13.9 us
  starting transfers between devices: 17 us -> 9 us
    all_gather x0 -> x4, waiting for transfers between devices: none -> 251 us  [body(): lax.all_gather(embedded[at:at + chunk], 'agent', axis=0, tiled=True)]
    all_to_all x2 -> x0, waiting for transfers between devices: 151 us -> none  [the longest x1 150 us: body(): lax.all_to_all(outgoing, 'agent', split_axis=0, concat_axis=0, tiled=True)]
    dot_general x16 -> x0, matrix products: 106 us -> none  [the longest x4 50 us: agent_group(): jnp.einsum('thqk,tkhe->tqhe', attention, key_part[:, :, 1], preferred_ele...]
    pallas_call x0 -> x6, Pallas kernels: none -> 61.3 us  [the longest x4 40.9 us: agent_stage(): pl.pallas_call(functools.partial(agent_kernel, list_length, width // HEAD...]
    reshape x4 -> x0, local copies, waits for them, and re-layouts: 34.8 us -> none  [the longest x1 13 us: body(): padded[:steps_here]]
    concatenate x2 -> x0, local copies, waits for them, and re-layouts: 22.3 us -> none  [body(): jnp.concatenate([keyvals, listed], axis=1)]
    sub x5 -> x0, other arithmetic: 20.2 us -> none  [softmax_rows(): shifted = scores - jnp.max(scores, axis=-1, keepdims=True)]
    convert_element_type x2 -> x0, local copies, waits for them, and re-layouts: 19.4 us -> none  [the longest x1 11.3 us: body(): listed = jnp.dot(listed_rows.reshape(-1, model_width), agent_proj[:, mode...]
  transfers between devices with their start and end apart: 4 -> 9, of which waited for: 3 -> 6; matrix products, arithmetic and copies ran while one was open for 13% -> 0% of each run, Pallas kernels for 0% -> 11%
where the time goes in v1:
time: 358 us
  waiting for transfers between devices  256 us (72%)
  Pallas kernels  61.3 us (17%)
  local copies, waits for them, and re-layouts  17.6 us (5%)
  between operations  13.9 us (4%)
  starting transfers between devices  9 us (3%)
    all_gather x4, waiting for transfers between devices, body(): lax.all_gather(embedded[at:at + chunk], 'agent', axis=0, tiled=True)  251 us
    pallas_call x4, Pallas kernels, agent_stage(): pl.pallas_call(functools.partial(agent_kernel, list_length, width // HEAD...  40.9 us
    pallas_call x1, Pallas kernels, time_stage(): pl.pallas_call(functools.partial(time_kernel, len(residuals), steps, tile...  19 us
    unnamed x40, local copies, waits for them, and re-layouts  13.8 us
    ppermute x4, starting transfers between devices, body(): rims = [lax.ppermute(part, 'tm', forward) for part in normed]  7.57 us
  transfers between devices with their start and end apart: 9, of which 6 were waited for; matrix products, arithmetic and copies ran while one was open for 0% of the time, Pallas kernels for 11%

profile of v1, /device:TPU:0, one launch (start us, length us, event | category | flops | bytes accessed | tf_op | source)
XLA Modules:
  0.0 357.7 jit_solution(11639585933541763618)
XLA Ops:
  7.2 3.0 fusion
  10.3 0.7 all-gather.7.cloned.1.call-update
  11.1 0.7 all-gather.9.cloned.1.call-update
  13.3 73.3 %all-gather.5.cloned.1.call-done.refs_1_.refs_2_ = bf16[32,128,512]{2,1,0:T(8,128)(2,1)} async-done(((bf16[4,128,512]{2,1,0:T(8,128)(2,1)}), bf16[32,128,512]{2,1,0:T(8,128)(2,1)}) %all-gather.5.cloned.1.call-update) | async-done | bytes 4194320 | tf_op jit(solution)/shard_map/all_gather | solution.py:283
  86.6 1.4 copy-done.1
  88.0 10.3 %agent_stage.4 = (f32[4,128,512]{2,1,0:T(8,128)S(1)}, bf16[4,128,512]{2,1,0:T(8,128)(2,1)}) custom-call(s32[8]{0:T(128)S(1)} %get-tuple-element.35.where_ref, bf16[16,128,512]{2,1,0:T(8,128)(2,1)S(1)} %copy-done, bf16[32,128,512]{2,1,0:T(8,128)(2,1)} %all-gather.5.cloned.1.call-done.refs_1_.refs_2_, ...), custom_call_target="tpu_custom_call" | custom-call | tf_op jit(solution)/shard_map/agent_stage/pallas_call | solution.py:81
  98.2 1.0 copy-done.6
  99.2 2.1 collective-permute-start
  101.3 59.1 %all-gather.7.cloned.1.call-done.refs_1_.refs_2_ = bf16[32,128,512]{2,1,0:T(8,128)(2,1)} async-done(((bf16[4,128,512]{2,1,0:T(8,128)(2,1)}), bf16[32,128,512]{2,1,0:T(8,128)(2,1)}) %all-gather.7.cloned.1.call-update) | async-done | bytes 4194320 | tf_op jit(solution)/shard_map/all_gather | solution.py:283
  160.4 1.4 copy-done.2
  161.8 10.2 %agent_stage.5 = (f32[4,128,512]{2,1,0:T(8,128)S(1)}, bf16[4,128,512]{2,1,0:T(8,128)(2,1)}) custom-call(s32[8]{0:T(128)S(1)} %get-tuple-element.34.where_ref, bf16[16,128,512]{2,1,0:T(8,128)(2,1)S(1)} %copy-done, bf16[32,128,512]{2,1,0:T(8,128)(2,1)} %all-gather.7.cloned.1.call-done.refs_1_.refs_2_, ...), custom_call_target="tpu_custom_call" | custom-call | tf_op jit(solution)/shard_map/agent_stage/pallas_call | solution.py:81
  172.0 1.0 copy-done.8
  172.9 2.1 collective-permute-start.1
  175.0 59.2 %all-gather.9.cloned.1.call-done.refs_1_.refs_2_ = bf16[32,128,512]{2,1,0:T(8,128)(2,1)} async-done(((bf16[4,128,512]{2,1,0:T(8,128)(2,1)}), bf16[32,128,512]{2,1,0:T(8,128)(2,1)}) %all-gather.9.cloned.1.call-update) | async-done | bytes 4194320 | tf_op jit(solution)/shard_map/all_gather | solution.py:283
  234.2 1.4 copy-done.3
  235.6 10.2 %agent_stage.6 = (f32[4,128,512]{2,1,0:T(8,128)S(1)}, bf16[4,128,512]{2,1,0:T(8,128)(2,1)}) custom-call(s32[8]{0:T(128)S(1)} %get-tuple-element.33.where_ref, bf16[16,128,512]{2,1,0:T(8,128)(2,1)S(1)} %copy-done, bf16[32,128,512]{2,1,0:T(8,128)(2,1)} %all-gather.9.cloned.1.call-done.refs_1_.refs_2_, ...), custom_call_target="tpu_custom_call" | custom-call | tf_op jit(solution)/shard_map/agent_stage/pallas_call | solution.py:81
  245.8 1.0 copy-done.10
  246.8 2.1 collective-permute-start.2
  248.9 59.0 %all-gather.11.cloned.1.call-done.refs_1_.refs_2_ = bf16[32,128,512]{2,1,0:T(8,128)(2,1)} async-done(((bf16[4,128,512]{2,1,0:T(8,128)(2,1)}), bf16[32,128,512]{2,1,0:T(8,128)(2,1)}) %all-gather.11.cloned.1.call-update) | async-done | bytes 4194320 | tf_op jit(solution)/shard_map/all_gather | solution.py:283
  307.9 1.4 copy-done.4
  309.3 10.2 %agent_stage.7 = (f32[4,128,512]{2,1,0:T(8,128)S(1)}, bf16[4,128,512]{2,1,0:T(8,128)(2,1)}) custom-call(s32[8]{0:T(128)S(1)} %get-tuple-element.32.where_ref, bf16[16,128,512]{2,1,0:T(8,128)(2,1)S(1)} %copy-done, bf16[32,128,512]{2,1,0:T(8,128)(2,1)} %all-gather.11.cloned.1.call-done.refs_1_.refs_2_, ...), custom_call_target="tpu_custom_call" | custom-call | tf_op jit(solution)/shard_map/agent_stage/pallas_call | solution.py:81
  319.5 1.0 copy-done.12
  320.5 1.3 collective-permute-start.3
  321.8 1.7 collective-permute-done.3.refs_7_
  323.5 1.2 copy-done.7
  324.8 1.2 copy-done.9
  326.0 1.2 copy-done.11
  327.2 19.0 %time_stage.1 = (f32[16,128]{1,0:T(8,128)}, f32[2,128]{1,0:T(2,128)S(1)}) custom-call(s32[1]{0:T(128)} %bitcast.offset_ref, f32[4,128,512]{2,1,0:T(8,128)S(1)} %copy-done.7, f32[4,128,512]{2,1,0:T(8,128)S(1)} %copy-done.9, f32[4,128,512]{2,1,0:T(8,128)S(1)} %copy-done.11, f32[4,128,512]{2,1,0:T(8,128)} %copy-done.12, ...), custom_call_target="tpu_custom_call" | custom-call | tf_op jit(solution)/shard_map/time_stage/pallas_call | solution.py:195
  346.2 1.3 collective-permute-start.4
  347.5 1.7 collective-permute-done.4.edge_ref
  349.2 0.6 copy-done.19
  349.8 1.4 advantage_stage.1
  (49 shorter events, 1.6 us)
Async XLA Ops:
  7.2 79.4 %copy-start = (bf16[16,128,512]{2,1,0:T(8,128)(2,1)S(1)}, bf16[16,128,512]{2,1,0:T(8,128)(2,1)}, u32[]{:S(2)}) copy-start(bf16[16,128,512]{2,1,0:T(8,128)(2,1)} %refs_0_.7) | copy-start | bytes 6291460
  7.2 5.2 %copy-start.18 = (s32[1,16,2]{1,2,0:T(2,128)S(1)}, s32[1,16,2]{1,2,0:T(2,128)}, u32[]{:S(2)}) copy-start(s32[1,16,2]{1,2,0:T(2,128)} %param.11) | copy-start | bytes 388
  7.2 79.4 %copy-start.5 = (bf16[512,512]{1,0:T(8,128)(2,1)S(1)}, bf16[512,512]{1,0:T(8,128)(2,1)}, u32[]{:S(2)}) copy-start(bf16[512,512]{1,0:T(8,128)(2,1)} %refs_4_.7) | copy-start | bytes 1572868
  7.2 79.4 %all-gather.5.cloned.1.call-start = ((), (), s32[]{:S(2)}) async-start(), calls=%async_computation | async-start | bytes 4718592 | tf_op jit(solution)/shard_map/all_gather | solution.py:283
  10.3 150.1 %all-gather.7.cloned.1.call-start = ((), (), s32[]{:S(2)}) async-start(), calls=%async_computation.1 | async-start | bytes 4718592 | tf_op jit(solution)/shard_map/all_gather | solution.py:283
  11.0 223.1 %all-gather.9.cloned.1.call-start = ((), (), s32[]{:S(2)}) async-start(), calls=%async_computation.2 | async-start | bytes 4718592 | tf_op jit(solution)/shard_map/all_gather | solution.py:283
  11.8 296.1 %all-gather.11.cloned.1.call-start = ((), (), s32[]{:S(2)}) async-start(), calls=%async_computation.3 | async-start | bytes 4718592 | tf_op jit(solution)/shard_map/all_gather | solution.py:283
  86.6 1.4 copy-start.1
  98.2 1.0 copy-start.6
  99.2 222.6 %collective-permute-start = (bf16[4,128,512]{2,1,0:T(8,128)(2,1)}, bf16[4,128,512]{2,1,0:T(8,128)(2,1)}, u32[]{:S(2)}, u32[]{:S(2)}) collective-permute-start(bf16[4,128,512]{2,1,0:T(8,128)(2,1)} %get-tuple-element.17), channel_id=1, source_target_pairs={{0,1},{2,3},{4,5},{6,7},{8,9},{10,11},{12,13},{14,15},{16,17},{18,... | collective-permute-start | bytes 1572872 | tf_op jit(solution)/shard_map/ppermute | solution.py:303
  160.4 1.4 copy-start.2
  172.0 1.0 copy-start.8
  172.9 148.9 %collective-permute-start.1 = (bf16[4,128,512]{2,1,0:T(8,128)(2,1)}, bf16[4,128,512]{2,1,0:T(8,128)(2,1)}, u32[]{:S(2)}, u32[]{:S(2)}) collective-permute-start(bf16[4,128,512]{2,1,0:T(8,128)(2,1)} %get-tuple-element.18), channel_id=1, source_target_pairs={{0,1},{2,3},{4,5},{6,7},{8,9},{10,11},{12,13},{14,15},{16,17},{18,... | collective-permute-start | bytes 1572872 | tf_op jit(solution)/shard_map/ppermute | solution.py:303
  234.2 1.4 copy-start.3
  245.8 1.0 copy-start.10
  246.8 75.1 %collective-permute-start.2 = (bf16[4,128,512]{2,1,0:T(8,128)(2,1)}, bf16[4,128,512]{2,1,0:T(8,128)(2,1)}, u32[]{:S(2)}, u32[]{:S(2)}) collective-permute-start(bf16[4,128,512]{2,1,0:T(8,128)(2,1)} %get-tuple-element.19), channel_id=1, source_target_pairs={{0,1},{2,3},{4,5},{6,7},{8,9},{10,11},{12,13},{14,15},{16,17},{18,... | collective-permute-start | bytes 1572872 | tf_op jit(solution)/shard_map/ppermute | solution.py:303
  307.9 1.4 copy-start.4
  309.3 14.2 %copy-start.13 = (bf16[512,512]{1,0:T(8,128)(2,1)S(1)}, bf16[512,512]{1,0:T(8,128)(2,1)}, u32[]{:S(2)}) copy-start(bf16[512,512]{1,0:T(8,128)(2,1)} %refs_9_.1) | copy-start | bytes 1572868
  309.3 14.2 %copy-start.14 = (s32[16,128]{1,0:T(8,128)S(1)}, s32[16,128]{1,0:T(8,128)}, u32[]{:S(2)}) copy-start(s32[16,128]{1,0:T(8,128)} %done_ref.1) | copy-start | bytes 24580
  309.3 14.2 %copy-start.15 = (f32[16,128]{1,0:T(8,128)S(1)}, f32[16,128]{1,0:T(8,128)}, u32[]{:S(2)}) copy-start(f32[16,128]{1,0:T(8,128)} %rewards_ref.1) | copy-start | bytes 24580
  309.3 14.2 %copy-start.16 = (f32[512]{0:T(512)S(1)}, f32[512]{0:T(512)}, u32[]{:S(2)}) copy-start(f32[512]{0:T(512)} %param.19) | copy-start | bytes 6148
  309.3 14.2 %copy-start.17 = (f32[128]{0:T(128)S(1)}, f32[128]{0:T(128)}, u32[]{:S(2)}) copy-start(f32[128]{0:T(128)} %param.14) | copy-start | bytes 1540
  319.5 1.0 copy-start.12
  320.5 3.0 collective-permute-start.3
  323.5 1.2 copy-start.7
  324.8 1.2 copy-start.9
  326.0 1.2 copy-start.11
  346.2 3.0 collective-permute-start.4
  349.2 0.6 copy-start.19
Sparse Core Ops, SparseCore 0:
  10.4 76.0 all-gather.4
  88.7 71.6 all-gather.6
  162.5 71.6 all-gather.8
  236.2 71.6 all-gather.10

commit v2 on v1

--- a/solution.py
+++ b/solution.py
@@ -15,6 +15,9 @@
 bf16 = jnp.bfloat16
 f32 = jnp.float32
 VMEM_LIMIT = 48 * 1024 * 1024
+SPAN = 1024
+COLUMNS = 4
+ROWS = 2
 
 
 def rms(values):
@@ -53,15 +56,41 @@
     return jnp.concatenate(mixed, axis=1)
 
 
-def agent_kernel(list_length, head_size, where_ref, *refs):
-    own_ref, listed_refs = refs[0], refs[1 : 1 + list_length]
-    proj_ref, merge_ref, residual_ref, normed_ref = refs[1 + list_length :]
+def fetch(entry, arrays, target, sem):
+    for code, ref in arrays.items():
+
+        @pl.when(entry // SPAN == code)
+        def _(ref=ref):
+            pltpu.make_async_copy(ref.at[entry % SPAN], target, sem).start()
+
+
+def agent_kernel(list_length, first_step, codes, head_size, table_ref, own_ref, *refs):
+    arrays = dict(zip(codes, refs))
+    proj_ref, merge_ref, residual_ref, normed_ref, held_ref, sems = refs[len(codes) :]
     width = own_ref.shape[-1]
+    turn = pl.program_id(0)
+
+    def begin(step):
+        for j in range(list_length):
+            slot = step % 2
+            entry = table_ref[(first_step + step) * list_length + j]
+            fetch(entry, arrays, held_ref.at[slot, j], sems.at[slot, j])
+
+    @pl.when(turn == 0)
+    def _():
+        begin(turn)
+
+    @pl.when(turn + 1 < pl.num_programs(0))
+    def _():
+        begin(turn + 1)
+
     own = own_ref[0].astype(f32)
     rows = [rms(own).astype(bf16)]
-    for listed in listed_refs:
-        rows.append(rms(listed[0].astype(f32)).astype(bf16))
     queries = dot(rows[0], proj_ref[:, :width]).astype(bf16)
+    slot = turn % 2
+    for j in range(list_length):
+        pltpu.make_async_copy(refs[0].at[0], held_ref.at[slot, j], sems.at[slot, j]).wait()
+        rows.append(rms(held_ref[slot, j].astype(f32)).astype(bf16))
     keyvals = dot(jnp.concatenate(rows, axis=0), proj_ref[:, width:]).astype(bf16)
     mixed = attend(queries, keyvals[:, :width], keyvals[:, width:], head_size, None)
     residual = own + dot(mixed, merge_ref[...])
@@ -69,32 +98,68 @@
     normed_ref[0] = rms(residual).astype(bf16)
 
 
-def agent_stage(embedded, pool, where, first_step, steps, proj, merge):
+def agent_stage(embedded, arrays, table, first_step, steps, list_length, proj, merge):
     _, agents, width = embedded.shape
-    list_length = where.shape[0] // steps
     piece = (1, agents, width)
-
-    def listed_spec(j):
-        return pl.BlockSpec(piece, lambda i, w: (w[i * list_length + j], 0, 0))
-
     whole = lambda i, w: (0, 0)
+    flops = 2 * steps * agents * width * width * (4 + 2 * list_length + 2 * (1 + list_length))
     return pl.pallas_call(
-        functools.partial(agent_kernel, list_length, width // HEADS),
+        functools.partial(
+            agent_kernel, list_length, first_step, tuple(arrays), width // HEADS
+        ),
         grid_spec=pltpu.PrefetchScalarGridSpec(
             num_scalar_prefetch=1,
             grid=(steps,),
             in_specs=[pl.BlockSpec(piece, lambda i, w: (first_step + i, 0, 0))]
-            + [listed_spec(j) for j in range(list_length)]
+            + [pl.BlockSpec(memory_space=pl.ANY)] * len(arrays)
             + [pl.BlockSpec(proj.shape, whole), pl.BlockSpec(merge.shape, whole)],
             out_specs=[pl.BlockSpec(piece, lambda i, w: (i, 0, 0))] * 2,
+            scratch_shapes=[
+                pltpu.VMEM((2, list_length, agents, width), bf16),
+                pltpu.SemaphoreType.DMA((2, list_length)),
+            ],
         ),
         out_shape=[
             jax.ShapeDtypeStruct((steps, agents, width), f32),
             jax.ShapeDtypeStruct((steps, agents, width), bf16),
         ],
         compiler_params=pltpu.CompilerParams(vmem_limit_bytes=VMEM_LIMIT),
+        cost_estimate=pl.CostEstimate(
+            flops=5 * flops, bytes_accessed=steps * agents * width * 12, transcendentals=0
+        ),
         name="agent_stage",
-    )(where, embedded, *([pool] * list_length), proj, merge)
+    )(table, embedded, *arrays.values(), proj, merge)
+
+
+def pack_kernel(codes, parts, table_ref, *refs):
+    arrays = dict(zip(codes, refs))
+    outs, sems = refs[len(codes) : -1], refs[-1]
+    slots = [
+        (offset + n, out.at[n]) for out, (offset, count) in zip(outs, parts) for n in range(count)
+    ]
+    for n, (at, target) in enumerate(slots):
+        fetch(table_ref[at], arrays, target, sems.at[n])
+    for n, (at, target) in enumerate(slots):
+
+        @pl.when(table_ref[at] >= 0)
+        def _(n=n, target=target):
+            pltpu.make_async_copy(refs[0].at[0], target, sems.at[n]).wait()
+
+
+def pack(table, arrays, parts):
+    piece = next(iter(arrays.values())).shape[1:]
+    return pl.pallas_call(
+        functools.partial(pack_kernel, tuple(arrays), parts),
+        in_specs=[pl.BlockSpec(memory_space=pltpu.SMEM)]
+        + [pl.BlockSpec(memory_space=pl.ANY)] * len(arrays),
+        out_specs=[pl.BlockSpec(memory_space=pl.ANY)] * len(parts),
+        out_shape=[jax.ShapeDtypeStruct((count,) + piece, bf16) for _, count in parts],
+        scratch_shapes=[pltpu.SemaphoreType.DMA((sum(count for _, count in parts),))],
+        cost_estimate=pl.CostEstimate(
+            flops=0, bytes_accessed=4 * sum(c for _, c in parts) * piece[0] * piece[1], transcendentals=0
+        ),
+        name="pack",
+    )(table, *arrays.values())
 
 
 def suffix(values, rewards, done, next_value, next_advantage):
@@ -259,6 +324,250 @@
     return arrived.reshape(blocks * capacity, agents, width), named * capacity + slot
 
 
+def relay_sizes(steps, capacity):
+    chunk = steps // 4
+    chunks = [chunk] * 4
+    outward = [2 * chunk] * 3 + [chunk + 1] * 2
+    across = [capacity] + [2 * chunk] * 3 + [chunk + 1, chunk]
+    return chunks, outward, across
+
+
+def relay_codes(chunks, outward, across):
+    count = len(chunks)
+    return {
+        "own": 0,
+        "outer": [1 + k for k in range(count)],
+        "inner": [1 + count + k for k in range(count)],
+        "far": [1 + 2 * count + k for k in range(count)],
+        "outward": [1 + 3 * count + b for b in range(len(outward))],
+        "across": [1 + 3 * count + len(outward) + b for b in range(len(across))],
+    }
+
+
+def relay_ready(count, k):
+    return max(1, k), k + 1
+
+
+def plan_kernel(steps, list_length, chunks, outward, across, place_ref, lists_ref, out_ref, in_ref, flag_ref, eloc, yloc, room):
+    codes = relay_codes(chunks, outward, across)
+    column, row = place_ref[0], place_ref[1]
+    far_side = column >= COLUMNS // 2
+    mirror = lambda u: jnp.where(far_side, COLUMNS - 1 - u, u)
+    me = mirror(column)
+    inner = me == 1
+    starts = [sum(chunks[:k]) for k in range(len(chunks))]
+    e_base = [sum(outward[:b]) for b in range(len(outward))]
+    y_base = [sum(outward) + sum(across[:b]) for b in range(len(across))]
+    block = lambda c, r: c * ROWS + r
+    entry = lambda b, t, j: lists_ref[(b * steps + t) * list_length + j]
+
+    def clear(n, _):
+        out_ref[n] = -1
+        return 0
+
+    lax.fori_loop(0, sum(outward) + sum(across), clear, 0)
+
+    def named(dest, t, source):
+        hit = entry(dest, t, 0) == source
+        for j in range(1, list_length):
+            hit = hit | (entry(dest, t, j) == source)
+        return hit
+
+    def choose(sizes, ready):
+        batch = jnp.int32(-1)
+        for b in range(len(sizes) - 1, -1, -1):
+            batch = jnp.where((room[b] < sizes[b]) & (b >= ready), b, batch)
+        return batch
+
+    def base_of(bases, batch):
+        base = jnp.int32(0)
+        for b, value in enumerate(bases):
+            base = jnp.where(batch == b, value, base)
+        return base
+
+    def empty(sizes):
+        for b in range(len(sizes)):
+            room[b] = 0
+
+    for turn in range(2):
+        sender = row if turn == 0 else 1 - row
+        empty(outward)
+        for k, count in enumerate(chunks):
+            ready = (0, 0) + relay_ready(len(chunks), k)
+            held = (0, codes["own"] * SPAN + starts[k], codes["inner"][k] * SPAN, codes["far"][k] * SPAN)
+            for u in (1, 2, 3):
+
+                def outer_piece(n, _, u=u, k=k, ready=ready, held=held):
+                    t = starts[k] + n
+                    source = block(mirror(u), sender)
+                    need = named(block(mirror(0), 0), t, source)
+                    for r in range(1, ROWS):
+                        need = need | named(block(mirror(0), r), t, source)
+                    batch = choose(outward, ready[u])
+                    eloc[(turn * COLUMNS + u) * steps + t] = -1
+
+                    @pl.when(need & (batch >= 0))
+                    def _():
+                        slot = room[batch]
+                        room[batch] = slot + 1
+                        eloc[(turn * COLUMNS + u) * steps + t] = batch * SPAN + slot
+                        if turn == 0:
+
+                            @pl.when(inner)
+                            def _():
+                                out_ref[base_of(e_base, batch) + slot] = held[u] + n
+
+                    return 0
+
+                lax.fori_loop(0, count, outer_piece, 0)
+
+    for turn in range(2):
+        sender = row if turn == 0 else 1 - row
+        empty(across)
+        for k, count in enumerate(chunks):
+            ready = relay_ready(len(chunks), k)
+            ready = (ready[0], 0) + ready
+            held = (codes["outer"][k] * SPAN, codes["own"] * SPAN + starts[k], codes["inner"][k] * SPAN, codes["far"][k] * SPAN)
+            for u in range(COLUMNS):
+
+                def row_piece(n, _, u=u, k=k, ready=ready, held=held):
+                    t = starts[k] + n
+                    need = named(block(column, 1 - sender), t, block(mirror(u), sender))
+                    if u == 0:
+                        lies = jnp.int32(codes["own"] * SPAN) + t
+                        when = jnp.int32(0)
+                    else:
+                        where = eloc[(turn * COLUMNS + u) * steps + t]
+                        lies = codes["outward"][0] * SPAN + where
+                        when = jnp.where(where < 0, len(across), where // SPAN + 1)
+                    when = jnp.where(inner, ready[u], when)
+                    lies = jnp.where(inner, held[u] + n, lies)
+                    batch = choose(across, when)
+                    yloc[(turn * COLUMNS + u) * steps + t] = -1
+
+                    @pl.when(need & (batch >= 0))
+                    def _():
+                        slot = room[batch]
+                        room[batch] = slot + 1
+                        yloc[(turn * COLUMNS + u) * steps + t] = batch * SPAN + slot
+                        if turn == 0:
+                            out_ref[base_of(y_base, batch) + slot] = lies
+
+                    return 0
+
+                lax.fori_loop(0, count, row_piece, 0)
+
+    flag_ref[0] = 0
+    for k, count in enumerate(chunks):
+
+        def listed_piece(n, _, k=k):
+            t = starts[k] + n // list_length
+            source = entry(block(column, row), t, n % list_length)
+            u = mirror(source // ROWS)
+            same = source % ROWS == row
+            e = eloc[u * steps + t]
+            y = yloc[(COLUMNS + u) * steps + t]
+            code = jnp.where(u == 0, codes["outer"][k], jnp.where(u == 2, codes["inner"][k], codes["far"][k]))
+            direct = jnp.where(inner, code * SPAN + t - starts[k], codes["outward"][0] * SPAN + e)
+            direct = jnp.where(u == me, codes["own"] * SPAN + t, direct)
+            local = inner | (u == me)
+            bad = jnp.where(
+                same,
+                jnp.logical_not(local) & ((e < 0) | (e // SPAN > min(k + 2, len(outward) - 1))),
+                (y < 0) | (y // SPAN > k + 2),
+            )
+            place = jnp.where(same, direct, codes["across"][0] * SPAN + y)
+            in_ref[t * list_length + n % list_length] = jnp.where(bad, codes["own"] * SPAN, place)
+
+            @pl.when(bad)
+            def _():
+                flag_ref[0] = 1
+
+            return 0
+
+        lax.fori_loop(0, count * list_length, listed_piece, 0)
+
+
+def plan(lists_all, place, steps, list_length, chunks, outward, across):
+    smem = pl.BlockSpec(memory_space=pltpu.SMEM)
+    slots = sum(outward) + sum(across)
+    return pl.pallas_call(
+        functools.partial(plan_kernel, steps, list_length, chunks, outward, across),
+        in_specs=[smem, smem],
+        out_specs=[smem] * 3,
+        out_shape=[
+            jax.ShapeDtypeStruct((slots,), jnp.int32),
+            jax.ShapeDtypeStruct((steps * list_length,), jnp.int32),
+            jax.ShapeDtypeStruct((1,), jnp.int32),
+        ],
+        scratch_shapes=[
+            pltpu.SMEM((2 * COLUMNS * steps,), jnp.int32),
+            pltpu.SMEM((2 * COLUMNS * steps,), jnp.int32),
+            pltpu.SMEM((max(len(outward), len(across)),), jnp.int32),
+        ],
+        name="plan",
+    )(place, lists_all)
+
+
+def column_pairs(moves):
+    return [(a * ROWS + r, b * ROWS + r) for a, b in moves for r in range(ROWS)]
+
+
+def relay(embedded, lists, capacity):
+    steps, agents, width = embedded.shape
+    list_length = lists.shape[1]
+    chunks, outward, across = relay_sizes(steps, capacity)
+    codes = relay_codes(chunks, outward, across)
+    starts = [sum(chunks[:k]) for k in range(len(chunks))]
+    index = lax.axis_index("agent")
+    place = jnp.stack([index // ROWS, index % ROWS]).astype(jnp.int32)
+    send = lambda value, pairs: lax.ppermute(value, "agent", pairs)
+    inward = column_pairs([(0, 1), (3, 2)])
+    swap = column_pairs([(1, 2), (2, 1)])
+    away = column_pairs([(1, 0), (2, 3)])
+    over = [(c * ROWS + r, c * ROWS + 1 - r) for c in range(COLUMNS) for r in range(ROWS)]
+    everyone = lax.all_gather(lists.reshape(-1), "agent", axis=0, tiled=True)
+    out_table, in_table, flag = plan(
+        everyone, place, steps, list_length, chunks, outward, across
+    )
+    arrays = {codes["own"]: embedded}
+
+    def begin(k, part):
+        arrays[codes["outer"][k]] = send(part, inward)
+        arrays[codes["inner"][k]] = send(part, swap)
+        arrays[codes["far"][k]] = send(arrays[codes["outer"][k]], swap)
+
+    def own_part(k):
+        return embedded[starts[k] : starts[k] + chunks[k]]
+
+    for k in range(len(chunks)):
+        begin(k, own_part(k))
+    e_base = [sum(outward[:b]) for b in range(len(outward))]
+    y_base = [sum(outward) + sum(across[:b]) for b in range(len(across))]
+    for stage in range(len(across)):
+        known = {codes["own"]: embedded}
+        for k in range(len(chunks)):
+            near, far = relay_ready(len(chunks), k)
+            if near <= stage:
+                known[codes["outer"][k]] = arrays[codes["outer"][k]]
+                known[codes["inner"][k]] = arrays[codes["inner"][k]]
+            if far <= stage:
+                known[codes["far"][k]] = arrays[codes["far"][k]]
+        for b in range(min(stage, len(outward))):
+            known[codes["outward"][b]] = arrays[codes["outward"][b]]
+        parts = [(e_base[stage], outward[stage])] if stage < len(outward) else []
+        packed = pack(out_table, known, tuple(parts + [(y_base[stage], across[stage])]))
+        if parts:
+            arrays[codes["outward"][stage]] = send(packed[0], away)
+        arrays[codes["across"][stage]] = send(packed[-1], over)
+    work = []
+    for k in range(len(chunks)):
+        wanted = [codes["own"], codes["outer"][k], codes["inner"][k], codes["far"][k]]
+        wanted += codes["outward"][: k + 3] + codes["across"][: k + 3]
+        work.append((starts[k], chunks[k], {code: arrays[code] for code in wanted}))
+    return work, in_table, flag
+
+
 def body(
     embedded,
     block_lists,
@@ -276,50 +585,48 @@
     blocks = lax.axis_size("agent")
     lists = block_lists[0]
     capacity = max(2, (2 * steps * list_length + blocks - 1) // blocks)
-    residuals, normed = [], []
-    if steps <= 2 * capacity:
-        chunk = max(1, steps // 4)
-        pools = [
-            lax.all_gather(embedded[at : at + chunk], "agent", axis=0, tiled=True)
-            for at in range(0, steps, chunk)
-        ]
-        for n, pool in enumerate(pools):
-            mine = lists[n * chunk : (n + 1) * chunk]
-            where = mine * chunk + jnp.arange(chunk, dtype=jnp.int32)[:, None]
-            first, second = agent_stage(
-                embedded, pool, where.reshape(-1), n * chunk, chunk, agent_proj, agent_merge
-            )
-            residuals.append(first)
-            normed.append(second)
-    else:
-        pool, where = exchange_slots(embedded, lists, capacity)
-        first, second = agent_stage(embedded, pool, where, 0, steps, agent_proj, agent_merge)
-        residuals.append(first)
-        normed.append(second)
-
     spans = lax.axis_size("tm")
-    forward = [(i, i + 1) for i in range(spans - 1)]
-    backward = [(i + 1, i) for i in range(spans - 1)]
-    rims = [lax.ppermute(part, "tm", forward) for part in normed]
     index = lax.axis_index("tm")
     offset = (index * steps).astype(jnp.int32).reshape(1)
     boot = bootstrap.reshape(1, agents)
-    values, edge = time_stage(
-        residuals,
-        rims,
-        offset,
-        time_proj,
-        time_merge,
-        value_weight.reshape(1, width),
-        done_flags,
-        rewards,
-        boot,
-    )
-    last = (index == spans - 1).astype(jnp.int32).reshape(1)
-    for _ in range(max(1, spans - 1)):
-        arriving = lax.ppermute(edge, "tm", backward)
-        advantages, edge = advantage_stage(last, values, rewards, done_flags, boot, arriving)
-    return (values, advantages)
+    forward = [(i, i + 1) for i in range(spans - 1)]
+    backward = [(i + 1, i) for i in range(spans - 1)]
+
+    def finish(work, table):
+        residuals, rims = [], []
+        for first, count, arrays in work:
+            residual, normed = agent_stage(
+                embedded, arrays, table, first, count, list_length, agent_proj, agent_merge
+            )
+            residuals.append(residual)
+            rims.append(lax.ppermute(normed, "tm", forward))
+        values, edge = time_stage(
+            residuals,
+            rims,
+            offset,
+            time_proj,
+            time_merge,
+            value_weight.reshape(1, width),
+            done_flags,
+            rewards,
+            boot,
+        )
+        last = (index == spans - 1).astype(jnp.int32).reshape(1)
+        for _ in range(max(1, spans - 1)):
+            arriving = lax.ppermute(edge, "tm", backward)
+            advantages, edge = advantage_stage(last, values, rewards, done_flags, boot, arriving)
+        return values, advantages
+
+    def padded():
+        pool, where = exchange_slots(embedded, lists, capacity)
+        return finish([(0, steps, {1: pool})], where + SPAN)
+
+    if blocks != COLUMNS * ROWS or steps % 4:
+        return padded()
+    work, table, flag = relay(embedded, lists, capacity)
+    crowded = lax.pmax(flag[0], ("groups", "agent", "tm"))
+    found = finish(work, table)
+    return lax.cond(crowded > 0, padded, lambda: found)
 
 
 def solution(mesh):

time: 358 us -> 450 us (1.26)
  waiting for transfers between devices: 256 us -> 90 us
  Pallas kernels: 61.3 us -> 162 us
  starting transfers between devices: 9 us -> 106 us
  blocking collectives: 0 us -> 73.8 us
  between operations: 13.9 us -> 2.64 us
  local copies, waits for them, and re-layouts: 17.6 us -> 11.6 us
    all_gather x4 -> x0, waiting for transfers between devices: 251 us -> none  [body(): lax.all_gather(embedded[at:at + chunk], 'agent', axis=0, tiled=True)]
    pallas_call x4 -> x11, Pallas kernels: 40.9 us -> 142 us  [the longest x6 82.2 us: pack(): pl.pallas_call(functools.partial(pack_kernel, tuple(arrays), parts), in_s...]
    ppermute x5 -> x28, starting transfers between devices: 8.85 us -> 106 us  [the longest x23 80.5 us: relay(): send = lambda value, pairs: lax.ppermute(value, 'agent', pairs)]
    ppermute x5 -> x28, waiting for transfers between devices: 3.4 us -> 90 us  [the longest x23 88.9 us: relay(): send = lambda value, pairs: lax.ppermute(value, 'agent', pairs)]
    pmax x0 -> x1, blocking collectives: none -> 58.4 us  [body(): crowded = lax.pmax(flag[0], ('groups', 'agent', 'tm'))]
    unnamed x0 -> x1, blocking collectives: none -> 15.4 us
    unnamed x40 -> x84, local copies, waits for them, and re-layouts: 13.8 us -> 8.43 us
  transfers between devices with their start and end apart: 9 -> 28, of which waited for: 6 -> 8; matrix products, arithmetic and copies ran while one was open for 0% -> 0% of each run, Pallas kernels for 11% -> 26%
where the time goes in v2:
time: 450 us; the launch traced here: 446 us
  Pallas kernels  162 us (36%)
  starting transfers between devices  106 us (24%)
  waiting for transfers between devices  90 us (20%)
  blocking collectives  73.8 us (16%)
  local copies, waits for them, and re-layouts  11.6 us (3%)
    ppermute x23, waiting for transfers between devices, relay(): send = lambda value, pairs: lax.ppermute(value, 'agent', pairs)  88.9 us
    pallas_call x6, Pallas kernels, pack(): pl.pallas_call(functools.partial(pack_kernel, tuple(arrays), parts), in_s...  82.2 us
    ppermute x23, starting transfers between devices, relay(): send = lambda value, pairs: lax.ppermute(value, 'agent', pairs)  80.5 us
    pmax x1, blocking collectives, body(): crowded = lax.pmax(flag[0], ('groups', 'agent', 'tm'))  58.4 us
    pallas_call x4, Pallas kernels, agent_stage(): pl.pallas_call(functools.partial(agent_kernel, list_length, first_step, t...  51 us
    ppermute x4, starting transfers between devices, finish(): rims.append(lax.ppermute(normed, 'tm', forward))  23.9 us
    pallas_call x1, Pallas kernels, time_stage(): pl.pallas_call(functools.partial(time_kernel, len(residuals), steps, tile...  19.1 us
    unnamed x1, blocking collectives  15.4 us
  transfers between devices with their start and end apart: 28, of which 8 were waited for; matrix products, arithmetic and copies ran while one was open for 0% of the time, Pallas kernels for 26%

profile of v2, /device:TPU:0, one launch (start us, length us, event | category | flops | bytes accessed | tf_op | source)
XLA Modules:
  0.0 446.3 jit_solution(15745575194315840730)
XLA Ops:
  0.7 3.0 fusion.4
  3.7 4.9 %collective-permute-start.2 = (bf16[4,128,512]{2,1,0:T(8,128)(2,1)}, bf16[4,128,512]{2,1,0:T(8,128)(2,1)S(1)}, u32[]{:S(2)}, u32[]{:S(2)}) collective-permute-start(bf16[4,128,512]{2,1,0:T(8,128)(2,1)} %get-tuple-element.152), channel_id=1, source_target_pairs={{0,4},{2,6},{12,8},{14,10},{1,5},{3,7},{13,9},{15,11},{16,20},{18,... | collective-permute-start | bytes 1572872 | tf_op jit(solution)/shard_map/ppermute | solution.py:524
  10.4 15.4 %all-reduce.lists_ref = s32[256]{0:T(256)} all-reduce(s32[256]{0:T(256)S(1)} %dynamic-update-slice), channel_id=1, replica_groups=mesh['groups'=2,'agent'=8,'tm'=2] {'agent'}, use_global_device_ids=true, to_apply=%add | all-reduce | flops 256 | bytes 2048
  26.4 8.4 %plan.1 = (s32[75]{0:T(128)}, s32[32]{0:T(128)}, s32[1]{0:T(128)}) custom-call(s32[2]{0:T(128)} %pad_add_fusion.place_ref, s32[256]{0:T(256)} %all-reduce.lists_ref), custom_call_target="tpu_custom_call" | custom-call | tf_op jit(solution)/shard_map/plan/pallas_call | solution.py:494
  34.7 1.6 pack.6
  37.7 4.6 %collective-permute-start.6 = (bf16[4,128,512]{2,1,0:T(8,128)(2,1)}, bf16[4,128,512]{2,1,0:T(8,128)(2,1)S(1)}, u32[]{:S(2)}, u32[]{:S(2)}) collective-permute-start(bf16[4,128,512]{2,1,0:T(8,128)(2,1)} %get-tuple-element.151), channel_id=1, source_target_pairs={{0,4},{2,6},{12,8},{14,10},{1,5},{3,7},{13,9},{15,11},{16,20},{18,... | collective-permute-start | bytes 1572872 | tf_op jit(solution)/shard_map/ppermute | solution.py:524
  45.2 6.5 %collective-permute-done.6.refs_4_.refs_1_ = bf16[4,128,512]{2,1,0:T(8,128)(2,1)S(1)} collective-permute-done((bf16[4,128,512]{2,1,0:T(8,128)(2,1)}, bf16[4,128,512]{2,1,0:T(8,128)(2,1)S(1)}, u32[]{:S(2)}, u32[]{:S(2)}) %collective-permute-start.6) | collective-permute-done | bytes 524320 | tf_op jit(solution)/shard_map/ppermute | solution.py:524
  51.8 9.9 %collective-permute-done.5.refs_6_.refs_9_.refs_4_.refs_12_.refs_13_ = bf16[8,128,512]{2,1,0:T(8,128)(2,1)S(1)} collective-permute-done((bf16[8,128,512]{2,1,0:T(8,128)(2,1)}, bf16[8,128,512]{2,1,0:T(8,128)(2,1)S(1)}, u32[]{:S(2)}, u32[]{:S(2)}) %collective-permute-start.5) | collective-permute-done | bytes 1048608 | tf_op jit(solution)/shard_map/ppermute | solution.py:524
  62.6 25.9 %pack.7 = (bf16[8,128,512]{2,1,0:T(8,128)(2,1)}, bf16[8,128,512]{2,1,0:T(8,128)(2,1)}) custom-call(s32[75]{0:T(128)} %get-tuple-element.73.table_ref, bf16[16,128,512]{2,1,0:T(8,128)(2,1)} %refs_0_.19, bf16[4,128,512]{2,1,0:T(8,128)(2,1)} %copy-done.7, bf16[4,128,512]{2,1,0:T(8,128)(2,1)} %copy-done.11, bf16[4,128,512]{2,1,0:T(8,128)(2,1)} %collective-permute-done.4.refs_3_, ...), custom_call_target="tpu_custom_call" | custom-call | bytes 4194304 | tf_op jit(solution)/shard_map/pack/pallas_call | solution.py:151
  89.8 45.1 %collective-permute-start.10 = (bf16[4,128,512]{2,1,0:T(8,128)(2,1)}, bf16[4,128,512]{2,1,0:T(8,128)(2,1)S(1)}, u32[]{:S(2)}, u32[]{:S(2)}) collective-permute-start(bf16[4,128,512]{2,1,0:T(8,128)(2,1)} %get-tuple-element.150), channel_id=1, source_target_pairs={{0,4},{2,6},{12,8},{14,10},{1,5},{3,7},{13,9},{15,11},{16,20},{18,... | collective-permute-start | bytes 1572872 | tf_op jit(solution)/shard_map/ppermute | solution.py:524
  136.3 8.2 %collective-permute-start.17 = (bf16[4,128,512]{2,1,0:T(8,128)(2,1)}, bf16[4,128,512]{2,1,0:T(8,128)(2,1)S(1)}, u32[]{:S(2)}, u32[]{:S(2)}) collective-permute-start(bf16[4,128,512]{2,1,0:T(8,128)(2,1)} %get-tuple-element.149), channel_id=1, source_target_pairs={{0,4},{2,6},{12,8},{14,10},{1,5},{3,7},{13,9},{15,11},{16,20},{18,... | collective-permute-start | bytes 1572872 | tf_op jit(solution)/shard_map/ppermute | solution.py:524
  144.5 1.5 collective-permute-start.18
  146.0 3.4 collective-permute-done.8.refs_10_.refs_5_.refs_13_.refs_14_
  150.3 18.0 %pack.8 = (bf16[8,128,512]{2,1,0:T(8,128)(2,1)}, bf16[8,128,512]{2,1,0:T(8,128)(2,1)}) custom-call(s32[75]{0:T(128)} %get-tuple-element.73.table_ref, bf16[16,128,512]{2,1,0:T(8,128)(2,1)} %refs_0_.19, bf16[4,128,512]{2,1,0:T(8,128)(2,1)} %copy-done.7, bf16[4,128,512]{2,1,0:T(8,128)(2,1)} %copy-done.11, bf16[4,128,512]{2,1,0:T(8,128)(2,1)} %collective-permute-done.4.refs_3_, ...), custom_call_target="tpu_custom_call" | custom-call | bytes 4194304 | tf_op jit(solution)/shard_map/pack/pallas_call | solution.py:151
  169.7 2.0 collective-permute-start.14
  172.7 1.6 collective-permute-start.16
  175.8 46.2 %collective-permute-done.12.refs_6_.refs_14_.refs_15_ = bf16[8,128,512]{2,1,0:T(8,128)(2,1)} collective-permute-done((bf16[8,128,512]{2,1,0:T(8,128)(2,1)}, bf16[8,128,512]{2,1,0:T(8,128)(2,1)}, u32[]{:S(2)}, u32[]{:S(2)}) %collective-permute-start.12) | collective-permute-done | bytes 1048608 | tf_op jit(solution)/shard_map/ppermute | solution.py:524
  222.0 14.0 %pack.9 = (bf16[5,128,512]{2,1,0:T(8,128)(2,1)}, bf16[8,128,512]{2,1,0:T(8,128)(2,1)}) custom-call(s32[75]{0:T(128)} %get-tuple-element.73.table_ref, bf16[16,128,512]{2,1,0:T(8,128)(2,1)} %refs_0_.19, bf16[4,128,512]{2,1,0:T(8,128)(2,1)} %copy-done.7, bf16[4,128,512]{2,1,0:T(8,128)(2,1)} %copy-done.11, bf16[4,128,512]{2,1,0:T(8,128)(2,1)} %collective-permute-done.4.refs_3_, ...), custom_call_target="tpu_custom_call" | custom-call | bytes 3407872 | tf_op jit(solution)/shard_map/pack/pallas_call | solution.py:151
  237.4 2.9 collective-permute-done.15.refs_9_.refs_10_.refs_11_
  240.3 13.2 %agent_stage.6 = (f32[4,128,512]{2,1,0:T(8,128)S(1)}, bf16[4,128,512]{2,1,0:T(8,128)(2,1)}) custom-call(s32[32]{0:T(128)S(1)} %copy-done.28, bf16[16,128,512]{2,1,0:T(8,128)(2,1)} %refs_0_.19, bf16[16,128,512]{2,1,0:T(8,128)(2,1)} %refs_0_.19, bf16[4,128,512]{2,1,0:T(8,128)(2,1)S(1)} %copy-done.8, bf16[4,128,512]{2,1,0:T(8,128)(2,1)S(1)} %copy-done.12, ...), custom_call_target="tpu_custom_call" | custom-call | flops 18790481920 | bytes 3145728 | tf_op jit(solution)/shard_map/agent_stage/pallas_call | solution.py:106
  254.5 7.7 %collective-permute-start.25 = (bf16[4,128,512]{2,1,0:T(8,128)(2,1)}, bf16[4,128,512]{2,1,0:T(8,128)(2,1)}, u32[]{:S(2)}, u32[]{:S(2)}) collective-permute-start(bf16[4,128,512]{2,1,0:T(8,128)(2,1)} %get-tuple-element.88), channel_id=1, source_target_pairs={{0,1},{2,3},{4,5},{6,7},{8,9},{10,11},{12,13},{14,15},{16,17},{18,... | collective-permute-start | bytes 1572872 | tf_op jit(solution)/shard_map/ppermute | solution.py:602
  262.2 6.9 %collective-permute-done.19.refs_7_.refs_16_ = bf16[5,128,512]{2,1,0:T(8,128)(2,1)} collective-permute-done((bf16[5,128,512]{2,1,0:T(8,128)(2,1)}, bf16[5,128,512]{2,1,0:T(8,128)(2,1)}, u32[]{:S(2)}, u32[]{:S(2)}) %collective-permute-start.19) | collective-permute-done | bytes 655392 | tf_op jit(solution)/shard_map/ppermute | solution.py:524
  269.1 21.9 %pack.10 = (bf16[5,128,512]{2,1,0:T(8,128)(2,1)}, bf16[5,128,512]{2,1,0:T(8,128)(2,1)}) custom-call(s32[75]{0:T(128)} %get-tuple-element.73.table_ref, bf16[16,128,512]{2,1,0:T(8,128)(2,1)} %refs_0_.19, bf16[4,128,512]{2,1,0:T(8,128)(2,1)} %copy-done.7, bf16[4,128,512]{2,1,0:T(8,128)(2,1)} %copy-done.11, ...), custom_call_target="tpu_custom_call" | custom-call | bytes 2621440 | tf_op jit(solution)/shard_map/pack/pallas_call | solution.py:151
  293.5 13.3 %agent_stage.7 = (f32[4,128,512]{2,1,0:T(8,128)S(1)}, bf16[4,128,512]{2,1,0:T(8,128)(2,1)}) custom-call(s32[32]{0:T(128)S(1)} %copy-done.28, bf16[16,128,512]{2,1,0:T(8,128)(2,1)} %refs_0_.19, bf16[16,128,512]{2,1,0:T(8,128)(2,1)} %refs_0_.19, bf16[4,128,512]{2,1,0:T(8,128)(2,1)S(1)} %copy-done.10, bf16[4,128,512]{2,1,0:T(8,128)(2,1)S(1)} %copy-done.14, ...), custom_call_target="tpu_custom_call" | custom-call | flops 18790481920 | bytes 3145728 | tf_op jit(solution)/shard_map/agent_stage/pallas_call | solution.py:106
  307.8 8.3 %collective-permute-start.26 = (bf16[4,128,512]{2,1,0:T(8,128)(2,1)}, bf16[4,128,512]{2,1,0:T(8,128)(2,1)}, u32[]{:S(2)}, u32[]{:S(2)}) collective-permute-start(bf16[4,128,512]{2,1,0:T(8,128)(2,1)} %get-tuple-element.89), channel_id=1, source_target_pairs={{0,1},{2,3},{4,5},{6,7},{8,9},{10,11},{12,13},{14,15},{16,17},{18,... | collective-permute-start | bytes 1572872 | tf_op jit(solution)/shard_map/ppermute | solution.py:602
  316.1 13.2 %collective-permute-done.22.refs_8_.refs_17_ = bf16[5,128,512]{2,1,0:T(8,128)(2,1)} collective-permute-done((bf16[5,128,512]{2,1,0:T(8,128)(2,1)}, bf16[5,128,512]{2,1,0:T(8,128)(2,1)}, u32[]{:S(2)}, u32[]{:S(2)}) %collective-permute-start.22) | collective-permute-done | bytes 655392 | tf_op jit(solution)/shard_map/ppermute | solution.py:524
  330.3 13.1 %agent_stage.8 = (f32[4,128,512]{2,1,0:T(8,128)S(1)}, bf16[4,128,512]{2,1,0:T(8,128)(2,1)}) custom-call(s32[32]{0:T(128)S(1)} %copy-done.28, bf16[16,128,512]{2,1,0:T(8,128)(2,1)} %refs_0_.19, bf16[16,128,512]{2,1,0:T(8,128)(2,1)} %refs_0_.19, bf16[4,128,512]{2,1,0:T(8,128)(2,1)S(1)} %copy-done.16, bf16[4,128,512]{2,1,0:T(8,128)(2,1)S(1)} %copy-done.18, ...), custom_call_target="tpu_custom_call" | custom-call | flops 18790481920 | bytes 3145728 | tf_op jit(solution)/shard_map/agent_stage/pallas_call | solution.py:106
  343.5 5.8 %collective-permute-start.27 = (bf16[4,128,512]{2,1,0:T(8,128)(2,1)}, bf16[4,128,512]{2,1,0:T(8,128)(2,1)}, u32[]{:S(2)}, u32[]{:S(2)}) collective-permute-start(bf16[4,128,512]{2,1,0:T(8,128)(2,1)} %get-tuple-element.90), channel_id=1, source_target_pairs={{0,1},{2,3},{4,5},{6,7},{8,9},{10,11},{12,13},{14,15},{16,17},{18,... | collective-permute-start | bytes 1572872 | tf_op jit(solution)/shard_map/ppermute | solution.py:602
  349.3 11.4 %agent_stage.9 = (f32[4,128,512]{2,1,0:T(8,128)S(1)}, bf16[4,128,512]{2,1,0:T(8,128)(2,1)}) custom-call(s32[32]{0:T(128)S(1)} %copy-done.28, bf16[16,128,512]{2,1,0:T(8,128)(2,1)S(1)} %copy-done.30, bf16[16,128,512]{2,1,0:T(8,128)(2,1)S(1)} %copy-done.30, bf16[4,128,512]{2,1,0:T(8,128)(2,1)S(1)} %copy-done.22, ...), custom_call_target="tpu_custom_call" | custom-call | flops 18790481920 | bytes 3145728 | tf_op jit(solution)/shard_map/agent_stage/pallas_call | solution.py:106
  361.7 2.1 collective-permute-start.28
  364.9 19.1 %time_stage.3 = (f32[16,128]{1,0:T(8,128)}, f32[2,128]{1,0:T(2,128)S(1)}) custom-call(s32[1]{0:T(128)} %bitcast.12.offset_ref, f32[4,128,512]{2,1,0:T(8,128)S(1)} %copy-done.24, f32[4,128,512]{2,1,0:T(8,128)S(1)} %copy-done.26, f32[4,128,512]{2,1,0:T(8,128)S(1)} %get-tuple-element.86.refs_2_, f32[4,128,512]{2,1,0:T(8,128)} %copy-done.27, ...), custom_call_target="tpu_custom_call" | custom-call | tf_op jit(solution)/shard_map/time_stage/pallas_call | solution.py:260
  385.3 58.4 %pmax.7 = s32[]{:T(128)} all-reduce(s32[]{:T(128)} %bitcast.11), channel_id=1, replica_groups=mesh['groups'=2,'agent'=8,'tm'=2] {'groups','agent','tm'}, use_global_device_ids=true, to_apply=%region_0.1 | all-reduce | flops 1 | bytes 8 | tf_op jit(solution)/shard_map/pmax | solution.py:627
  (127 shorter events, 26.3 us)
Async XLA Ops:
  3.7 40.0 %collective-permute-start.2 = (bf16[4,128,512]{2,1,0:T(8,128)(2,1)}, bf16[4,128,512]{2,1,0:T(8,128)(2,1)S(1)}, u32[]{:S(2)}, u32[]{:S(2)}) collective-permute-start(bf16[4,128,512]{2,1,0:T(8,128)(2,1)} %get-tuple-element.152), channel_id=1, source_target_pairs={{0,4},{2,6},{12,8},{14,10},{1,5},{3,7},{13,9},{15,11},{16,20},{18,... | collective-permute-start | bytes 1572872 | tf_op jit(solution)/shard_map/ppermute | solution.py:524
  36.4 25.3 %collective-permute-start.5 = (bf16[8,128,512]{2,1,0:T(8,128)(2,1)}, bf16[8,128,512]{2,1,0:T(8,128)(2,1)S(1)}, u32[]{:S(2)}, u32[]{:S(2)}) collective-permute-start(bf16[8,128,512]{2,1,0:T(8,128)(2,1)} %get-tuple-element.74), channel_id=1, source_target_pairs={{4,0},{6,2},{8,12},{10,14},{5,1},{7,3},{9,13},{11,15},{20,16},{22,... | collective-permute-start | bytes 3145736 | tf_op jit(solution)/shard_map/ppermute | solution.py:524
  37.7 14.1 %collective-permute-start.6 = (bf16[4,128,512]{2,1,0:T(8,128)(2,1)}, bf16[4,128,512]{2,1,0:T(8,128)(2,1)S(1)}, u32[]{:S(2)}, u32[]{:S(2)}) collective-permute-start(bf16[4,128,512]{2,1,0:T(8,128)(2,1)} %get-tuple-element.151), channel_id=1, source_target_pairs={{0,4},{2,6},{12,8},{14,10},{1,5},{3,7},{13,9},{15,11},{16,20},{18,... | collective-permute-start | bytes 1572872 | tf_op jit(solution)/shard_map/ppermute | solution.py:524
  42.3 9.4 %collective-permute-start.3 = (bf16[4,128,512]{2,1,0:T(8,128)(2,1)}, bf16[4,128,512]{2,1,0:T(8,128)(2,1)S(1)}, u32[]{:S(2)}, u32[]{:S(2)}) collective-permute-start(bf16[4,128,512]{2,1,0:T(8,128)(2,1)} %get-tuple-element.152), channel_id=1, source_target_pairs={{4,8},{6,10},{8,4},{10,6},{5,9},{7,11},{9,5},{11,7},{20,24},{22,26... | collective-permute-start | bytes 1572872 | tf_op jit(solution)/shard_map/ppermute | solution.py:524
  43.0 8.8 %collective-permute-start.7 = (bf16[4,128,512]{2,1,0:T(8,128)(2,1)}, bf16[4,128,512]{2,1,0:T(8,128)(2,1)S(1)}, u32[]{:S(2)}, u32[]{:S(2)}) collective-permute-start(bf16[4,128,512]{2,1,0:T(8,128)(2,1)} %get-tuple-element.151), channel_id=1, source_target_pairs={{4,8},{6,10},{8,4},{10,6},{5,9},{7,11},{9,5},{11,7},{20,24},{22,26... | collective-permute-start | bytes 1572872 | tf_op jit(solution)/shard_map/ppermute | solution.py:524
  43.7 17.9 %collective-permute-start.4 = (bf16[4,128,512]{2,1,0:T(8,128)(2,1)S(1)}, bf16[4,128,512]{2,1,0:T(8,128)(2,1)}, u32[]{:S(2)}, u32[]{:S(2)}) collective-permute-start(bf16[4,128,512]{2,1,0:T(8,128)(2,1)S(1)} %collective-permute-done.2.refs_1_), channel_id=1, source_target_pairs={{4,8},{6,10},{8,4},{10,6},{5,9},{7,11},{9,5},{11,7},{20,24},{22,26... | collective-permute-start | bytes 1572872 | tf_op jit(solution)/shard_map/ppermute | solution.py:524
  88.5 60.8 %collective-permute-start.8 = (bf16[8,128,512]{2,1,0:T(8,128)(2,1)}, bf16[8,128,512]{2,1,0:T(8,128)(2,1)S(1)}, u32[]{:S(2)}, u32[]{:S(2)}) collective-permute-start(bf16[8,128,512]{2,1,0:T(8,128)(2,1)} %get-tuple-element.75), channel_id=1, source_target_pairs={{4,0},{6,2},{8,12},{10,14},{5,1},{7,3},{9,13},{11,15},{20,16},{22,... | collective-permute-start | bytes 3145736 | tf_op jit(solution)/shard_map/ppermute | solution.py:524
  89.8 54.6 %collective-permute-start.10 = (bf16[4,128,512]{2,1,0:T(8,128)(2,1)}, bf16[4,128,512]{2,1,0:T(8,128)(2,1)S(1)}, u32[]{:S(2)}, u32[]{:S(2)}) collective-permute-start(bf16[4,128,512]{2,1,0:T(8,128)(2,1)} %get-tuple-element.150), channel_id=1, source_target_pairs={{0,4},{2,6},{12,8},{14,10},{1,5},{3,7},{13,9},{15,11},{16,20},{18,... | collective-permute-start | bytes 1572872 | tf_op jit(solution)/shard_map/ppermute | solution.py:524
  134.9 11.1 %collective-permute-start.11 = (bf16[4,128,512]{2,1,0:T(8,128)(2,1)}, bf16[4,128,512]{2,1,0:T(8,128)(2,1)S(1)}, u32[]{:S(2)}, u32[]{:S(2)}) collective-permute-start(bf16[4,128,512]{2,1,0:T(8,128)(2,1)} %get-tuple-element.150), channel_id=1, source_target_pairs={{4,8},{6,10},{8,4},{10,6},{5,9},{7,11},{9,5},{11,7},{20,24},{22,26... | collective-permute-start | bytes 1572872 | tf_op jit(solution)/shard_map/ppermute | solution.py:524
  135.6 10.4 %collective-permute-start.9 = (bf16[4,128,512]{2,1,0:T(8,128)(2,1)}, bf16[4,128,512]{2,1,0:T(8,128)(2,1)S(1)}, u32[]{:S(2)}, u32[]{:S(2)}) collective-permute-start(bf16[4,128,512]{2,1,0:T(8,128)(2,1)} %copy-done.9), channel_id=1, source_target_pairs={{4,8},{6,10},{8,4},{10,6},{5,9},{7,11},{9,5},{11,7},{20,24},{22,26... | collective-permute-start | bytes 1572872 | tf_op jit(solution)/shard_map/ppermute | solution.py:524
  136.3 35.4 %collective-permute-start.17 = (bf16[4,128,512]{2,1,0:T(8,128)(2,1)}, bf16[4,128,512]{2,1,0:T(8,128)(2,1)S(1)}, u32[]{:S(2)}, u32[]{:S(2)}) collective-permute-start(bf16[4,128,512]{2,1,0:T(8,128)(2,1)} %get-tuple-element.149), channel_id=1, source_target_pairs={{0,4},{2,6},{12,8},{14,10},{1,5},{3,7},{13,9},{15,11},{16,20},{18,... | collective-permute-start | bytes 1572872 | tf_op jit(solution)/shard_map/ppermute | solution.py:524
  144.5 28.2 %collective-permute-start.18 = (bf16[4,128,512]{2,1,0:T(8,128)(2,1)}, bf16[4,128,512]{2,1,0:T(8,128)(2,1)}, u32[]{:S(2)}, u32[]{:S(2)}) collective-permute-start(bf16[4,128,512]{2,1,0:T(8,128)(2,1)} %get-tuple-element.149), channel_id=1, source_target_pairs={{4,8},{6,10},{8,4},{10,6},{5,9},{7,11},{9,5},{11,7},{20,24},{22,26... | collective-permute-start | bytes 1572872 | tf_op jit(solution)/shard_map/ppermute | solution.py:524
  168.3 53.7 %collective-permute-start.12 = (bf16[8,128,512]{2,1,0:T(8,128)(2,1)}, bf16[8,128,512]{2,1,0:T(8,128)(2,1)}, u32[]{:S(2)}, u32[]{:S(2)}) collective-permute-start(bf16[8,128,512]{2,1,0:T(8,128)(2,1)} %get-tuple-element.76), channel_id=1, source_target_pairs={{4,0},{6,2},{8,12},{10,14},{5,1},{7,3},{9,13},{11,15},{20,16},{22,... | collective-permute-start | bytes 3145736 | tf_op jit(solution)/shard_map/ppermute | solution.py:524
  169.6 67.7 %collective-permute-start.13 = (bf16[8,128,512]{2,1,0:T(8,128)(2,1)}, bf16[8,128,512]{2,1,0:T(8,128)(2,1)}, u32[]{:S(2)}, u32[]{:S(2)}) collective-permute-start(bf16[8,128,512]{2,1,0:T(8,128)(2,1)} %get-tuple-element.77), channel_id=1, source_target_pairs={{0,2},{2,0},{4,6},{6,4},{8,10},{10,8},{12,14},{14,12},{1,3},{3,1},... | collective-permute-start | bytes 3145736 | tf_op jit(solution)/shard_map/ppermute | solution.py:524
  169.7 67.7 %collective-permute-start.14 = (bf16[8,128,512]{2,1,0:T(8,128)(2,1)}, bf16[8,128,512]{2,1,0:T(8,128)(2,1)}, u32[]{:S(2)}, u32[]{:S(2)}) collective-permute-start(bf16[8,128,512]{2,1,0:T(8,128)(2,1)} %get-tuple-element.78), channel_id=1, source_target_pairs={{0,2},{2,0},{4,6},{6,4},{8,10},{10,8},{12,14},{14,12},{1,3},{3,1},... | collective-permute-start | bytes 3145736 | tf_op jit(solution)/shard_map/ppermute | solution.py:524
  172.5 67.7 %copy-start.5 = (bf16[8,128,512]{2,1,0:T(8,128)(2,1)S(1)}, bf16[8,128,512]{2,1,0:T(8,128)(2,1)}, u32[]{:S(2)}) copy-start(bf16[8,128,512]{2,1,0:T(8,128)(2,1)} %copy-done.4) | copy-start | bytes 3145732
  172.5 67.7 %copy-start.8 = (bf16[4,128,512]{2,1,0:T(8,128)(2,1)S(1)}, bf16[4,128,512]{2,1,0:T(8,128)(2,1)}, u32[]{:S(2)}) copy-start(bf16[4,128,512]{2,1,0:T(8,128)(2,1)} %copy-done.7) | copy-start | bytes 1572868
  172.5 67.7 %copy-start.12 = (bf16[4,128,512]{2,1,0:T(8,128)(2,1)S(1)}, bf16[4,128,512]{2,1,0:T(8,128)(2,1)}, u32[]{:S(2)}) copy-start(bf16[4,128,512]{2,1,0:T(8,128)(2,1)} %copy-done.11) | copy-start | bytes 1572868
  172.5 67.7 %copy-start.28 = (s32[32]{0:T(128)S(1)}, s32[32]{0:T(128)}, u32[]{:S(2)}) copy-start(s32[32]{0:T(128)} %get-tuple-element.72.table_ref) | copy-start | bytes 388
  172.5 67.7 %collective-permute-start.15 = (bf16[8,128,512]{2,1,0:T(8,128)(2,1)}, bf16[8,128,512]{2,1,0:T(8,128)(2,1)}, u32[]{:S(2)}, u32[]{:S(2)}) collective-permute-start(bf16[8,128,512]{2,1,0:T(8,128)(2,1)} %get-tuple-element.79), channel_id=1, source_target_pairs={{0,2},{2,0},{4,6},{6,4},{8,10},{10,8},{12,14},{14,12},{1,3},{3,1},... | collective-permute-start | bytes 3145736 | tf_op jit(solution)/shard_map/ppermute | solution.py:524
  172.7 1.6 collective-permute-start.16
  174.3 87.9 %collective-permute-start.21 = (bf16[4,128,512]{2,1,0:T(8,128)(2,1)}, bf16[4,128,512]{2,1,0:T(8,128)(2,1)}, u32[]{:S(2)}, u32[]{:S(2)}) collective-permute-start(bf16[4,128,512]{2,1,0:T(8,128)(2,1)} %copy-done.21), channel_id=1, source_target_pairs={{4,8},{6,10},{8,4},{10,6},{5,9},{7,11},{9,5},{11,7},{20,24},{22,26... | collective-permute-start | bytes 1572872 | tf_op jit(solution)/shard_map/ppermute | solution.py:524
  236.0 33.1 %collective-permute-start.19 = (bf16[5,128,512]{2,1,0:T(8,128)(2,1)}, bf16[5,128,512]{2,1,0:T(8,128)(2,1)}, u32[]{:S(2)}, u32[]{:S(2)}) collective-permute-start(bf16[5,128,512]{2,1,0:T(8,128)(2,1)} %get-tuple-element.81), channel_id=1, source_target_pairs={{4,0},{6,2},{8,12},{10,14},{5,1},{7,3},{9,13},{11,15},{20,16},{22,... | collective-permute-start | bytes 1966088 | tf_op jit(solution)/shard_map/ppermute | solution.py:524
  237.3 55.1 %collective-permute-start.20 = (bf16[8,128,512]{2,1,0:T(8,128)(2,1)}, bf16[8,128,512]{2,1,0:T(8,128)(2,1)}, u32[]{:S(2)}, u32[]{:S(2)}) collective-permute-start(bf16[8,128,512]{2,1,0:T(8,128)(2,1)} %get-tuple-element.82), channel_id=1, source_target_pairs={{0,2},{2,0},{4,6},{6,4},{8,10},{10,8},{12,14},{14,12},{1,3},{3,1},... | collective-permute-start | bytes 3145736 | tf_op jit(solution)/shard_map/ppermute | solution.py:524
  254.5 109.3 %collective-permute-start.25 = (bf16[4,128,512]{2,1,0:T(8,128)(2,1)}, bf16[4,128,512]{2,1,0:T(8,128)(2,1)}, u32[]{:S(2)}, u32[]{:S(2)}) collective-permute-start(bf16[4,128,512]{2,1,0:T(8,128)(2,1)} %get-tuple-element.88), channel_id=1, source_target_pairs={{0,1},{2,3},{4,5},{6,7},{8,9},{10,11},{12,13},{14,15},{16,17},{18,... | collective-permute-start | bytes 1572872 | tf_op jit(solution)/shard_map/ppermute | solution.py:602
  291.0 38.3 %collective-permute-start.22 = (bf16[5,128,512]{2,1,0:T(8,128)(2,1)}, bf16[5,128,512]{2,1,0:T(8,128)(2,1)}, u32[]{:S(2)}, u32[]{:S(2)}) collective-permute-start(bf16[5,128,512]{2,1,0:T(8,128)(2,1)} %get-tuple-element.84), channel_id=1, source_target_pairs={{4,0},{6,2},{8,12},{10,14},{5,1},{7,3},{9,13},{11,15},{20,16},{22,... | collective-permute-start | bytes 1966088 | tf_op jit(solution)/shard_map/ppermute | solution.py:524
  292.3 38.0 %collective-permute-start.23 = (bf16[5,128,512]{2,1,0:T(8,128)(2,1)}, bf16[5,128,512]{2,1,0:T(8,128)(2,1)}, u32[]{:S(2)}, u32[]{:S(2)}) collective-permute-start(bf16[5,128,512]{2,1,0:T(8,128)(2,1)} %get-tuple-element.85), channel_id=1, source_target_pairs={{0,2},{2,0},{4,6},{6,4},{8,10},{10,8},{12,14},{14,12},{1,3},{3,1},... | collective-permute-start | bytes 1966088 | tf_op jit(solution)/shard_map/ppermute | solution.py:524
  307.8 56.0 %collective-permute-start.26 = (bf16[4,128,512]{2,1,0:T(8,128)(2,1)}, bf16[4,128,512]{2,1,0:T(8,128)(2,1)}, u32[]{:S(2)}, u32[]{:S(2)}) collective-permute-start(bf16[4,128,512]{2,1,0:T(8,128)(2,1)} %get-tuple-element.89), channel_id=1, source_target_pairs={{0,1},{2,3},{4,5},{6,7},{8,9},{10,11},{12,13},{14,15},{16,17},{18,... | collective-permute-start | bytes 1572872 | tf_op jit(solution)/shard_map/ppermute | solution.py:602
  330.2 19.1 %collective-permute-start.24 = (bf16[4,128,512]{2,1,0:T(8,128)(2,1)}, bf16[4,128,512]{2,1,0:T(8,128)(2,1)S(1)}, u32[]{:S(2)}, u32[]{:S(2)}) collective-permute-start(bf16[4,128,512]{2,1,0:T(8,128)(2,1)} %pack.11), channel_id=1, source_target_pairs={{0,2},{2,0},{4,6},{6,4},{8,10},{10,8},{12,14},{14,12},{1,3},{3,1},... | collective-permute-start | bytes 1572872 | tf_op jit(solution)/shard_map/ppermute | solution.py:524
  343.5 20.3 %collective-permute-start.27 = (bf16[4,128,512]{2,1,0:T(8,128)(2,1)}, bf16[4,128,512]{2,1,0:T(8,128)(2,1)}, u32[]{:S(2)}, u32[]{:S(2)}) collective-permute-start(bf16[4,128,512]{2,1,0:T(8,128)(2,1)} %get-tuple-element.90), channel_id=1, source_target_pairs={{0,1},{2,3},{4,5},{6,7},{8,9},{10,11},{12,13},{14,15},{16,17},{18,... | collective-permute-start | bytes 1572872 | tf_op jit(solution)/shard_map/ppermute | solution.py:602
  361.7 3.1 collective-permute-start.28
  384.0 60.3 %collective-permute-start.29 = (f32[2,128]{1,0:T(2,128)S(1)}, f32[2,128]{1,0:T(2,128)S(1)}, u32[]{:S(2)}, u32[]{:S(2)}) collective-permute-start(f32[2,128]{1,0:T(2,128)S(1)} %get-tuple-element.93), channel_id=1, source_target_pairs={{1,0},{3,2},{5,4},{7,6},{9,8},{11,10},{13,12},{15,14},{17,16},{19,... | collective-permute-start | bytes 3080 | tf_op jit(solution)/shard_map/ppermute | solution.py:616
  (36 other events, 609.0 us)

commit v3 on v2

--- a/solution.py
+++ b/solution.py
@@ -64,9 +64,9 @@
             pltpu.make_async_copy(ref.at[entry % SPAN], target, sem).start()
 
 
-def agent_kernel(list_length, first_step, codes, head_size, table_ref, own_ref, *refs):
+def agent_kernel(list_length, first_step, codes, idle, head_size, table_ref, own_ref, *refs):
     arrays = dict(zip(codes, refs))
-    proj_ref, merge_ref, residual_ref, normed_ref, held_ref, sems = refs[len(codes) :]
+    proj_ref, merge_ref, residual_ref, normed_ref, held_ref, sems = refs[len(codes) + idle :]
     width = own_ref.shape[-1]
     turn = pl.program_id(0)
 
@@ -98,20 +98,20 @@
     normed_ref[0] = rms(residual).astype(bf16)
 
 
-def agent_stage(embedded, arrays, table, first_step, steps, list_length, proj, merge):
+def agent_stage(embedded, arrays, table, first_step, steps, list_length, proj, merge, after=()):
     _, agents, width = embedded.shape
     piece = (1, agents, width)
     whole = lambda i, w: (0, 0)
     flops = 2 * steps * agents * width * width * (4 + 2 * list_length + 2 * (1 + list_length))
     return pl.pallas_call(
         functools.partial(
-            agent_kernel, list_length, first_step, tuple(arrays), width // HEADS
+            agent_kernel, list_length, first_step, tuple(arrays), len(after), width // HEADS
         ),
         grid_spec=pltpu.PrefetchScalarGridSpec(
             num_scalar_prefetch=1,
             grid=(steps,),
             in_specs=[pl.BlockSpec(piece, lambda i, w: (first_step + i, 0, 0))]
-            + [pl.BlockSpec(memory_space=pl.ANY)] * len(arrays)
+            + [pl.BlockSpec(memory_space=pl.ANY)] * (len(arrays) + len(after))
             + [pl.BlockSpec(proj.shape, whole), pl.BlockSpec(merge.shape, whole)],
             out_specs=[pl.BlockSpec(piece, lambda i, w: (i, 0, 0))] * 2,
             scratch_shapes=[
@@ -128,38 +128,63 @@
             flops=5 * flops, bytes_accessed=steps * agents * width * 12, transcendentals=0
         ),
         name="agent_stage",
-    )(table, embedded, *arrays.values(), proj, merge)
-
-
-def pack_kernel(codes, parts, table_ref, *refs):
+    )(table, embedded, *arrays.values(), *after, proj, merge)
+
+
+def pack_kernel(codes, parts, idle, table_ref, *refs):
     arrays = dict(zip(codes, refs))
-    outs, sems = refs[len(codes) : -1], refs[-1]
-    slots = [
-        (offset + n, out.at[n]) for out, (offset, count) in zip(outs, parts) for n in range(count)
-    ]
-    for n, (at, target) in enumerate(slots):
-        fetch(table_ref[at], arrays, target, sems.at[n])
-    for n, (at, target) in enumerate(slots):
-
-        @pl.when(table_ref[at] >= 0)
-        def _(n=n, target=target):
-            pltpu.make_async_copy(refs[0].at[0], target, sems.at[n]).wait()
-
-
-def pack(table, arrays, parts):
+    outs, (held_ref, in_sems, out_sems) = refs[len(codes) + idle : -3], refs[-3:]
+    slots = []
+    for out, (offset, count, first) in zip(outs, parts):
+        slots += [(offset, first, n, out.at[n]) for n in range(count)]
+
+    def guarded(offset, n, action):
+        if offset is None:
+            action()
+        else:
+            pl.when(table_ref[offset + n] >= 0)(action)
+
+    for at, (offset, first, n, _) in enumerate(slots):
+        if offset is None:
+            own = arrays[0].at[first + n]
+            pltpu.make_async_copy(own, held_ref.at[at], in_sems.at[at]).start()
+        else:
+            fetch(table_ref[offset + n], arrays, held_ref.at[at], in_sems.at[at])
+    for at, (offset, first, n, target) in enumerate(slots):
+
+        def pass_on(at=at, target=target):
+            pltpu.make_async_copy(refs[0].at[0], held_ref.at[at], in_sems.at[at]).wait()
+            pltpu.make_async_copy(held_ref.at[at], target, out_sems.at[at]).start()
+
+        guarded(offset, n, pass_on)
+    for at, (offset, first, n, target) in enumerate(slots):
+
+        def finish(at=at, target=target):
+            pltpu.make_async_copy(held_ref.at[at], target, out_sems.at[at]).wait()
+
+        guarded(offset, n, finish)
+
+
+def pack(table, arrays, parts, after=()):
     piece = next(iter(arrays.values())).shape[1:]
+    slots = sum(count for _, count, _ in parts)
     return pl.pallas_call(
-        functools.partial(pack_kernel, tuple(arrays), parts),
+        functools.partial(pack_kernel, tuple(arrays), tuple(parts), len(after)),
         in_specs=[pl.BlockSpec(memory_space=pltpu.SMEM)]
-        + [pl.BlockSpec(memory_space=pl.ANY)] * len(arrays),
+        + [pl.BlockSpec(memory_space=pl.ANY)] * (len(arrays) + len(after)),
         out_specs=[pl.BlockSpec(memory_space=pl.ANY)] * len(parts),
-        out_shape=[jax.ShapeDtypeStruct((count,) + piece, bf16) for _, count in parts],
-        scratch_shapes=[pltpu.SemaphoreType.DMA((sum(count for _, count in parts),))],
+        out_shape=[jax.ShapeDtypeStruct((count,) + piece, bf16) for _, count, _ in parts],
+        scratch_shapes=[
+            pltpu.VMEM((slots,) + piece, bf16),
+            pltpu.SemaphoreType.DMA((slots,)),
+            pltpu.SemaphoreType.DMA((slots,)),
+        ],
         cost_estimate=pl.CostEstimate(
-            flops=0, bytes_accessed=4 * sum(c for _, c in parts) * piece[0] * piece[1], transcendentals=0
+            flops=0, bytes_accessed=4 * slots * piece[0] * piece[1], transcendentals=0
         ),
+        compiler_params=pltpu.CompilerParams(vmem_limit_bytes=VMEM_LIMIT),
         name="pack",
-    )(table, *arrays.values())
+    )(table, *arrays.values(), *after)
 
 
 def suffix(values, rewards, done, next_value, next_advantage):
@@ -324,11 +349,17 @@
     return arrived.reshape(blocks * capacity, agents, width), named * capacity + slot
 
 
+OUTWARD_READY = {1: (0, 1), 2: (1, 3), 3: (2, 4)}
+ACROSS_READY = {0: (1, 2), 1: (0, 0), 2: (1, 3), 3: (2, 4)}
+OUTWARD_DUE = (3, 4)
+ACROSS_DUE = (3, 5)
+
+
 def relay_sizes(steps, capacity):
-    chunk = steps // 4
-    chunks = [chunk] * 4
-    outward = [2 * chunk] * 3 + [chunk + 1] * 2
-    across = [capacity] + [2 * chunk] * 3 + [chunk + 1, chunk]
+    half, quarter = steps // 2, steps // 4
+    chunks = [half, half]
+    outward = [half, half, half, half - 1, half]
+    across = [capacity - 2, half - 1, half, half - 1, quarter + 2, half - 1]
     return chunks, outward, across
 
 
@@ -336,16 +367,12 @@
     count = len(chunks)
     return {
         "own": 0,
-        "outer": [1 + k for k in range(count)],
+        "outer": [1 + 3 * count + k for k in range(count)],
         "inner": [1 + count + k for k in range(count)],
         "far": [1 + 2 * count + k for k in range(count)],
         "outward": [1 + 3 * count + b for b in range(len(outward))],
         "across": [1 + 3 * count + len(outward) + b for b in range(len(across))],
     }
-
-
-def relay_ready(count, k):
-    return max(1, k), k + 1
 
 
 def plan_kernel(steps, list_length, chunks, outward, across, place_ref, lists_ref, out_ref, in_ref, flag_ref, eloc, yloc, room):
@@ -367,6 +394,11 @@
 
     lax.fori_loop(0, sum(outward) + sum(across), clear, 0)
 
+    @pl.when(me == 0)
+    def _():
+        for n in range(chunks[1]):
+            out_ref[e_base[1] + n] = codes["own"] * SPAN + starts[1] + n
+
     def named(dest, t, source):
         hit = entry(dest, t, 0) == source
         for j in range(1, list_length):
@@ -392,18 +424,26 @@
     for turn in range(2):
         sender = row if turn == 0 else 1 - row
         empty(outward)
+        room[0] = outward[0]
         for k, count in enumerate(chunks):
-            ready = (0, 0) + relay_ready(len(chunks), k)
             held = (0, codes["own"] * SPAN + starts[k], codes["inner"][k] * SPAN, codes["far"][k] * SPAN)
             for u in (1, 2, 3):
 
-                def outer_piece(n, _, u=u, k=k, ready=ready, held=held):
+                def first_piece(n, _):
+                    eloc[(turn * COLUMNS + 1) * steps + n] = n
+                    return 0
+
+                if u == 1 and k == 0:
+                    lax.fori_loop(0, count, first_piece, 0)
+                    continue
+
+                def outer_piece(n, _, u=u, k=k, held=held):
                     t = starts[k] + n
                     source = block(mirror(u), sender)
                     need = named(block(mirror(0), 0), t, source)
                     for r in range(1, ROWS):
                         need = need | named(block(mirror(0), r), t, source)
-                    batch = choose(outward, ready[u])
+                    batch = choose(outward, OUTWARD_READY[u][k])
                     eloc[(turn * COLUMNS + u) * steps + t] = -1
 
                     @pl.when(need & (batch >= 0))
@@ -425,12 +465,10 @@
         sender = row if turn == 0 else 1 - row
         empty(across)
         for k, count in enumerate(chunks):
-            ready = relay_ready(len(chunks), k)
-            ready = (ready[0], 0) + ready
             held = (codes["outer"][k] * SPAN, codes["own"] * SPAN + starts[k], codes["inner"][k] * SPAN, codes["far"][k] * SPAN)
             for u in range(COLUMNS):
 
-                def row_piece(n, _, u=u, k=k, ready=ready, held=held):
+                def row_piece(n, _, u=u, k=k, held=held):
                     t = starts[k] + n
                     need = named(block(column, 1 - sender), t, block(mirror(u), sender))
                     if u == 0:
@@ -440,7 +478,7 @@
                         where = eloc[(turn * COLUMNS + u) * steps + t]
                         lies = codes["outward"][0] * SPAN + where
                         when = jnp.where(where < 0, len(across), where // SPAN + 1)
-                    when = jnp.where(inner, ready[u], when)
+                    when = jnp.where(inner, ACROSS_READY[u][k], when)
                     lies = jnp.where(inner, held[u] + n, lies)
                     batch = choose(across, when)
                     yloc[(turn * COLUMNS + u) * steps + t] = -1
@@ -473,8 +511,8 @@
             local = inner | (u == me)
             bad = jnp.where(
                 same,
-                jnp.logical_not(local) & ((e < 0) | (e // SPAN > min(k + 2, len(outward) - 1))),
-                (y < 0) | (y // SPAN > k + 2),
+                jnp.logical_not(local) & ((e < 0) | (e // SPAN > OUTWARD_DUE[k])),
+                (y < 0) | (y // SPAN > ACROSS_DUE[k]),
             )
             place = jnp.where(same, direct, codes["across"][0] * SPAN + y)
             in_ref[t * list_length + n % list_length] = jnp.where(bad, codes["own"] * SPAN, place)
@@ -509,63 +547,89 @@
     )(place, lists_all)
 
 
+def shared(value, axes):
+    count = lax.axis_size(axes)
+    rows = jnp.broadcast_to(value[None], (count,) + value.shape)
+    return lax.all_to_all(rows, axes, split_axis=0, concat_axis=0, tiled=True)
+
+
 def column_pairs(moves):
     return [(a * ROWS + r, b * ROWS + r) for a, b in moves for r in range(ROWS)]
 
 
-def relay(embedded, lists, capacity):
+def relay(embedded, lists, capacity, attention):
     steps, agents, width = embedded.shape
     list_length = lists.shape[1]
     chunks, outward, across = relay_sizes(steps, capacity)
     codes = relay_codes(chunks, outward, across)
     starts = [sum(chunks[:k]) for k in range(len(chunks))]
+    e_base = [sum(outward[:b]) for b in range(len(outward))]
+    y_base = [sum(outward) + sum(across[:b]) for b in range(len(across))]
     index = lax.axis_index("agent")
     place = jnp.stack([index // ROWS, index % ROWS]).astype(jnp.int32)
     send = lambda value, pairs: lax.ppermute(value, "agent", pairs)
-    inward = column_pairs([(0, 1), (3, 2)])
+    edges = column_pairs([(0, 1), (1, 0), (2, 3), (3, 2)])
     swap = column_pairs([(1, 2), (2, 1)])
-    away = column_pairs([(1, 0), (2, 3)])
     over = [(c * ROWS + r, c * ROWS + 1 - r) for c in range(COLUMNS) for r in range(ROWS)]
-    everyone = lax.all_gather(lists.reshape(-1), "agent", axis=0, tiled=True)
+    arrays = {codes["own"]: embedded}
+
+    def pick(names):
+        return {code: arrays[code] for code in names}
+
+    def outward_part(stage):
+        return (e_base[stage], outward[stage], None)
+
+    def across_part(stage):
+        return (y_base[stage], across[stage], None)
+
+    reads = [[codes["own"]] for _ in across]
+    for stage in range(1, len(across)):
+        reads[stage] += codes["outward"][: min(stage, len(outward))]
+        for name, u in (("inner", 2), ("far", 3)):
+            for k in range(len(chunks)):
+                if OUTWARD_READY[u][k] <= stage:
+                    reads[stage].append(codes[name][k])
+
+    settled = [(), (), (0, 1)] + [(stage - 1,) for stage in range(3, len(across))]
+    first = embedded[: chunks[0]]
+    arrays[codes["outward"][0]] = send(first, edges)
+    arrays[codes["inner"][0]] = send(first, swap)
+    everyone = shared(lists.reshape(-1), "agent").reshape(-1)
     out_table, in_table, flag = plan(
         everyone, place, steps, list_length, chunks, outward, across
     )
-    arrays = {codes["own"]: embedded}
-
-    def begin(k, part):
-        arrays[codes["outer"][k]] = send(part, inward)
-        arrays[codes["inner"][k]] = send(part, swap)
-        arrays[codes["far"][k]] = send(arrays[codes["outer"][k]], swap)
-
-    def own_part(k):
-        return embedded[starts[k] : starts[k] + chunks[k]]
-
-    for k in range(len(chunks)):
-        begin(k, own_part(k))
-    e_base = [sum(outward[:b]) for b in range(len(outward))]
-    y_base = [sum(outward) + sum(across[:b]) for b in range(len(across))]
-    for stage in range(len(across)):
-        known = {codes["own"]: embedded}
-        for k in range(len(chunks)):
-            near, far = relay_ready(len(chunks), k)
-            if near <= stage:
-                known[codes["outer"][k]] = arrays[codes["outer"][k]]
-                known[codes["inner"][k]] = arrays[codes["inner"][k]]
-            if far <= stage:
-                known[codes["far"][k]] = arrays[codes["far"][k]]
-        for b in range(min(stage, len(outward))):
-            known[codes["outward"][b]] = arrays[codes["outward"][b]]
-        parts = [(e_base[stage], outward[stage])] if stage < len(outward) else []
-        packed = pack(out_table, known, tuple(parts + [(y_base[stage], across[stage])]))
-        if parts:
-            arrays[codes["outward"][stage]] = send(packed[0], away)
-        arrays[codes["across"][stage]] = send(packed[-1], over)
-    work = []
-    for k in range(len(chunks)):
-        wanted = [codes["own"], codes["outer"][k], codes["inner"][k], codes["far"][k]]
-        wanted += codes["outward"][: k + 3] + codes["across"][: k + 3]
-        work.append((starts[k], chunks[k], {code: arrays[code] for code in wanted}))
-    return work, in_table, flag
+    (packed,) = pack(out_table, pick(reads[0]), [across_part(0)])
+    arrays[codes["across"][0]] = send(packed, over)
+    arrays[codes["far"][0]] = send(arrays[codes["outward"][0]], swap)
+    done, after = [], ()
+    for stage in range(1, len(across)):
+        parts = [across_part(stage)]
+        if stage < len(outward):
+            parts.append(outward_part(stage))
+        if stage == 1:
+            parts.append((None, chunks[1], starts[1]))
+        if stage == len(across) - 1:
+            done.append(attention(0, chunks[0], due(arrays, codes, 0), in_table, after))
+            after = (done[0][0],)
+        else:
+            after += tuple(arrays[codes["across"][b]] for b in settled[stage])
+        packed = pack(out_table, pick(reads[stage]), parts, after)
+        arrays[codes["across"][stage]] = send(packed[0], over)
+        if stage < len(outward):
+            arrays[codes["outward"][stage]] = send(packed[1], edges)
+        if stage == 1:
+            arrays[codes["inner"][1]] = send(packed[2], swap)
+            arrays[codes["far"][1]] = send(arrays[codes["outward"][1]], swap)
+            crowded = jnp.max(shared(flag, ("groups", "agent", "tm")))
+        after = (crowded.reshape(1),) if stage == 2 else ()
+    done.append(attention(starts[1], chunks[1], due(arrays, codes, 1), in_table, ()))
+    return done, crowded
+
+
+def due(arrays, codes, k):
+    wanted = [codes["own"], codes["inner"][k], codes["far"][k]]
+    wanted += codes["outward"][: OUTWARD_DUE[k] + 1] + codes["across"][: ACROSS_DUE[k] + 1]
+    return {code: arrays[code] for code in wanted}
 
 
 def body(
@@ -592,14 +656,14 @@
     forward = [(i, i + 1) for i in range(spans - 1)]
     backward = [(i + 1, i) for i in range(spans - 1)]
 
-    def finish(work, table):
-        residuals, rims = [], []
-        for first, count, arrays in work:
-            residual, normed = agent_stage(
-                embedded, arrays, table, first, count, list_length, agent_proj, agent_merge
-            )
-            residuals.append(residual)
-            rims.append(lax.ppermute(normed, "tm", forward))
+    def attention(first, count, arrays, table, after=()):
+        residual, normed = agent_stage(
+            embedded, arrays, table, first, count, list_length, agent_proj, agent_merge, after
+        )
+        return residual, lax.ppermute(normed, "tm", forward)
+
+    def finish(done):
+        residuals, rims = [part[0] for part in done], [part[1] for part in done]
         values, edge = time_stage(
             residuals,
             rims,
@@ -619,13 +683,12 @@
 
     def padded():
         pool, where = exchange_slots(embedded, lists, capacity)
-        return finish([(0, steps, {1: pool})], where + SPAN)
+        return finish([attention(0, steps, {1: pool}, where + SPAN)])
 
     if blocks != COLUMNS * ROWS or steps % 4:
         return padded()
-    work, table, flag = relay(embedded, lists, capacity)
-    crowded = lax.pmax(flag[0], ("groups", "agent", "tm"))
-    found = finish(work, table)
+    done, crowded = relay(embedded, lists, capacity, attention)
+    found = finish(done)
     return lax.cond(crowded > 0, padded, lambda: found)
 
 

time: 450 us -> 267 us (0.59)
  starting transfers between devices: 106 us -> 33.9 us
  Pallas kernels: 162 us -> 90.1 us
  blocking collectives: 73.8 us -> 22.9 us
  waiting for transfers between devices: 90 us -> 109 us
  local copies, waits for them, and re-layouts: 11.6 us -> 6.31 us
    pallas_call x6, Pallas kernels: 82.2 us -> 16.6 us  [pack(): pl.pallas_call(functools.partial(pack_kernel, tuple(arrays), tuple(parts)...]
    pmax x1 -> x0, blocking collectives: 58.4 us -> none  [body(): crowded = lax.pmax(flag[0], ('groups', 'agent', 'tm'))]
    ppermute x23 -> x15, starting transfers between devices: 80.5 us -> 22.2 us  [relay(): send = lambda value, pairs: lax.ppermute(value, 'agent', pairs)]
    all_to_all x0 -> x1, blocking collectives: none -> 22.9 us  [shared(): return lax.all_to_all(rows, axes, split_axis=0, concat_axis=0, tiled=True)]
    ppermute x4 -> x2, starting transfers between devices: 23.9 us -> 3.79 us  [attention(): return (residual, lax.ppermute(normed, 'tm', forward))]
    all_to_all x0 -> x1, waiting for transfers between devices: none -> 19.6 us  [shared(): return lax.all_to_all(rows, axes, split_axis=0, concat_axis=0, tiled=True)]
    unnamed x1 -> x0, blocking collectives: 15.4 us -> none
    all_to_all x0 -> x1, starting transfers between devices: none -> 6.57 us  [shared(): return lax.all_to_all(rows, axes, split_axis=0, concat_axis=0, tiled=True)]
  transfers between devices with their start and end apart: 28 -> 19, of which waited for: 8 -> 7; matrix products, arithmetic and copies ran while one was open for 0% -> 2% of each run, Pallas kernels for 26% -> 23%
where the time goes in v3:
time: 267 us; the launch traced here: 265 us
  waiting for transfers between devices  109 us (41%)
  Pallas kernels  90.1 us (34%)
  starting transfers between devices  33.9 us (13%)
  blocking collectives  22.9 us (9%)
  local copies, waits for them, and re-layouts  6.31 us (2%)
    ppermute x15, waiting for transfers between devices, relay(): send = lambda value, pairs: lax.ppermute(value, 'agent', pairs)  86.3 us
    pallas_call x2, Pallas kernels, agent_stage(): pl.pallas_call(functools.partial(agent_kernel, list_length, first_step, t...  45.1 us
    all_to_all x1, blocking collectives, shared(): return lax.all_to_all(rows, axes, split_axis=0, concat_axis=0, tiled=True)  22.9 us
    ppermute x15, starting transfers between devices, relay(): send = lambda value, pairs: lax.ppermute(value, 'agent', pairs)  22.2 us
    all_to_all x1, waiting for transfers between devices, shared(): return lax.all_to_all(rows, axes, split_axis=0, concat_axis=0, tiled=True)  19.6 us
    pallas_call x1, Pallas kernels, time_stage(): pl.pallas_call(functools.partial(time_kernel, len(residuals), steps, tile...  18.9 us
    pallas_call x6, Pallas kernels, pack(): pl.pallas_call(functools.partial(pack_kernel, tuple(arrays), tuple(parts)...  16.6 us
    pallas_call x1, Pallas kernels, plan(): pl.pallas_call(functools.partial(plan_kernel, steps, list_length, chunks,...  8.2 us
  transfers between devices with their start and end apart: 19, of which 7 were waited for; matrix products, arithmetic and copies ran while one was open for 2% of the time, Pallas kernels for 23%

profile of v3, /device:TPU:0, one launch (start us, length us, event | category | flops | bytes accessed | tf_op | source)
XLA Modules:
  0.0 265.5 jit_solution(16083361020474708327)
XLA Ops:
  0.6 1.3 slice.3
  2.0 3.1 %collective-permute-start.3 = (bf16[8,128,512]{2,1,0:T(8,128)(2,1)S(1)}, bf16[8,128,512]{2,1,0:T(8,128)(2,1)S(1)}, u32[]{:S(2)}, u32[]{:S(2)}) collective-permute-start(bf16[8,128,512]{2,1,0:T(8,128)(2,1)S(1)} %slice.3), channel_id=1, source_target_pairs={{0,4},{2,6},{4,0},{6,2},{8,12},{10,14},{12,8},{14,10},{1,5},{3,7},... | collective-permute-start | bytes 3145736 | tf_op jit(solution)/shard_map/ppermute | solution.py:570
  6.6 6.6 %all-to-all-start.2 = ((s32[8,1,32]{2,1,0:T(1,128)}), s32[8,1,32]{2,1,0:T(1,128)S(1)}, u32[]{:S(2)}, u32[]{:S(2)}) async-start(s32[8,1,32]{2,1,0:T(1,128)} %broadcast_in_dim.9), calls=%async_computation.2 | async-start | bytes 8192 | tf_op jit(solution)/shard_map/all_to_all | solution.py:553
  13.8 19.6 %all-to-all-done.2 = s32[8,1,32]{2,1,0:T(1,128)S(1)} async-done(((s32[8,1,32]{2,1,0:T(1,128)}), s32[8,1,32]{2,1,0:T(1,128)S(1)}, u32[]{:S(2)}, u32[]{:S(2)}) %all-to-all-start.2) | async-done | bytes 1056 | tf_op jit(solution)/shard_map/all_to_all | solution.py:553
  35.2 8.2 %plan.1 = (s32[80]{0:T(128)}, s32[32]{0:T(128)}, s32[1]{0:T(128)}) custom-call(s32[2]{0:T(128)} %pad_add_fusion.place_ref, s32[256]{0:T(256)} %reshape.157.lists_ref), custom_call_target="tpu_custom_call" | custom-call | tf_op jit(solution)/shard_map/plan/pallas_call | solution.py:532
  44.2 4.9 %pack.6 = (bf16[7,128,512]{2,1,0:T(8,128)(2,1)S(1)}, bf16[8,128,512]{2,1,0:T(8,128)(2,1)S(1)}, bf16[8,128,512]{2,1,0:T(8,128)(2,1)}) custom-call(s32[80]{0:T(128)S(1)} %copy-done.13, bf16[16,128,512]{2,1,0:T(8,128)(2,1)} %refs_0_.15, bf16[8,128,512]{2,1,0:T(8,128)(2,1)S(1)} %collective-permute-done.3.refs_1_.refs_3_, ...), custom_call_target="tpu_custom_call" | custom-call | bytes 6029312 | tf_op jit(solution)/shard_map/pack/pallas_call | solution.py:171
  50.8 1.5 collective-permute-start.7
  52.3 2.8 %pack.7 = bf16[6,128,512]{2,1,0:T(8,128)(2,1)S(1)} custom-call(s32[80]{0:T(128)S(1)} %copy-done.13, bf16[16,128,512]{2,1,0:T(8,128)(2,1)S(1)} %copy-done.16), custom_call_target="tpu_custom_call" | custom-call | bytes 1572864 | tf_op jit(solution)/shard_map/pack/pallas_call | solution.py:171
  55.3 1.8 collective-permute-start.9
  57.1 31.7 %collective-permute-done.6.refs_5_.refs_7_.refs_8_ = bf16[6,128,512]{2,1,0:T(8,128)(2,1)S(1)} collective-permute-done((bf16[6,128,512]{2,1,0:T(8,128)(2,1)S(1)}, bf16[6,128,512]{2,1,0:T(8,128)(2,1)S(1)}, u32[]{:S(2)}, u32[]{:S(2)}) %collective-permute-start.6) | collective-permute-done | bytes 786464 | tf_op jit(solution)/shard_map/ppermute | solution.py:570
  89.9 2.6 pack.8
  92.4 1.8 collective-permute-start.10
  94.2 3.0 %collective-permute-start.8 = (bf16[8,128,512]{2,1,0:T(8,128)(2,1)}, bf16[8,128,512]{2,1,0:T(8,128)(2,1)}, u32[]{:S(2)}, u32[]{:S(2)}) collective-permute-start(bf16[8,128,512]{2,1,0:T(8,128)(2,1)} %get-tuple-element.71), channel_id=1, source_target_pairs={{0,4},{2,6},{4,0},{6,2},{8,12},{10,14},{12,8},{14,10},{1,5},{3,7},... | collective-permute-start | bytes 3145736 | tf_op jit(solution)/shard_map/ppermute | solution.py:570
  97.2 1.6 collective-permute-start.13
  99.6 22.9 %all_to_all.24 = s32[32,1,1]{2,1,0:T(1,128)S(1)} all-to-all(s32[32,1,1]{2,1,0:T(1,128)S(1)} %broadcast_in_dim.11), channel_id=1, replica_groups=mesh['groups'=2,'agent'=8,'tm'=2] {'groups','agent','tm'}, dimensions={0} | all-to-all | bytes 256 | tf_op jit(solution)/shard_map/all_to_all | solution.py:553
  123.2 3.1 %pack.9 = (bf16[7,128,512]{2,1,0:T(8,128)(2,1)S(1)}, bf16[7,128,512]{2,1,0:T(8,128)(2,1)S(1)}) custom-call(s32[80]{0:T(128)S(1)} %copy-done.14, bf16[16,128,512]{2,1,0:T(8,128)(2,1)} %refs_0_.15, bf16[8,128,512]{2,1,0:T(8,128)(2,1)S(1)} %collective-permute-done.3.refs_1_.refs_3_, bf16[8,128,512]{2,1,0:T(8,128)(2,1)S(1)} %collective-permute-done.5.refs_2_.refs_4_, ...), custom_call_target="tpu_custom_call" | custom-call | bytes 3670016 | tf_op jit(solution)/shard_map/pack/pallas_call | solution.py:171
  127.0 2.7 %collective-permute-start.12 = (bf16[7,128,512]{2,1,0:T(8,128)(2,1)S(1)}, bf16[7,128,512]{2,1,0:T(8,128)(2,1)S(1)}, u32[]{:S(2)}, u32[]{:S(2)}) collective-permute-start(bf16[7,128,512]{2,1,0:T(8,128)(2,1)S(1)} %get-tuple-element.75), channel_id=1, source_target_pairs={{0,2},{2,0},{4,6},{6,4},{8,10},{10,8},{12,14},{14,12},{1,3},{3,1},... | collective-permute-start | bytes 2752520 | tf_op jit(solution)/shard_map/ppermute | solution.py:570
  129.7 19.0 %collective-permute-done.11.refs_6_.refs_4_ = bf16[7,128,512]{2,1,0:T(8,128)(2,1)S(1)} collective-permute-done((bf16[7,128,512]{2,1,0:T(8,128)(2,1)S(1)}, bf16[7,128,512]{2,1,0:T(8,128)(2,1)S(1)}, u32[]{:S(2)}, u32[]{:S(2)}) %collective-permute-start.11) | collective-permute-done | bytes 917536 | tf_op jit(solution)/shard_map/ppermute | solution.py:570
  148.6 1.3 collective-permute-done.12.refs_10_.refs_9_.refs_11_
  149.9 1.8 pack.10
  151.7 1.5 collective-permute-start.14
  153.3 23.2 %agent_stage.4 = (f32[8,128,512]{2,1,0:T(8,128)}, bf16[8,128,512]{2,1,0:T(8,128)(2,1)}) custom-call(s32[32]{0:T(128)S(1)} %copy-done.15, bf16[16,128,512]{2,1,0:T(8,128)(2,1)S(1)} %copy-done.17, bf16[16,128,512]{2,1,0:T(8,128)(2,1)S(1)} %copy-done.17, bf16[8,128,512]{2,1,0:T(8,128)(2,1)S(1)} %copy-done.4, bf16[8,128,512]{2,1,0:T(8,128)(2,1)} %copy-done.19, ...), custom_call_target="tpu_custom_call" | custom-call | flops 37580963840 | bytes 6291456 | tf_op jit(solution)/shard_map/agent_stage/pallas_call | solution.py:106
  176.5 1.4 pack.11
  177.9 1.7 collective-permute-start.16
  180.0 1.5 collective-permute-start.17
  181.5 34.3 %collective-permute-done.15.refs_12_ = bf16[6,128,512]{2,1,0:T(8,128)(2,1)S(1)} collective-permute-done((bf16[6,128,512]{2,1,0:T(8,128)(2,1)S(1)}, bf16[6,128,512]{2,1,0:T(8,128)(2,1)S(1)}, u32[]{:S(2)}, u32[]{:S(2)}) %collective-permute-start.15) | collective-permute-done | bytes 786464 | tf_op jit(solution)/shard_map/ppermute | solution.py:570
  215.8 21.9 %agent_stage.5 = (f32[8,128,512]{2,1,0:T(8,128)}, bf16[8,128,512]{2,1,0:T(8,128)(2,1)}) custom-call(s32[32]{0:T(128)S(1)} %copy-done.15, bf16[16,128,512]{2,1,0:T(8,128)(2,1)S(1)} %copy-done.17, bf16[16,128,512]{2,1,0:T(8,128)(2,1)S(1)} %copy-done.17, bf16[8,128,512]{2,1,0:T(8,128)(2,1)} %collective-permute-done.9.refs_5_.refs_6_.refs_7_.refs_1_, ...), custom_call_target="tpu_custom_call" | custom-call | flops 37580963840 | bytes 6291456 | tf_op jit(solution)/shard_map/agent_stage/pallas_call | solution.py:106
  237.7 2.3 collective-permute-start.18
  240.0 1.6 collective-permute-done.18.refs_3_
  241.6 18.9 %time_stage.3 = (f32[16,128]{1,0:T(8,128)}, f32[2,128]{1,0:T(2,128)S(1)}) custom-call(s32[1]{0:T(128)} %bitcast.11.offset_ref, f32[8,128,512]{2,1,0:T(8,128)S(1)} %copy-done.7, f32[8,128,512]{2,1,0:T(8,128)} %get-tuple-element.79.refs_1_, bf16[8,128,512]{2,1,0:T(8,128)(2,1)S(1)} %collective-permute-done.17.refs_2_, ...), custom_call_target="tpu_custom_call" | custom-call | tf_op jit(solution)/shard_map/time_stage/pallas_call | solution.py:285
  260.5 1.3 collective-permute-start.19
  264.1 1.4 advantage_stage.3
  (83 shorter events, 11.5 us)
Async XLA Ops:
  2.0 41.5 %collective-permute-start.3 = (bf16[8,128,512]{2,1,0:T(8,128)(2,1)S(1)}, bf16[8,128,512]{2,1,0:T(8,128)(2,1)S(1)}, u32[]{:S(2)}, u32[]{:S(2)}) collective-permute-start(bf16[8,128,512]{2,1,0:T(8,128)(2,1)S(1)} %slice.3), channel_id=1, source_target_pairs={{0,4},{2,6},{4,0},{6,2},{8,12},{10,14},{12,8},{14,10},{1,5},{3,7},... | collective-permute-start | bytes 3145736 | tf_op jit(solution)/shard_map/ppermute | solution.py:570
  5.1 38.4 %collective-permute-start.2 = (bf16[8,128,512]{2,1,0:T(8,128)(2,1)S(1)}, bf16[8,128,512]{2,1,0:T(8,128)(2,1)S(1)}, u32[]{:S(2)}, u32[]{:S(2)}) collective-permute-start(bf16[8,128,512]{2,1,0:T(8,128)(2,1)S(1)} %slice.3), channel_id=1, source_target_pairs={{4,8},{6,10},{8,4},{10,6},{5,9},{7,11},{9,5},{11,7},{20,24},{22,26... | collective-permute-start | bytes 3145736 | tf_op jit(solution)/shard_map/ppermute | solution.py:570
  6.6 26.8 %all-to-all-start.2 = ((s32[8,1,32]{2,1,0:T(1,128)}), s32[8,1,32]{2,1,0:T(1,128)S(1)}, u32[]{:S(2)}, u32[]{:S(2)}) async-start(s32[8,1,32]{2,1,0:T(1,128)} %broadcast_in_dim.9), calls=%async_computation.2 | async-start | bytes 8192 | tf_op jit(solution)/shard_map/all_to_all | solution.py:553
  43.5 106.4 %copy-start = (bf16[8,128,512]{2,1,0:T(8,128)(2,1)}, bf16[8,128,512]{2,1,0:T(8,128)(2,1)S(1)}, u32[]{:S(2)}) copy-start(bf16[8,128,512]{2,1,0:T(8,128)(2,1)S(1)} %collective-permute-done.3.refs_1_.refs_3_) | copy-start | bytes 3145732
  49.1 39.7 %collective-permute-start.5 = (bf16[8,128,512]{2,1,0:T(8,128)(2,1)S(1)}, bf16[8,128,512]{2,1,0:T(8,128)(2,1)S(1)}, u32[]{:S(2)}, u32[]{:S(2)}) collective-permute-start(bf16[8,128,512]{2,1,0:T(8,128)(2,1)S(1)} %get-tuple-element.69), channel_id=1, source_target_pairs={{0,4},{2,6},{4,0},{6,2},{8,12},{10,14},{12,8},{14,10},{1,5},{3,7},... | collective-permute-start | bytes 3145736 | tf_op jit(solution)/shard_map/ppermute | solution.py:570
  50.1 38.8 %collective-permute-start.4 = (bf16[8,128,512]{2,1,0:T(8,128)(2,1)S(1)}, bf16[8,128,512]{2,1,0:T(8,128)(2,1)S(1)}, u32[]{:S(2)}, u32[]{:S(2)}) collective-permute-start(bf16[8,128,512]{2,1,0:T(8,128)(2,1)S(1)} %collective-permute-done.3.refs_1_.refs_3_), channel_id=1, source_target_pairs={{4,8},{6,10},{8,4},{10,6},{5,9},{7,11},{9,5},{11,7},{20,24},{22,26... | collective-permute-start | bytes 3145736 | tf_op jit(solution)/shard_map/ppermute | solution.py:570
  50.8 38.0 %collective-permute-start.7 = (bf16[7,128,512]{2,1,0:T(8,128)(2,1)S(1)}, bf16[7,128,512]{2,1,0:T(8,128)(2,1)S(1)}, u32[]{:S(2)}, u32[]{:S(2)}) collective-permute-start(bf16[7,128,512]{2,1,0:T(8,128)(2,1)S(1)} %get-tuple-element.70), channel_id=1, source_target_pairs={{0,2},{2,0},{4,6},{6,4},{8,10},{10,8},{12,14},{14,12},{1,3},{3,1},... | collective-permute-start | bytes 2752520 | tf_op jit(solution)/shard_map/ppermute | solution.py:570
  55.2 33.6 %collective-permute-start.6 = (bf16[6,128,512]{2,1,0:T(8,128)(2,1)S(1)}, bf16[6,128,512]{2,1,0:T(8,128)(2,1)S(1)}, u32[]{:S(2)}, u32[]{:S(2)}) collective-permute-start(bf16[6,128,512]{2,1,0:T(8,128)(2,1)S(1)} %pack.7), channel_id=1, source_target_pairs={{0,2},{2,0},{4,6},{6,4},{8,10},{10,8},{12,14},{14,12},{1,3},{3,1},... | collective-permute-start | bytes 2359304 | tf_op jit(solution)/shard_map/ppermute | solution.py:570
  55.2 67.9 %copy-start.3 = (bf16[8,128,512]{2,1,0:T(8,128)(2,1)S(1)}, bf16[8,128,512]{2,1,0:T(8,128)(2,1)}, u32[]{:S(2)}) copy-start(bf16[8,128,512]{2,1,0:T(8,128)(2,1)} %copy-done.2) | copy-start | bytes 3145732
  55.3 67.9 %copy-start.14 = (s32[80]{0:T(128)S(1)}, s32[80]{0:T(128)}, u32[]{:S(2)}) copy-start(s32[80]{0:T(128)} %get-tuple-element.68.table_ref) | copy-start | bytes 964
  55.3 67.9 %collective-permute-start.9 = (bf16[8,128,512]{2,1,0:T(8,128)(2,1)}, bf16[8,128,512]{2,1,0:T(8,128)(2,1)}, u32[]{:S(2)}, u32[]{:S(2)}) collective-permute-start(bf16[8,128,512]{2,1,0:T(8,128)(2,1)} %get-tuple-element.72), channel_id=1, source_target_pairs={{4,8},{6,10},{8,4},{10,6},{5,9},{7,11},{9,5},{11,7},{20,24},{22,26... | collective-permute-start | bytes 3145736 | tf_op jit(solution)/shard_map/ppermute | solution.py:570
  88.8 61.1 %copy-start.5 = (bf16[8,128,512]{2,1,0:T(8,128)(2,1)}, bf16[8,128,512]{2,1,0:T(8,128)(2,1)S(1)}, u32[]{:S(2)}) copy-start(bf16[8,128,512]{2,1,0:T(8,128)(2,1)S(1)} %collective-permute-done.5.refs_2_.refs_4_) | copy-start | bytes 3145732
  92.4 30.7 %collective-permute-start.10 = (bf16[8,128,512]{2,1,0:T(8,128)(2,1)}, bf16[8,128,512]{2,1,0:T(8,128)(2,1)}, u32[]{:S(2)}, u32[]{:S(2)}) collective-permute-start(bf16[8,128,512]{2,1,0:T(8,128)(2,1)} %get-tuple-element.73), channel_id=1, source_target_pairs={{0,2},{2,0},{4,6},{6,4},{8,10},{10,8},{12,14},{14,12},{1,3},{3,1},... | collective-permute-start | bytes 3145736 | tf_op jit(solution)/shard_map/ppermute | solution.py:570
  94.2 28.9 %collective-permute-start.8 = (bf16[8,128,512]{2,1,0:T(8,128)(2,1)}, bf16[8,128,512]{2,1,0:T(8,128)(2,1)}, u32[]{:S(2)}, u32[]{:S(2)}) collective-permute-start(bf16[8,128,512]{2,1,0:T(8,128)(2,1)} %get-tuple-element.71), channel_id=1, source_target_pairs={{0,4},{2,6},{4,0},{6,2},{8,12},{10,14},{12,8},{14,10},{1,5},{3,7},... | collective-permute-start | bytes 3145736 | tf_op jit(solution)/shard_map/ppermute | solution.py:570
  97.2 32.4 %collective-permute-start.13 = (bf16[8,128,512]{2,1,0:T(8,128)(2,1)S(1)}, bf16[8,128,512]{2,1,0:T(8,128)(2,1)}, u32[]{:S(2)}, u32[]{:S(2)}) collective-permute-start(bf16[8,128,512]{2,1,0:T(8,128)(2,1)S(1)} %collective-permute-done.5.refs_2_.refs_4_), channel_id=1, source_target_pairs={{4,8},{6,10},{8,4},{10,6},{5,9},{7,11},{9,5},{11,7},{20,24},{22,26... | collective-permute-start | bytes 3145736 | tf_op jit(solution)/shard_map/ppermute | solution.py:570
  123.2 26.7 %copy-start.17 = (bf16[16,128,512]{2,1,0:T(8,128)(2,1)S(1)}, bf16[16,128,512]{2,1,0:T(8,128)(2,1)}, u32[]{:S(2)}) copy-start(bf16[16,128,512]{2,1,0:T(8,128)(2,1)} %refs_0_.15) | copy-start | bytes 6291460
  126.4 22.3 %collective-permute-start.11 = (bf16[7,128,512]{2,1,0:T(8,128)(2,1)S(1)}, bf16[7,128,512]{2,1,0:T(8,128)(2,1)S(1)}, u32[]{:S(2)}, u32[]{:S(2)}) collective-permute-start(bf16[7,128,512]{2,1,0:T(8,128)(2,1)S(1)} %get-tuple-element.74), channel_id=1, source_target_pairs={{0,4},{2,6},{4,0},{6,2},{8,12},{10,14},{12,8},{14,10},{1,5},{3,7},... | collective-permute-start | bytes 2752520 | tf_op jit(solution)/shard_map/ppermute | solution.py:570
  127.0 26.3 %copy-start.15 = (s32[32]{0:T(128)S(1)}, s32[32]{0:T(128)}, u32[]{:S(2)}) copy-start(s32[32]{0:T(128)} %get-tuple-element.67.table_ref) | copy-start | bytes 388
  127.0 26.3 %copy-start.30 = (bf16[512,512]{1,0:T(8,128)(2,1)S(1)}, bf16[512,512]{1,0:T(8,128)(2,1)}, u32[]{:S(2)}) copy-start(bf16[512,512]{1,0:T(8,128)(2,1)} %refs_15_.1) | copy-start | bytes 1572868
  127.0 22.9 %collective-permute-start.12 = (bf16[7,128,512]{2,1,0:T(8,128)(2,1)S(1)}, bf16[7,128,512]{2,1,0:T(8,128)(2,1)S(1)}, u32[]{:S(2)}, u32[]{:S(2)}) collective-permute-start(bf16[7,128,512]{2,1,0:T(8,128)(2,1)S(1)} %get-tuple-element.75), channel_id=1, source_target_pairs={{0,2},{2,0},{4,6},{6,4},{8,10},{10,8},{12,14},{14,12},{1,3},{3,1},... | collective-permute-start | bytes 2752520 | tf_op jit(solution)/shard_map/ppermute | solution.py:570
  151.7 24.7 %collective-permute-start.14 = (bf16[8,128,512]{2,1,0:T(8,128)(2,1)S(1)}, bf16[8,128,512]{2,1,0:T(8,128)(2,1)S(1)}, u32[]{:S(2)}, u32[]{:S(2)}) collective-permute-start(bf16[8,128,512]{2,1,0:T(8,128)(2,1)S(1)} %get-tuple-element.77), channel_id=1, source_target_pairs={{0,4},{2,6},{4,0},{6,2},{8,12},{10,14},{12,8},{14,10},{1,5},{3,7},... | collective-permute-start | bytes 3145736 | tf_op jit(solution)/shard_map/ppermute | solution.py:570
  176.5 39.3 %copy-start.29 = (bf16[512,1536]{1,0:T(8,128)(2,1)S(1)}, bf16[512,1536]{1,0:T(8,128)(2,1)}, u32[]{:S(2)}) copy-start(bf16[512,1536]{1,0:T(8,128)(2,1)} %refs_14_.1) | copy-start | bytes 4718596
  177.9 37.9 %collective-permute-start.16 = (bf16[7,128,512]{2,1,0:T(8,128)(2,1)S(1)}, bf16[7,128,512]{2,1,0:T(8,128)(2,1)S(1)}, u32[]{:S(2)}, u32[]{:S(2)}) collective-permute-start(bf16[7,128,512]{2,1,0:T(8,128)(2,1)S(1)} %pack.11), channel_id=1, source_target_pairs={{0,2},{2,0},{4,6},{6,4},{8,10},{10,8},{12,14},{14,12},{1,3},{3,1},... | collective-permute-start | bytes 2752520 | tf_op jit(solution)/shard_map/ppermute | solution.py:570
  179.7 36.1 %collective-permute-start.15 = (bf16[6,128,512]{2,1,0:T(8,128)(2,1)S(1)}, bf16[6,128,512]{2,1,0:T(8,128)(2,1)S(1)}, u32[]{:S(2)}, u32[]{:S(2)}) collective-permute-start(bf16[6,128,512]{2,1,0:T(8,128)(2,1)S(1)} %get-tuple-element.78), channel_id=1, source_target_pairs={{0,2},{2,0},{4,6},{6,4},{8,10},{10,8},{12,14},{14,12},{1,3},{3,1},... | collective-permute-start | bytes 2359304 | tf_op jit(solution)/shard_map/ppermute | solution.py:570
  180.0 61.6 %copy-start.7 = (f32[8,128,512]{2,1,0:T(8,128)S(1)}, f32[8,128,512]{2,1,0:T(8,128)}, u32[]{:S(2)}) copy-start(f32[8,128,512]{2,1,0:T(8,128)} %get-tuple-element.76.refs_10_.refs_0_) | copy-start | bytes 6291460
  180.0 61.6 %copy-start.22 = (s32[16,128]{1,0:T(8,128)S(1)}, s32[16,128]{1,0:T(8,128)}, u32[]{:S(2)}) copy-start(s32[16,128]{1,0:T(8,128)} %done_ref.1) | copy-start | bytes 24580
  180.0 61.6 %copy-start.23 = (f32[16,128]{1,0:T(8,128)S(1)}, f32[16,128]{1,0:T(8,128)}, u32[]{:S(2)}) copy-start(f32[16,128]{1,0:T(8,128)} %rewards_ref.1) | copy-start | bytes 24580
  180.0 61.6 %copy-start.24 = (f32[512]{0:T(512)S(1)}, f32[512]{0:T(512)}, u32[]{:S(2)}) copy-start(f32[512]{0:T(512)} %param.21) | copy-start | bytes 6148
  180.0 61.6 %copy-start.25 = (f32[128]{0:T(128)S(1)}, f32[128]{0:T(128)}, u32[]{:S(2)}) copy-start(f32[128]{0:T(128)} %param.16) | copy-start | bytes 1540
  180.0 60.0 %collective-permute-start.17 = (bf16[8,128,512]{2,1,0:T(8,128)(2,1)}, bf16[8,128,512]{2,1,0:T(8,128)(2,1)S(1)}, u32[]{:S(2)}, u32[]{:S(2)}) collective-permute-start(bf16[8,128,512]{2,1,0:T(8,128)(2,1)} %get-tuple-element.80), channel_id=1, source_target_pairs={{0,1},{2,3},{4,5},{6,7},{8,9},{10,11},{12,13},{14,15},{16,17},{18,... | collective-permute-start | bytes 3145736 | tf_op jit(solution)/shard_map/ppermute | solution.py:663
  237.7 3.9 %collective-permute-start.18 = (bf16[8,128,512]{2,1,0:T(8,128)(2,1)}, bf16[8,128,512]{2,1,0:T(8,128)(2,1)}, u32[]{:S(2)}, u32[]{:S(2)}) collective-permute-start(bf16[8,128,512]{2,1,0:T(8,128)(2,1)} %get-tuple-element.81), channel_id=1, source_target_pairs={{0,1},{2,3},{4,5},{6,7},{8,9},{10,11},{12,13},{14,15},{16,17},{18,... | collective-permute-start | bytes 3145736 | tf_op jit(solution)/shard_map/ppermute | solution.py:663
  260.5 3.0 %collective-permute-start.19 = (f32[2,128]{1,0:T(2,128)S(1)}, f32[2,128]{1,0:T(2,128)S(1)}, u32[]{:S(2)}, u32[]{:S(2)}) collective-permute-start(f32[2,128]{1,0:T(2,128)S(1)} %get-tuple-element.83), channel_id=1, source_target_pairs={{1,0},{3,2},{5,4},{7,6},{9,8},{11,10},{13,12},{15,14},{17,16},{19,... | collective-permute-start | bytes 3080 | tf_op jit(solution)/shard_map/ppermute | solution.py:680
  (14 other events, 155.2 us)

commit v4 on v3

--- a/solution.py
+++ b/solution.py
@@ -349,34 +349,43 @@
     return arrived.reshape(blocks * capacity, agents, width), named * capacity + slot
 
 
-OUTWARD_READY = {1: (0, 1), 2: (1, 3), 3: (2, 4)}
-ACROSS_READY = {0: (1, 2), 1: (0, 0), 2: (1, 3), 3: (2, 4)}
-OUTWARD_DUE = (3, 4)
-ACROSS_DUE = (3, 5)
+OUTWARD_READY = {1: (0, 2, 2), 2: (1, 3, 3), 3: (2, 3, 4)}
+ACROSS_READY = {0: (0, 1, 1), 1: (0, 0, 0), 2: (0, 2, 2), 3: (1, 2, 3)}
+OUTWARD_DUE = (3, 4, 4)
+ACROSS_DUE = (2, 3, 4)
 
 
 def relay_sizes(steps, capacity):
     half, quarter = steps // 2, steps // 4
-    chunks = [half, half]
-    outward = [half, half, half, half - 1, half]
-    across = [capacity - 2, half - 1, half, half - 1, quarter + 2, half - 1]
+    chunks = [half, quarter, quarter]
+    outward = [half, half, half + 1, half + 1, quarter + 2]
+    across = [capacity + 1, half, half, half - 1, quarter + 2]
     return chunks, outward, across
 
 
-def relay_codes(chunks, outward, across):
-    count = len(chunks)
-    return {
-        "own": 0,
-        "outer": [1 + 3 * count + k for k in range(count)],
-        "inner": [1 + count + k for k in range(count)],
-        "far": [1 + 2 * count + k for k in range(count)],
-        "outward": [1 + 3 * count + b for b in range(len(outward))],
-        "across": [1 + 3 * count + len(outward) + b for b in range(len(across))],
-    }
+def relay_codes(outward, across):
+    names = {}
+    code = 1
+    for name, count in (("edge", len(outward)), ("swap", 2), ("far", 3), ("across", len(across))):
+        names[name] = [code + n for n in range(count)]
+        code += count
+    names["own"] = 0
+    return names
+
+
+def inner_place(codes, starts, u, k):
+    behind = starts[k] - starts[min(k, 1)]
+    if u == 0:
+        return codes["edge"][min(k, 1)] * SPAN + behind
+    if u == 1:
+        return codes["own"] * SPAN + starts[k]
+    if u == 2:
+        return codes["swap"][min(k, 1)] * SPAN + behind
+    return codes["far"][k] * SPAN
 
 
 def plan_kernel(steps, list_length, chunks, outward, across, place_ref, lists_ref, out_ref, in_ref, flag_ref, eloc, yloc, room):
-    codes = relay_codes(chunks, outward, across)
+    codes = relay_codes(outward, across)
     column, row = place_ref[0], place_ref[1]
     far_side = column >= COLUMNS // 2
     mirror = lambda u: jnp.where(far_side, COLUMNS - 1 - u, u)
@@ -394,11 +403,6 @@
 
     lax.fori_loop(0, sum(outward) + sum(across), clear, 0)
 
-    @pl.when(me == 0)
-    def _():
-        for n in range(chunks[1]):
-            out_ref[e_base[1] + n] = codes["own"] * SPAN + starts[1] + n
-
     def named(dest, t, source):
         hit = entry(dest, t, 0) == source
         for j in range(1, list_length):
@@ -424,20 +428,19 @@
     for turn in range(2):
         sender = row if turn == 0 else 1 - row
         empty(outward)
-        room[0] = outward[0]
+        room[0], room[1] = outward[0], outward[1]
         for k, count in enumerate(chunks):
-            held = (0, codes["own"] * SPAN + starts[k], codes["inner"][k] * SPAN, codes["far"][k] * SPAN)
             for u in (1, 2, 3):
 
-                def first_piece(n, _):
-                    eloc[(turn * COLUMNS + 1) * steps + n] = n
+                def first_piece(n, _, u=u):
+                    eloc[(turn * COLUMNS + u) * steps + n] = (u - 1) * SPAN + n
                     return 0
 
-                if u == 1 and k == 0:
+                if u in (1, 2) and k == 0:
                     lax.fori_loop(0, count, first_piece, 0)
                     continue
 
-                def outer_piece(n, _, u=u, k=k, held=held):
+                def outer_piece(n, _, u=u, k=k):
                     t = starts[k] + n
                     source = block(mirror(u), sender)
                     need = named(block(mirror(0), 0), t, source)
@@ -455,7 +458,7 @@
 
                             @pl.when(inner)
                             def _():
-                                out_ref[base_of(e_base, batch) + slot] = held[u] + n
+                                out_ref[base_of(e_base, batch) + slot] = inner_place(codes, starts, u, k) + n
 
                     return 0
 
@@ -465,10 +468,9 @@
         sender = row if turn == 0 else 1 - row
         empty(across)
         for k, count in enumerate(chunks):
-            held = (codes["outer"][k] * SPAN, codes["own"] * SPAN + starts[k], codes["inner"][k] * SPAN, codes["far"][k] * SPAN)
             for u in range(COLUMNS):
 
-                def row_piece(n, _, u=u, k=k, held=held):
+                def row_piece(n, _, u=u, k=k):
                     t = starts[k] + n
                     need = named(block(column, 1 - sender), t, block(mirror(u), sender))
                     if u == 0:
@@ -476,10 +478,10 @@
                         when = jnp.int32(0)
                     else:
                         where = eloc[(turn * COLUMNS + u) * steps + t]
-                        lies = codes["outward"][0] * SPAN + where
-                        when = jnp.where(where < 0, len(across), where // SPAN + 1)
+                        lies = codes["edge"][0] * SPAN + where
+                        when = jnp.where(where < 0, len(across), where // SPAN)
                     when = jnp.where(inner, ACROSS_READY[u][k], when)
-                    lies = jnp.where(inner, held[u] + n, lies)
+                    lies = jnp.where(inner, inner_place(codes, starts, u, k) + n, lies)
                     batch = choose(across, when)
                     yloc[(turn * COLUMNS + u) * steps + t] = -1
 
@@ -505,8 +507,10 @@
             same = source % ROWS == row
             e = eloc[u * steps + t]
             y = yloc[(COLUMNS + u) * steps + t]
-            code = jnp.where(u == 0, codes["outer"][k], jnp.where(u == 2, codes["inner"][k], codes["far"][k]))
-            direct = jnp.where(inner, code * SPAN + t - starts[k], codes["outward"][0] * SPAN + e)
+            first = jnp.int32(0)
+            for w in (0, 2, 3):
+                first = jnp.where(u == w, inner_place(codes, starts, w, k), first)
+            direct = jnp.where(inner, first + t - starts[k], codes["edge"][0] * SPAN + e)
             direct = jnp.where(u == me, codes["own"] * SPAN + t, direct)
             local = inner | (u == me)
             bad = jnp.where(
@@ -561,7 +565,7 @@
     steps, agents, width = embedded.shape
     list_length = lists.shape[1]
     chunks, outward, across = relay_sizes(steps, capacity)
-    codes = relay_codes(chunks, outward, across)
+    codes = relay_codes(outward, across)
     starts = [sum(chunks[:k]) for k in range(len(chunks))]
     e_base = [sum(outward[:b]) for b in range(len(outward))]
     y_base = [sum(outward) + sum(across[:b]) for b in range(len(across))]
@@ -571,65 +575,66 @@
     edges = column_pairs([(0, 1), (1, 0), (2, 3), (3, 2)])
     swap = column_pairs([(1, 2), (2, 1)])
     over = [(c * ROWS + r, c * ROWS + 1 - r) for c in range(COLUMNS) for r in range(ROWS)]
-    arrays = {codes["own"]: embedded}
+    own, edge, swapped, far, rows = (codes[n] for n in ("own", "edge", "swap", "far", "across"))
+    arrays = {own: embedded}
 
     def pick(names):
         return {code: arrays[code] for code in names}
 
-    def outward_part(stage):
-        return (e_base[stage], outward[stage], None)
-
-    def across_part(stage):
-        return (y_base[stage], across[stage], None)
-
-    reads = [[codes["own"]] for _ in across]
-    for stage in range(1, len(across)):
-        reads[stage] += codes["outward"][: min(stage, len(outward))]
-        for name, u in (("inner", 2), ("far", 3)):
-            for k in range(len(chunks)):
-                if OUTWARD_READY[u][k] <= stage:
-                    reads[stage].append(codes[name][k])
-
-    settled = [(), (), (0, 1)] + [(stage - 1,) for stage in range(3, len(across))]
     first = embedded[: chunks[0]]
-    arrays[codes["outward"][0]] = send(first, edges)
-    arrays[codes["inner"][0]] = send(first, swap)
+    arrays[edge[0]] = send(first, edges)
+    arrays[swapped[0]] = send(first, swap)
     everyone = shared(lists.reshape(-1), "agent").reshape(-1)
     out_table, in_table, flag = plan(
         everyone, place, steps, list_length, chunks, outward, across
     )
-    (packed,) = pack(out_table, pick(reads[0]), [across_part(0)])
-    arrays[codes["across"][0]] = send(packed, over)
-    arrays[codes["far"][0]] = send(arrays[codes["outward"][0]], swap)
-    done, after = [], ()
-    for stage in range(1, len(across)):
-        parts = [across_part(stage)]
-        if stage < len(outward):
-            parts.append(outward_part(stage))
-        if stage == 1:
-            parts.append((None, chunks[1], starts[1]))
-        if stage == len(across) - 1:
-            done.append(attention(0, chunks[0], due(arrays, codes, 0), in_table, after))
-            after = (done[0][0],)
-        else:
-            after += tuple(arrays[codes["across"][b]] for b in settled[stage])
-        packed = pack(out_table, pick(reads[stage]), parts, after)
-        arrays[codes["across"][stage]] = send(packed[0], over)
-        if stage < len(outward):
-            arrays[codes["outward"][stage]] = send(packed[1], edges)
-        if stage == 1:
-            arrays[codes["inner"][1]] = send(packed[2], swap)
-            arrays[codes["far"][1]] = send(arrays[codes["outward"][1]], swap)
-            crowded = jnp.max(shared(flag, ("groups", "agent", "tm")))
-        after = (crowded.reshape(1),) if stage == 2 else ()
-    done.append(attention(starts[1], chunks[1], due(arrays, codes, 1), in_table, ()))
+    arrays[far[0]] = send(arrays[edge[0]], swap)
+    column = index // ROWS
+    outer = (column == 0) | (column == COLUMNS - 1)
+    slots = jnp.arange(outward[1], dtype=jnp.int32)
+    table = jnp.where(outer, own * SPAN + starts[1] + slots, swapped[0] * SPAN + slots)
+    packed = pack(table, pick([own, swapped[0]]), [(0, outward[1], None), (None, outward[1], starts[1])])
+    arrays[edge[1]] = send(packed[0], edges)
+    arrays[swapped[1]] = send(packed[1], swap)
+    (packed,) = pack(out_table, pick([own, edge[0], swapped[0]]), [(y_base[0], across[0], None)], packed[:1])
+    arrays[rows[0]] = send(packed, over)
+    for k in (1, 2):
+        at = starts[k] - starts[1]
+        arrays[far[k]] = send(arrays[edge[1]][at : at + chunks[k]], swap)
+
+    def stage(n, reads, settled, after=()):
+        parts = [(y_base[n - 1], across[n - 1], None)]
+        if n < len(outward):
+            parts.append((e_base[n], outward[n], None))
+        after = tuple(arrays[rows[b]] for b in settled) + tuple(after)
+        packed = pack(out_table, pick([own] + reads), parts, after)
+        if n < len(outward):
+            arrays[edge[n]] = send(packed[1], edges)
+        arrays[rows[n - 1]] = send(packed[0], over)
+        return packed[0]
+
+    reads = edge[:2] + swapped[:1] + far[:1]
+    token = stage(2, reads, (), (packed,))
+    crowded = jnp.max(shared(flag, ("groups", "agent", "tm")))
+    reads = reads + edge[2:3] + swapped[1:] + far[1:2]
+    token = stage(3, reads, (0, 1), (token, crowded.reshape(1)))
+    reads = reads + edge[3:4] + far[2:3]
+    token = stage(4, reads, (2,), (token,))
+    done = [attention(0, chunks[0], due(arrays, codes, starts, 0), in_table, (token,))]
+    reads = reads + edge[4:5]
+    token = stage(5, reads, (3,), (done[0][0],))
+    for k in (1, 2):
+        done.append(
+            attention(starts[k], chunks[k], due(arrays, codes, starts, k), in_table, (token, done[-1][0]))
+        )
     return done, crowded
 
 
-def due(arrays, codes, k):
-    wanted = [codes["own"], codes["inner"][k], codes["far"][k]]
-    wanted += codes["outward"][: OUTWARD_DUE[k] + 1] + codes["across"][: ACROSS_DUE[k] + 1]
-    return {code: arrays[code] for code in wanted}
+def due(arrays, codes, starts, k):
+    wanted = {codes["own"], *codes["edge"][: OUTWARD_DUE[k] + 1]}
+    wanted |= {inner_place(codes, starts, u, k) // SPAN for u in (0, 2, 3)}
+    wanted |= set(codes["across"][: ACROSS_DUE[k] + 1])
+    return {code: arrays[code] for code in sorted(wanted)}
 
 
 def body(

time: 267 us -> 246 us (0.921)
  waiting for transfers between devices: 109 us -> 47.9 us
  starting transfers between devices: 33.9 us -> 59.7 us
  blocking collectives: 22.9 us -> 37.3 us
  local copies, waits for them, and re-layouts: 6.31 us -> 9.24 us
    ppermute x15, waiting for transfers between devices: 86.3 us -> 27.3 us  [relay(): send = lambda value, pairs: lax.ppermute(value, 'agent', pairs)]
    ppermute x15, starting transfers between devices: 22.2 us -> 48.1 us  [relay(): send = lambda value, pairs: lax.ppermute(value, 'agent', pairs)]
    all_to_all x1, blocking collectives: 22.9 us -> 37.3 us  [shared(): return lax.all_to_all(rows, axes, split_axis=0, concat_axis=0, tiled=True)]
    ppermute x2 -> x3, starting transfers between devices: 3.79 us -> 5.64 us  [attention(): return (residual, lax.ppermute(normed, 'tm', forward))]
    pallas_call x2 -> x3, Pallas kernels: 45.1 us -> 44.4 us  [agent_stage(): pl.pallas_call(functools.partial(agent_kernel, list_length, first_step, t...]
  transfers between devices with their start and end apart: 19 -> 20, of which waited for: 7 -> 6; matrix products, arithmetic and copies ran while one was open for 2% -> 2% of each run, Pallas kernels for 23% -> 25%
where the time goes in v4:
time: 246 us; the launch traced here: 245 us
  Pallas kernels  87.8 us (36%)
  starting transfers between devices  59.7 us (24%)
  waiting for transfers between devices  47.9 us (19%)
  blocking collectives  37.3 us (15%)
  local copies, waits for them, and re-layouts  9.24 us (4%)
    ppermute x15, starting transfers between devices, relay(): send = lambda value, pairs: lax.ppermute(value, 'agent', pairs)  48.1 us
    pallas_call x3, Pallas kernels, agent_stage(): pl.pallas_call(functools.partial(agent_kernel, list_length, first_step, t...  44.4 us
    all_to_all x1, blocking collectives, shared(): return lax.all_to_all(rows, axes, split_axis=0, concat_axis=0, tiled=True)  37.3 us
    ppermute x15, waiting for transfers between devices, relay(): send = lambda value, pairs: lax.ppermute(value, 'agent', pairs)  27.3 us
    pallas_call x1, Pallas kernels, time_stage(): pl.pallas_call(functools.partial(time_kernel, len(residuals), steps, tile...  19 us
    all_to_all x1, waiting for transfers between devices, shared(): return lax.all_to_all(rows, axes, split_axis=0, concat_axis=0, tiled=True)  18.5 us
    pallas_call x6, Pallas kernels, pack(): pl.pallas_call(functools.partial(pack_kernel, tuple(arrays), tuple(parts)...  15.5 us
    pallas_call x1, Pallas kernels, plan(): pl.pallas_call(functools.partial(plan_kernel, steps, list_length, chunks,...  7.54 us
  transfers between devices with their start and end apart: 20, of which 6 were waited for; matrix products, arithmetic and copies ran while one was open for 2% of the time, Pallas kernels for 25%

profile of v4, /device:TPU:0, one launch (start us, length us, event | category | flops | bytes accessed | tf_op | source)
XLA Modules:
  0.0 245.5 jit_solution(17458279887933238827)
XLA Ops:
  0.6 2.3 slice.9
  3.8 5.8 %collective-permute-start.2 = (bf16[8,128,512]{2,1,0:T(8,128)(2,1)}, bf16[8,128,512]{2,1,0:T(8,128)(2,1)S(1)}, u32[]{:S(2)}, u32[]{:S(2)}) collective-permute-start(bf16[8,128,512]{2,1,0:T(8,128)(2,1)} %slice.9), channel_id=1, source_target_pairs={{0,4},{2,6},{4,0},{6,2},{8,12},{10,14},{12,8},{14,10},{1,5},{3,7},... | collective-permute-start | bytes 3145736 | tf_op jit(solution)/shard_map/ppermute | solution.py:574
  9.6 3.6 %pack.6 = (bf16[8,128,512]{2,1,0:T(8,128)(2,1)}, bf16[8,128,512]{2,1,0:T(8,128)(2,1)}) custom-call(s32[8]{0:T(128)S(1)} %broadcast_select_fusion.table_ref, bf16[16,128,512]{2,1,0:T(8,128)(2,1)} %refs_0_.17, bf16[8,128,512]{2,1,0:T(8,128)(2,1)S(1)} %collective-permute-done.3.refs_1_.refs_2_.refs_3_.refs_5_), custom_call_target="tpu_custom_call" | custom-call | bytes 4194304 | tf_op jit(solution)/shard_map/pack/pallas_call | solution.py:171
  13.2 24.5 %collective-permute-start.4 = (bf16[8,128,512]{2,1,0:T(8,128)(2,1)}, bf16[8,128,512]{2,1,0:T(8,128)(2,1)S(1)}, u32[]{:S(2)}, u32[]{:S(2)}) collective-permute-start(bf16[8,128,512]{2,1,0:T(8,128)(2,1)} %get-tuple-element.69.refs_3_), channel_id=1, source_target_pairs={{0,4},{2,6},{4,0},{6,2},{8,12},{10,14},{12,8},{14,10},{1,5},{3,7},... | collective-permute-start | bytes 3145736 | tf_op jit(solution)/shard_map/ppermute | solution.py:574
  37.8 1.7 collective-permute-start.5
  40.3 4.7 %all-to-all-start.2 = ((s32[8,1,32]{2,1,0:T(1,128)}), s32[8,1,32]{2,1,0:T(1,128)S(1)}, u32[]{:S(2)}, u32[]{:S(2)}) async-start(s32[8,1,32]{2,1,0:T(1,128)} %broadcast_in_dim.9), calls=%async_computation.2 | async-start | bytes 8192 | tf_op jit(solution)/shard_map/all_to_all | solution.py:557
  45.6 18.5 %all-to-all-done.2 = s32[8,1,32]{2,1,0:T(1,128)S(1)} async-done(((s32[8,1,32]{2,1,0:T(1,128)}), s32[8,1,32]{2,1,0:T(1,128)S(1)}, u32[]{:S(2)}, u32[]{:S(2)}) %all-to-all-start.2) | async-done | bytes 1056 | tf_op jit(solution)/shard_map/all_to_all | solution.py:557
  66.0 7.5 %plan.1 = (s32[78]{0:T(128)}, s32[32]{0:T(128)}, s32[1]{0:T(128)}) custom-call(s32[2]{0:T(128)} %pad_add_fusion.place_ref, s32[256]{0:T(256)} %reshape.157.lists_ref), custom_call_target="tpu_custom_call" | custom-call | tf_op jit(solution)/shard_map/plan/pallas_call | solution.py:536
  74.2 2.7 %pack.7.refs_5_ = bf16[9,128,512]{2,1,0:T(8,128)(2,1)} custom-call(s32[78]{0:T(128)S(1)} %copy-done.6, bf16[16,128,512]{2,1,0:T(8,128)(2,1)} %refs_0_.17, bf16[8,128,512]{2,1,0:T(8,128)(2,1)S(1)} %collective-permute-done.2.refs_1_, bf16[8,128,512]{2,1,0:T(8,128)(2,1)S(1)} %collective-permute-done.3.refs_1_.refs_2_.refs_3_.refs_5_, ...), custom_call_target="tpu_custom_call" | custom-call | bytes 2359296 | tf_op jit(solution)/shard_map/pack/pallas_call | solution.py:171
  77.9 2.2 pack.8
  80.1 2.0 collective-permute-start.6
  82.2 1.6 collective-permute-start.7
  83.8 1.5 collective-permute-start.10
  86.4 1.4 collective-permute-start.8
  88.4 37.3 %all_to_all.24 = s32[32,1,1]{2,1,0:T(1,128)S(1)} all-to-all(s32[32,1,1]{2,1,0:T(1,128)S(1)} %broadcast_in_dim.11), channel_id=1, replica_groups=mesh['groups'=2,'agent'=8,'tm'=2] {'groups','agent','tm'}, dimensions={0} | all-to-all | bytes 256 | tf_op jit(solution)/shard_map/all_to_all | solution.py:557
  126.4 3.4 %pack.9 = (bf16[8,128,512]{2,1,0:T(8,128)(2,1)S(1)}, bf16[9,128,512]{2,1,0:T(8,128)(2,1)}) custom-call(s32[78]{0:T(128)S(1)} %copy-done.7, bf16[16,128,512]{2,1,0:T(8,128)(2,1)} %refs_0_.17, bf16[8,128,512]{2,1,0:T(8,128)(2,1)S(1)} %collective-permute-done.2.refs_1_, bf16[8,128,512]{2,1,0:T(8,128)(2,1)S(1)} %collective-permute-done.4.refs_2_, ...), custom_call_target="tpu_custom_call" | custom-call | bytes 4456448 | tf_op jit(solution)/shard_map/pack/pallas_call | solution.py:171
  130.8 1.4 collective-permute-start.12
  133.0 22.6 %collective-permute-done.12.refs_10_.refs_9_ = bf16[8,128,512]{2,1,0:T(8,128)(2,1)S(1)} collective-permute-done((bf16[8,128,512]{2,1,0:T(8,128)(2,1)S(1)}, bf16[8,128,512]{2,1,0:T(8,128)(2,1)S(1)}, u32[]{:S(2)}, u32[]{:S(2)}) %collective-permute-start.12) | collective-permute-done | bytes 1048608 | tf_op jit(solution)/shard_map/ppermute | solution.py:574
  155.6 2.1 collective-permute-done.11.refs_8_.refs_4_
  158.8 2.0 pack.10
  160.8 1.3 collective-permute-start.15
  162.1 2.2 collective-permute-start.14
  164.3 21.2 %agent_stage.5 = (f32[8,128,512]{2,1,0:T(8,128)}, bf16[8,128,512]{2,1,0:T(8,128)(2,1)}) custom-call(s32[32]{0:T(128)S(1)} %copy-done.8, bf16[16,128,512]{2,1,0:T(8,128)(2,1)S(1)} %copy-done.10, bf16[16,128,512]{2,1,0:T(8,128)(2,1)S(1)} %copy-done.10, bf16[8,128,512]{2,1,0:T(8,128)(2,1)S(1)} %collective-permute-done.2.refs_1_, ...), custom_call_target="tpu_custom_call" | custom-call | flops 37580963840 | bytes 6291456 | tf_op jit(solution)/shard_map/agent_stage/pallas_call | solution.py:106
  185.5 1.4 collective-permute-start.17
  187.0 1.6 pack.11.refs_12_.refs_13_
  189.5 11.7 %agent_stage.6 = (f32[4,128,512]{2,1,0:T(8,128)S(1)}, bf16[4,128,512]{2,1,0:T(8,128)(2,1)}) custom-call(s32[32]{0:T(128)S(1)} %copy-done.8, bf16[16,128,512]{2,1,0:T(8,128)(2,1)S(1)} %copy-done.10, bf16[16,128,512]{2,1,0:T(8,128)(2,1)S(1)} %copy-done.10, bf16[8,128,512]{2,1,0:T(8,128)(2,1)S(1)} %collective-permute-done.2.refs_1_, ...), custom_call_target="tpu_custom_call" | custom-call | flops 18790481920 | bytes 3145728 | tf_op jit(solution)/shard_map/agent_stage/pallas_call | solution.py:106
  202.2 2.1 collective-permute-start.18
  204.3 2.5 %collective-permute-done.16.refs_12_ = bf16[6,128,512]{2,1,0:T(8,128)(2,1)S(1)} collective-permute-done((bf16[6,128,512]{2,1,0:T(8,128)(2,1)S(1)}, bf16[6,128,512]{2,1,0:T(8,128)(2,1)S(1)}, u32[]{:S(2)}, u32[]{:S(2)}) %collective-permute-start.16) | collective-permute-done | bytes 786464 | tf_op jit(solution)/shard_map/ppermute | solution.py:574
  206.8 11.5 %agent_stage.7 = (f32[4,128,512]{2,1,0:T(8,128)S(1)}, bf16[4,128,512]{2,1,0:T(8,128)(2,1)}) custom-call(s32[32]{0:T(128)S(1)} %copy-done.8, bf16[16,128,512]{2,1,0:T(8,128)(2,1)S(1)} %copy-done.10, bf16[16,128,512]{2,1,0:T(8,128)(2,1)S(1)} %copy-done.10, bf16[8,128,512]{2,1,0:T(8,128)(2,1)} %copy-done.1, bf16[8,128,512]{2,1,0:T(8,128)(2,1)} %copy-done.2, ...), custom_call_target="tpu_custom_call" | custom-call | flops 18790481920 | bytes 3145728 | tf_op jit(solution)/shard_map/agent_stage/pallas_call | solution.py:106
  218.3 2.1 collective-permute-start.19
  221.5 19.0 %time_stage.3 = (f32[16,128]{1,0:T(8,128)}, f32[2,128]{1,0:T(2,128)S(1)}) custom-call(s32[1]{0:T(128)} %bitcast.11.offset_ref, f32[8,128,512]{2,1,0:T(8,128)} %get-tuple-element.77.refs_12_.refs_13_.refs_0_, f32[4,128,512]{2,1,0:T(8,128)S(1)} %copy-done.4, f32[4,128,512]{2,1,0:T(8,128)S(1)} %get-tuple-element.80.refs_2_, ...), custom_call_target="tpu_custom_call" | custom-call | tf_op jit(solution)/shard_map/time_stage/pallas_call | solution.py:285
  244.1 1.4 advantage_stage.3
  (78 shorter events, 16.9 us)
Async XLA Ops:
  2.9 36.6 %copy-start.21 = (s32[1,16,2]{1,2,0:T(2,128)S(1)}, s32[1,16,2]{1,2,0:T(2,128)}, u32[]{:S(2)}) copy-start(s32[1,16,2]{1,2,0:T(2,128)} %param.13) | copy-start | bytes 388
  2.9 6.7 %collective-permute-start.3 = (bf16[8,128,512]{2,1,0:T(8,128)(2,1)}, bf16[8,128,512]{2,1,0:T(8,128)(2,1)S(1)}, u32[]{:S(2)}, u32[]{:S(2)}) collective-permute-start(bf16[8,128,512]{2,1,0:T(8,128)(2,1)} %slice.9), channel_id=1, source_target_pairs={{4,8},{6,10},{8,4},{10,6},{5,9},{7,11},{9,5},{11,7},{20,24},{22,26... | collective-permute-start | bytes 3145736 | tf_op jit(solution)/shard_map/ppermute | solution.py:574
  3.8 34.0 %collective-permute-start.2 = (bf16[8,128,512]{2,1,0:T(8,128)(2,1)}, bf16[8,128,512]{2,1,0:T(8,128)(2,1)S(1)}, u32[]{:S(2)}, u32[]{:S(2)}) collective-permute-start(bf16[8,128,512]{2,1,0:T(8,128)(2,1)} %slice.9), channel_id=1, source_target_pairs={{0,4},{2,6},{4,0},{6,2},{8,12},{10,14},{12,8},{14,10},{1,5},{3,7},... | collective-permute-start | bytes 3145736 | tf_op jit(solution)/shard_map/ppermute | solution.py:574
  9.6 154.6 %copy-start = (bf16[8,128,512]{2,1,0:T(8,128)(2,1)}, bf16[8,128,512]{2,1,0:T(8,128)(2,1)S(1)}, u32[]{:S(2)}) copy-start(bf16[8,128,512]{2,1,0:T(8,128)(2,1)S(1)} %collective-permute-done.3.refs_1_.refs_2_.refs_3_.refs_5_) | copy-start | bytes 3145732
  13.2 64.7 %collective-permute-start.4 = (bf16[8,128,512]{2,1,0:T(8,128)(2,1)}, bf16[8,128,512]{2,1,0:T(8,128)(2,1)S(1)}, u32[]{:S(2)}, u32[]{:S(2)}) collective-permute-start(bf16[8,128,512]{2,1,0:T(8,128)(2,1)} %get-tuple-element.69.refs_3_), channel_id=1, source_target_pairs={{0,4},{2,6},{4,0},{6,2},{8,12},{10,14},{12,8},{14,10},{1,5},{3,7},... | collective-permute-start | bytes 3145736 | tf_op jit(solution)/shard_map/ppermute | solution.py:574
  37.8 151.7 %copy-start.1 = (bf16[8,128,512]{2,1,0:T(8,128)(2,1)}, bf16[8,128,512]{2,1,0:T(8,128)(2,1)S(1)}, u32[]{:S(2)}) copy-start(bf16[8,128,512]{2,1,0:T(8,128)(2,1)S(1)} %collective-permute-done.2.refs_1_) | copy-start | bytes 3145732
  37.8 40.1 %collective-permute-start.5 = (bf16[8,128,512]{2,1,0:T(8,128)(2,1)S(1)}, bf16[8,128,512]{2,1,0:T(8,128)(2,1)}, u32[]{:S(2)}, u32[]{:S(2)}) collective-permute-start(bf16[8,128,512]{2,1,0:T(8,128)(2,1)S(1)} %collective-permute-done.2.refs_1_), channel_id=1, source_target_pairs={{4,8},{6,10},{8,4},{10,6},{5,9},{7,11},{9,5},{11,7},{20,24},{22,26... | collective-permute-start | bytes 3145736 | tf_op jit(solution)/shard_map/ppermute | solution.py:574
  40.3 23.9 %all-to-all-start.2 = ((s32[8,1,32]{2,1,0:T(1,128)}), s32[8,1,32]{2,1,0:T(1,128)S(1)}, u32[]{:S(2)}, u32[]{:S(2)}) async-start(s32[8,1,32]{2,1,0:T(1,128)} %broadcast_in_dim.9), calls=%async_computation.2 | async-start | bytes 8192 | tf_op jit(solution)/shard_map/all_to_all | solution.py:557
  76.9 49.5 %collective-permute-start.9 = (bf16[9,128,512]{2,1,0:T(8,128)(2,1)}, bf16[9,128,512]{2,1,0:T(8,128)(2,1)}, u32[]{:S(2)}, u32[]{:S(2)}) collective-permute-start(bf16[9,128,512]{2,1,0:T(8,128)(2,1)} %pack.7.refs_5_), channel_id=1, source_target_pairs={{0,2},{2,0},{4,6},{6,4},{8,10},{10,8},{12,14},{14,12},{1,3},{3,1},... | collective-permute-start | bytes 3538952 | tf_op jit(solution)/shard_map/ppermute | solution.py:574
  77.9 109.1 %copy-start.2 = (bf16[8,128,512]{2,1,0:T(8,128)(2,1)}, bf16[8,128,512]{2,1,0:T(8,128)(2,1)S(1)}, u32[]{:S(2)}) copy-start(bf16[8,128,512]{2,1,0:T(8,128)(2,1)S(1)} %collective-permute-done.4.refs_2_) | copy-start | bytes 3145732
  80.1 46.3 %copy-start.7 = (s32[78]{0:T(128)S(1)}, s32[78]{0:T(128)}, u32[]{:S(2)}) copy-start(s32[78]{0:T(128)} %get-tuple-element.70.table_ref) | copy-start | bytes 940
  80.1 46.2 %collective-permute-start.6 = (bf16[9,128,512]{2,1,0:T(8,128)(2,1)}, bf16[9,128,512]{2,1,0:T(8,128)(2,1)}, u32[]{:S(2)}, u32[]{:S(2)}) collective-permute-start(bf16[9,128,512]{2,1,0:T(8,128)(2,1)} %get-tuple-element.71), channel_id=1, source_target_pairs={{0,4},{2,6},{4,0},{6,2},{8,12},{10,14},{12,8},{14,10},{1,5},{3,7},... | collective-permute-start | bytes 3538952 | tf_op jit(solution)/shard_map/ppermute | solution.py:574
  82.2 44.2 %collective-permute-start.7 = (bf16[8,128,512]{2,1,0:T(8,128)(2,1)}, bf16[8,128,512]{2,1,0:T(8,128)(2,1)}, u32[]{:S(2)}, u32[]{:S(2)}) collective-permute-start(bf16[8,128,512]{2,1,0:T(8,128)(2,1)} %get-tuple-element.72), channel_id=1, source_target_pairs={{4,8},{6,10},{8,4},{10,6},{5,9},{7,11},{9,5},{11,7},{20,24},{22,26... | collective-permute-start | bytes 3145736 | tf_op jit(solution)/shard_map/ppermute | solution.py:574
  83.8 42.6 %collective-permute-start.10 = (bf16[8,128,512]{2,1,0:T(8,128)(2,1)}, bf16[8,128,512]{2,1,0:T(8,128)(2,1)}, u32[]{:S(2)}, u32[]{:S(2)}) collective-permute-start(bf16[8,128,512]{2,1,0:T(8,128)(2,1)} %get-tuple-element.73.refs_10_), channel_id=1, source_target_pairs={{0,2},{2,0},{4,6},{6,4},{8,10},{10,8},{12,14},{14,12},{1,3},{3,1},... | collective-permute-start | bytes 3145736 | tf_op jit(solution)/shard_map/ppermute | solution.py:574
  86.4 40.0 %collective-permute-start.8 = (bf16[4,128,512]{2,1,0:T(8,128)(2,1)}, bf16[4,128,512]{2,1,0:T(8,128)(2,1)}, u32[]{:S(2)}, u32[]{:S(2)}) collective-permute-start(bf16[4,128,512]{2,1,0:T(8,128)(2,1)} %get-tuple-element.154), channel_id=1, source_target_pairs={{4,8},{6,10},{8,4},{10,6},{5,9},{7,11},{9,5},{11,7},{20,24},{22,26... | collective-permute-start | bytes 1572872 | tf_op jit(solution)/shard_map/ppermute | solution.py:574
  126.4 32.4 %copy-start.10 = (bf16[16,128,512]{2,1,0:T(8,128)(2,1)S(1)}, bf16[16,128,512]{2,1,0:T(8,128)(2,1)}, u32[]{:S(2)}) copy-start(bf16[16,128,512]{2,1,0:T(8,128)(2,1)} %refs_0_.17) | copy-start | bytes 6291460
  129.8 27.9 %copy-start.5 = (bf16[8,128,512]{2,1,0:T(8,128)(2,1)}, bf16[8,128,512]{2,1,0:T(8,128)(2,1)S(1)}, u32[]{:S(2)}) copy-start(bf16[8,128,512]{2,1,0:T(8,128)(2,1)S(1)} %get-tuple-element.75.refs_11_) | copy-start | bytes 3145732
  129.8 27.9 %collective-permute-start.11 = (bf16[9,128,512]{2,1,0:T(8,128)(2,1)}, bf16[9,128,512]{2,1,0:T(8,128)(2,1)S(1)}, u32[]{:S(2)}, u32[]{:S(2)}) collective-permute-start(bf16[9,128,512]{2,1,0:T(8,128)(2,1)} %get-tuple-element.74), channel_id=1, source_target_pairs={{0,4},{2,6},{4,0},{6,2},{8,12},{10,14},{12,8},{14,10},{1,5},{3,7},... | collective-permute-start | bytes 3538952 | tf_op jit(solution)/shard_map/ppermute | solution.py:574
  130.8 24.8 %collective-permute-start.12 = (bf16[8,128,512]{2,1,0:T(8,128)(2,1)S(1)}, bf16[8,128,512]{2,1,0:T(8,128)(2,1)S(1)}, u32[]{:S(2)}, u32[]{:S(2)}) collective-permute-start(bf16[8,128,512]{2,1,0:T(8,128)(2,1)S(1)} %get-tuple-element.75.refs_11_), channel_id=1, source_target_pairs={{0,2},{2,0},{4,6},{6,4},{8,10},{10,8},{12,14},{14,12},{1,3},{3,1},... | collective-permute-start | bytes 3145736 | tf_op jit(solution)/shard_map/ppermute | solution.py:574
  132.2 32.1 %copy-start.8 = (s32[32]{0:T(128)S(1)}, s32[32]{0:T(128)}, u32[]{:S(2)}) copy-start(s32[32]{0:T(128)} %get-tuple-element.68.table_ref) | copy-start | bytes 388
  132.2 32.1 %copy-start.24 = (bf16[512,1536]{1,0:T(8,128)(2,1)S(1)}, bf16[512,1536]{1,0:T(8,128)(2,1)}, u32[]{:S(2)}) copy-start(bf16[512,1536]{1,0:T(8,128)(2,1)} %refs_15_.3) | copy-start | bytes 4718596
  132.2 32.1 %copy-start.25 = (bf16[512,512]{1,0:T(8,128)(2,1)S(1)}, bf16[512,512]{1,0:T(8,128)(2,1)}, u32[]{:S(2)}) copy-start(bf16[512,512]{1,0:T(8,128)(2,1)} %refs_16_.1) | copy-start | bytes 1572868
  132.2 0.8 collective-permute-start.13
  160.8 26.2 %collective-permute-start.15 = (bf16[7,128,512]{2,1,0:T(8,128)(2,1)S(1)}, bf16[7,128,512]{2,1,0:T(8,128)(2,1)S(1)}, u32[]{:S(2)}, u32[]{:S(2)}) collective-permute-start(bf16[7,128,512]{2,1,0:T(8,128)(2,1)S(1)} %get-tuple-element.76.refs_10_), channel_id=1, source_target_pairs={{0,2},{2,0},{4,6},{6,4},{8,10},{10,8},{12,14},{14,12},{1,3},{3,1},... | collective-permute-start | bytes 2752520 | tf_op jit(solution)/shard_map/ppermute | solution.py:574
  162.1 24.8 %collective-permute-start.14 = (bf16[6,128,512]{2,1,0:T(8,128)(2,1)S(1)}, bf16[6,128,512]{2,1,0:T(8,128)(2,1)S(1)}, u32[]{:S(2)}, u32[]{:S(2)}) collective-permute-start(bf16[6,128,512]{2,1,0:T(8,128)(2,1)S(1)} %get-tuple-element.78), channel_id=1, source_target_pairs={{0,4},{2,6},{4,0},{6,2},{8,12},{10,14},{12,8},{14,10},{1,5},{3,7},... | collective-permute-start | bytes 2359304 | tf_op jit(solution)/shard_map/ppermute | solution.py:574
  185.5 35.0 %collective-permute-start.17 = (bf16[8,128,512]{2,1,0:T(8,128)(2,1)}, bf16[8,128,512]{2,1,0:T(8,128)(2,1)S(1)}, u32[]{:S(2)}, u32[]{:S(2)}) collective-permute-start(bf16[8,128,512]{2,1,0:T(8,128)(2,1)} %get-tuple-element.81), channel_id=1, source_target_pairs={{0,1},{2,3},{4,5},{6,7},{8,9},{10,11},{12,13},{14,15},{16,17},{18,... | collective-permute-start | bytes 3145736 | tf_op jit(solution)/shard_map/ppermute | solution.py:668
  188.6 18.2 %collective-permute-start.16 = (bf16[6,128,512]{2,1,0:T(8,128)(2,1)S(1)}, bf16[6,128,512]{2,1,0:T(8,128)(2,1)S(1)}, u32[]{:S(2)}, u32[]{:S(2)}) collective-permute-start(bf16[6,128,512]{2,1,0:T(8,128)(2,1)S(1)} %pack.11.refs_12_.refs_13_), channel_id=1, source_target_pairs={{0,2},{2,0},{4,6},{6,4},{8,10},{10,8},{12,14},{14,12},{1,3},{3,1},... | collective-permute-start | bytes 2359304 | tf_op jit(solution)/shard_map/ppermute | solution.py:574
  202.2 18.3 %collective-permute-start.18 = (bf16[4,128,512]{2,1,0:T(8,128)(2,1)}, bf16[4,128,512]{2,1,0:T(8,128)(2,1)}, u32[]{:S(2)}, u32[]{:S(2)}) collective-permute-start(bf16[4,128,512]{2,1,0:T(8,128)(2,1)} %get-tuple-element.82), channel_id=1, source_target_pairs={{0,1},{2,3},{4,5},{6,7},{8,9},{10,11},{12,13},{14,15},{16,17},{18,... | collective-permute-start | bytes 1572872 | tf_op jit(solution)/shard_map/ppermute | solution.py:668
  206.8 14.7 %copy-start.19 = (f32[512]{0:T(512)S(1)}, f32[512]{0:T(512)}, u32[]{:S(2)}) copy-start(f32[512]{0:T(512)} %param.21) | copy-start | bytes 6148
  206.8 14.7 %copy-start.20 = (f32[128]{0:T(128)S(1)}, f32[128]{0:T(128)}, u32[]{:S(2)}) copy-start(f32[128]{0:T(128)} %param.16) | copy-start | bytes 1540
  218.3 3.2 %collective-permute-start.19 = (bf16[4,128,512]{2,1,0:T(8,128)(2,1)}, bf16[4,128,512]{2,1,0:T(8,128)(2,1)}, u32[]{:S(2)}, u32[]{:S(2)}) collective-permute-start(bf16[4,128,512]{2,1,0:T(8,128)(2,1)} %get-tuple-element.83), channel_id=1, source_target_pairs={{0,1},{2,3},{4,5},{6,7},{8,9},{10,11},{12,13},{14,15},{16,17},{18,... | collective-permute-start | bytes 1572872 | tf_op jit(solution)/shard_map/ppermute | solution.py:668
  240.5 3.0 %collective-permute-start.20 = (f32[2,128]{1,0:T(2,128)S(1)}, f32[2,128]{1,0:T(2,128)S(1)}, u32[]{:S(2)}, u32[]{:S(2)}) collective-permute-start(f32[2,128]{1,0:T(2,128)S(1)} %get-tuple-element.85), channel_id=1, source_target_pairs={{1,0},{3,2},{5,4},{7,6},{9,8},{11,10},{13,12},{15,14},{17,16},{19,... | collective-permute-start | bytes 3080 | tf_op jit(solution)/shard_map/ppermute | solution.py:685
  (10 other events, 59.0 us)

commit v5 on v4

--- a/solution.py
+++ b/solution.py
@@ -180,7 +180,7 @@
             pltpu.SemaphoreType.DMA((slots,)),
         ],
         cost_estimate=pl.CostEstimate(
-            flops=0, bytes_accessed=4 * slots * piece[0] * piece[1], transcendentals=0
+            flops=0, bytes_accessed=piece[0] * piece[1], transcendentals=0
         ),
         compiler_params=pltpu.CompilerParams(vmem_limit_bytes=VMEM_LIMIT),
         name="pack",
@@ -349,17 +349,17 @@
     return arrived.reshape(blocks * capacity, agents, width), named * capacity + slot
 
 
-OUTWARD_READY = {1: (0, 2, 2), 2: (1, 3, 3), 3: (2, 3, 4)}
-ACROSS_READY = {0: (0, 1, 1), 1: (0, 0, 0), 2: (0, 2, 2), 3: (1, 2, 3)}
+OUTWARD_READY = {1: (0, 1, 1), 2: (1, 3, 3), 3: (2, 3, 4)}
+ACROSS_READY = {0: (1, 2, 2), 1: (0, 0, 0), 2: (1, 3, 3), 3: (2, 3, 4)}
 OUTWARD_DUE = (3, 4, 4)
-ACROSS_DUE = (2, 3, 4)
+ACROSS_DUE = (3, 4, 5)
 
 
 def relay_sizes(steps, capacity):
     half, quarter = steps // 2, steps // 4
     chunks = [half, quarter, quarter]
-    outward = [half, half, half + 1, half + 1, quarter + 2]
-    across = [capacity + 1, half, half, half - 1, quarter + 2]
+    outward = [half, half, half, half, quarter + 2]
+    across = [quarter, half, half, half - 1, quarter + 2, quarter + 2]
     return chunks, outward, across
 
 
@@ -403,6 +403,11 @@
 
     lax.fori_loop(0, sum(outward) + sum(across), clear, 0)
 
+    @pl.when(me == 0)
+    def _():
+        for n in range(outward[1]):
+            out_ref[e_base[1] + n] = codes["own"] * SPAN + starts[1] + n
+
     def named(dest, t, source):
         hit = entry(dest, t, 0) == source
         for j in range(1, list_length):
@@ -428,15 +433,15 @@
     for turn in range(2):
         sender = row if turn == 0 else 1 - row
         empty(outward)
-        room[0], room[1] = outward[0], outward[1]
+        room[0] = outward[0]
         for k, count in enumerate(chunks):
             for u in (1, 2, 3):
 
-                def first_piece(n, _, u=u):
-                    eloc[(turn * COLUMNS + u) * steps + n] = (u - 1) * SPAN + n
+                def first_piece(n, _):
+                    eloc[(turn * COLUMNS + 1) * steps + n] = n
                     return 0
 
-                if u in (1, 2) and k == 0:
+                if u == 1 and k == 0:
                     lax.fori_loop(0, count, first_piece, 0)
                     continue
 
@@ -479,7 +484,7 @@
                     else:
                         where = eloc[(turn * COLUMNS + u) * steps + t]
                         lies = codes["edge"][0] * SPAN + where
-                        when = jnp.where(where < 0, len(across), where // SPAN)
+                        when = jnp.where(where < 0, len(across), where // SPAN + 1)
                     when = jnp.where(inner, ACROSS_READY[u][k], when)
                     lies = jnp.where(inner, inner_place(codes, starts, u, k) + n, lies)
                     batch = choose(across, when)
@@ -581,51 +586,52 @@
     def pick(names):
         return {code: arrays[code] for code in names}
 
-    first = embedded[: chunks[0]]
-    arrays[edge[0]] = send(first, edges)
-    arrays[swapped[0]] = send(first, swap)
-    everyone = shared(lists.reshape(-1), "agent").reshape(-1)
-    out_table, in_table, flag = plan(
-        everyone, place, steps, list_length, chunks, outward, across
-    )
-    arrays[far[0]] = send(arrays[edge[0]], swap)
-    column = index // ROWS
-    outer = (column == 0) | (column == COLUMNS - 1)
-    slots = jnp.arange(outward[1], dtype=jnp.int32)
-    table = jnp.where(outer, own * SPAN + starts[1] + slots, swapped[0] * SPAN + slots)
-    packed = pack(table, pick([own, swapped[0]]), [(0, outward[1], None), (None, outward[1], starts[1])])
-    arrays[edge[1]] = send(packed[0], edges)
-    arrays[swapped[1]] = send(packed[1], swap)
-    (packed,) = pack(out_table, pick([own, edge[0], swapped[0]]), [(y_base[0], across[0], None)], packed[:1])
-    arrays[rows[0]] = send(packed, over)
-    for k in (1, 2):
-        at = starts[k] - starts[1]
-        arrays[far[k]] = send(arrays[edge[1]][at : at + chunks[k]], swap)
+    def across_part(n):
+        return (y_base[n], across[n], None)
 
     def stage(n, reads, settled, after=()):
-        parts = [(y_base[n - 1], across[n - 1], None)]
+        parts = [across_part(n)]
         if n < len(outward):
             parts.append((e_base[n], outward[n], None))
+        if n == 1:
+            parts.append((None, outward[1], starts[1]))
         after = tuple(arrays[rows[b]] for b in settled) + tuple(after)
         packed = pack(out_table, pick([own] + reads), parts, after)
         if n < len(outward):
             arrays[edge[n]] = send(packed[1], edges)
-        arrays[rows[n - 1]] = send(packed[0], over)
-        return packed[0]
-
-    reads = edge[:2] + swapped[:1] + far[:1]
-    token = stage(2, reads, (), (packed,))
+        arrays[rows[n]] = send(packed[0], over)
+        return packed
+
+    everyone = shared(lists.reshape(-1), "agent").reshape(-1)
+    begin = jnp.minimum(everyone[0], 0)
+    first = lax.dynamic_slice_in_dim(embedded, begin, chunks[0], 0)
+    arrays[edge[0]] = send(first, edges)
+    arrays[swapped[0]] = send(first, swap)
+    out_table, in_table, flag = plan(
+        everyone, place, steps, list_length, chunks, outward, across
+    )
+    (token,) = pack(out_table, pick([own]), [across_part(0)])
+    arrays[rows[0]] = send(token, over)
     crowded = jnp.max(shared(flag, ("groups", "agent", "tm")))
+    arrays[far[0]] = send(arrays[edge[0]], swap)
+    reads = edge[:1] + swapped[:1]
+    packed = stage(1, reads, (0,), (token, crowded.reshape(1)))
+    arrays[swapped[1]] = send(packed[2], swap)
+    for k in (1, 2):
+        at = starts[k] - starts[1]
+        arrays[far[k]] = send(arrays[edge[1]][at : at + chunks[k]], swap)
+    reads = reads + edge[1:2] + far[:1]
+    packed = stage(2, reads, (1,), packed[:1])
     reads = reads + edge[2:3] + swapped[1:] + far[1:2]
-    token = stage(3, reads, (0, 1), (token, crowded.reshape(1)))
+    packed = stage(3, reads, (2,), packed[:1])
     reads = reads + edge[3:4] + far[2:3]
-    token = stage(4, reads, (2,), (token,))
-    done = [attention(0, chunks[0], due(arrays, codes, starts, 0), in_table, (token,))]
+    packed = stage(4, reads, (3,), packed[:1])
+    done = [attention(0, chunks[0], due(arrays, codes, starts, 0), in_table, packed[:1])]
     reads = reads + edge[4:5]
-    token = stage(5, reads, (3,), (done[0][0],))
+    packed = stage(5, reads, (4,), (done[0][0],))
     for k in (1, 2):
         done.append(
-            attention(starts[k], chunks[k], due(arrays, codes, starts, k), in_table, (token, done[-1][0]))
+            attention(starts[k], chunks[k], due(arrays, codes, starts, k), in_table, (packed[0], done[-1][0]))
         )
     return done, crowded
 

time: 246 us -> 236 us (0.959)
  starting transfers between devices: 59.7 us -> 32.7 us
  waiting for transfers between devices: 47.9 us -> 64.5 us
  blocking collectives: 37.3 us -> 27.4 us
  local copies, waits for them, and re-layouts: 9.24 us -> 14.6 us
  Pallas kernels: 87.8 us -> 91.3 us
    ppermute x15 -> x16, waiting for transfers between devices: 27.3 us -> 61.7 us  [relay(): send = lambda value, pairs: lax.ppermute(value, 'agent', pairs)]
    ppermute x15 -> x16, starting transfers between devices: 48.1 us -> 27.2 us  [relay(): send = lambda value, pairs: lax.ppermute(value, 'agent', pairs)]
    all_to_all x1 -> x0, waiting for transfers between devices: 18.5 us -> none  [shared(): return lax.all_to_all(rows, axes, split_axis=0, concat_axis=0, tiled=True)]
    all_to_all x1 -> x2, blocking collectives: 37.3 us -> 27.4 us  [shared(): return lax.all_to_all(rows, axes, split_axis=0, concat_axis=0, tiled=True)]
    unnamed x45 -> x61, local copies, waits for them, and re-layouts: 3.4 us -> 10.5 us
    all_to_all x1 -> x0, starting transfers between devices: 4.71 us -> none  [shared(): return lax.all_to_all(rows, axes, split_axis=0, concat_axis=0, tiled=True)]
  transfers between devices with their start and end apart: 20 -> 20, of which waited for: 6 -> 9; matrix products, arithmetic and copies ran while one was open for 2% -> 1% of each run, Pallas kernels for 25% -> 26%
where the time goes in v5:
time: 236 us; the launch traced here: 235 us
  Pallas kernels  91.3 us (39%)
  waiting for transfers between devices  64.5 us (27%)
  starting transfers between devices  32.7 us (14%)
  blocking collectives  27.4 us (12%)
  local copies, waits for them, and re-layouts  14.6 us (6%)
  between operations  2.37 us (1%)
    ppermute x16, waiting for transfers between devices, relay(): send = lambda value, pairs: lax.ppermute(value, 'agent', pairs)  61.7 us
    pallas_call x3, Pallas kernels, agent_stage(): pl.pallas_call(functools.partial(agent_kernel, list_length, first_step, t...  46.4 us
    all_to_all x2, blocking collectives, shared(): return lax.all_to_all(rows, axes, split_axis=0, concat_axis=0, tiled=True)  27.4 us
    ppermute x16, starting transfers between devices, relay(): send = lambda value, pairs: lax.ppermute(value, 'agent', pairs)  27.2 us
    pallas_call x1, Pallas kernels, time_stage(): pl.pallas_call(functools.partial(time_kernel, len(residuals), steps, tile...  18.9 us
    pallas_call x6, Pallas kernels, pack(): pl.pallas_call(functools.partial(pack_kernel, tuple(arrays), tuple(parts)...  16.5 us
    unnamed x61, local copies, waits for them, and re-layouts  10.5 us
    pallas_call x1, Pallas kernels, plan(): pl.pallas_call(functools.partial(plan_kernel, steps, list_length, chunks,...  8.16 us
  transfers between devices with their start and end apart: 20, of which 9 were waited for; matrix products, arithmetic and copies ran while one was open for 1% of the time, Pallas kernels for 26%

profile of v5, /device:TPU:0, one launch (start us, length us, event | category | flops | bytes accessed | tf_op | source)
XLA Modules:
  0.0 234.9 jit_solution(13339369513464814317)
XLA Ops:
  1.5 13.5 %all_to_all.24 = s32[8,1,32]{2,1,0:T(1,128)S(1)} all-to-all(s32[8,1,32]{2,1,0:T(1,128)S(1)} %broadcast_in_dim.9), channel_id=1, replica_groups=mesh['groups'=2,'agent'=8,'tm'=2] {'agent'}, dimensions={0} | all-to-all | bytes 2048 | tf_op jit(solution)/shard_map/all_to_all | solution.py:562
  17.5 2.3 constant_dynamic-slice_fusion
  21.7 8.2 %plan.1 = (s32[77]{0:T(128)}, s32[32]{0:T(128)}, s32[1]{0:T(128)}) custom-call(s32[2]{0:T(128)} %pad_add_fusion.place_ref, s32[256]{0:T(256)} %copy-done.29), custom_call_target="tpu_custom_call" | custom-call | tf_op jit(solution)/shard_map/plan/pallas_call | solution.py:541
  30.6 1.9 pack.6.refs_4_
  33.9 13.9 %all_to_all.25 = s32[32,1,1]{2,1,0:T(1,128)S(1)} all-to-all(s32[32,1,1]{2,1,0:T(1,128)S(1)} %broadcast_in_dim.11), channel_id=1, replica_groups=mesh['groups'=2,'agent'=8,'tm'=2] {'groups','agent','tm'}, dimensions={0} | all-to-all | bytes 256 | tf_op jit(solution)/shard_map/all_to_all | solution.py:562
  49.4 6.1 %pack.7 = (bf16[8,128,512]{2,1,0:T(8,128)(2,1)S(1)}, bf16[8,128,512]{2,1,0:T(8,128)(2,1)S(1)}, bf16[8,128,512]{2,1,0:T(8,128)(2,1)S(1)}) custom-call(s32[77]{0:T(128)S(1)} %copy-done.12, bf16[16,128,512]{2,1,0:T(8,128)(2,1)} %refs_0_.17, bf16[8,128,512]{2,1,0:T(8,128)(2,1)S(1)} %collective-permute-done.2.refs_1_, bf16[8,128,512]{2,1,0:T(8,128)(2,1)} %copy-done.3, ...), custom_call_target="tpu_custom_call" | custom-call | bytes 65536 | tf_op jit(solution)/shard_map/pack/pallas_call | solution.py:171
  56.4 1.4 collective-permute-start.7
  59.3 21.6 %collective-permute-done.5.refs_3_.refs_2_ = bf16[8,128,512]{2,1,0:T(8,128)(2,1)S(1)} collective-permute-done((bf16[8,128,512]{2,1,0:T(8,128)(2,1)S(1)}, bf16[8,128,512]{2,1,0:T(8,128)(2,1)S(1)}, u32[]{:S(2)}, u32[]{:S(2)}) %collective-permute-start.5) | collective-permute-done | bytes 1048608 | tf_op jit(solution)/shard_map/ppermute | solution.py:579
  83.1 1.2 copy-done.4
  84.4 2.9 %pack.8 = (bf16[8,128,512]{2,1,0:T(8,128)(2,1)S(1)}, bf16[8,128,512]{2,1,0:T(8,128)(2,1)S(1)}) custom-call(s32[77]{0:T(128)S(1)} %copy-done.12, bf16[16,128,512]{2,1,0:T(8,128)(2,1)S(1)} %copy-done.14, bf16[8,128,512]{2,1,0:T(8,128)(2,1)S(1)} %collective-permute-done.2.refs_1_, bf16[8,128,512]{2,1,0:T(8,128)(2,1)S(1)} %copy-done.4, ...), custom_call_target="tpu_custom_call" | custom-call | bytes 65536 | tf_op jit(solution)/shard_map/pack/pallas_call | solution.py:171
  87.2 1.5 collective-permute-start.11
  88.7 4.8 %collective-permute-start.8 = (bf16[8,128,512]{2,1,0:T(8,128)(2,1)S(1)}, bf16[8,128,512]{2,1,0:T(8,128)(2,1)S(1)}, u32[]{:S(2)}, u32[]{:S(2)}) collective-permute-start(bf16[8,128,512]{2,1,0:T(8,128)(2,1)S(1)} %get-tuple-element.73), channel_id=1, source_target_pairs={{0,4},{2,6},{4,0},{6,2},{8,12},{10,14},{12,8},{14,10},{1,5},{3,7},... | collective-permute-start | bytes 3145736 | tf_op jit(solution)/shard_map/ppermute | solution.py:579
  94.3 17.7 %collective-permute-done.11.refs_8_.refs_9_.refs_10_ = bf16[8,128,512]{2,1,0:T(8,128)(2,1)S(1)} collective-permute-done((bf16[8,128,512]{2,1,0:T(8,128)(2,1)S(1)}, bf16[8,128,512]{2,1,0:T(8,128)(2,1)S(1)}, u32[]{:S(2)}, u32[]{:S(2)}) %collective-permute-start.11) | collective-permute-done | bytes 1048608 | tf_op jit(solution)/shard_map/ppermute | solution.py:579
  112.1 2.0 collective-permute-done.8.refs_5_.refs_3_
  115.1 2.0 pack.9
  117.2 6.8 %collective-permute-start.12 = (bf16[8,128,512]{2,1,0:T(8,128)(2,1)S(1)}, bf16[8,128,512]{2,1,0:T(8,128)(2,1)S(1)}, u32[]{:S(2)}, u32[]{:S(2)}) collective-permute-start(bf16[8,128,512]{2,1,0:T(8,128)(2,1)S(1)} %get-tuple-element.76), channel_id=1, source_target_pairs={{0,4},{2,6},{4,0},{6,2},{8,12},{10,14},{12,8},{14,10},{1,5},{3,7},... | collective-permute-start | bytes 3145736 | tf_op jit(solution)/shard_map/ppermute | solution.py:579
  124.0 1.6 collective-permute-start.13
  126.5 17.8 %collective-permute-done.13.refs_10_.refs_11_ = bf16[7,128,512]{2,1,0:T(8,128)(2,1)S(1)} collective-permute-done((bf16[7,128,512]{2,1,0:T(8,128)(2,1)S(1)}, bf16[7,128,512]{2,1,0:T(8,128)(2,1)S(1)}, u32[]{:S(2)}, u32[]{:S(2)}) %collective-permute-start.13) | collective-permute-done | bytes 917536 | tf_op jit(solution)/shard_map/ppermute | solution.py:579
  146.3 2.3 pack.10
  149.7 3.1 %collective-permute-start.16 = (bf16[6,128,512]{2,1,0:T(8,128)(2,1)S(1)}, bf16[6,128,512]{2,1,0:T(8,128)(2,1)S(1)}, u32[]{:S(2)}, u32[]{:S(2)}) collective-permute-start(bf16[6,128,512]{2,1,0:T(8,128)(2,1)S(1)} %get-tuple-element.78.refs_11_), channel_id=1, source_target_pairs={{0,2},{2,0},{4,6},{6,4},{8,10},{10,8},{12,14},{14,12},{1,3},{3,1},... | collective-permute-start | bytes 2359304 | tf_op jit(solution)/shard_map/ppermute | solution.py:579
  152.9 23.1 %agent_stage.5 = (f32[8,128,512]{2,1,0:T(8,128)}, bf16[8,128,512]{2,1,0:T(8,128)(2,1)}) custom-call(s32[32]{0:T(128)S(1)} %copy-done.13, bf16[16,128,512]{2,1,0:T(8,128)(2,1)S(1)} %copy-done.14, bf16[16,128,512]{2,1,0:T(8,128)(2,1)S(1)} %copy-done.14, bf16[8,128,512]{2,1,0:T(8,128)(2,1)S(1)} %collective-permute-done.2.refs_1_, ...), custom_call_target="tpu_custom_call" | custom-call | flops 37580963840 | bytes 6291456 | tf_op jit(solution)/shard_map/agent_stage/pallas_call | solution.py:106
  176.0 1.4 collective-permute-start.18
  177.4 1.3 pack.11.refs_13_.refs_14_
  179.7 11.5 %agent_stage.6 = (f32[4,128,512]{2,1,0:T(8,128)S(1)}, bf16[4,128,512]{2,1,0:T(8,128)(2,1)}) custom-call(s32[32]{0:T(128)S(1)} %copy-done.13, bf16[16,128,512]{2,1,0:T(8,128)(2,1)S(1)} %copy-done.14, bf16[16,128,512]{2,1,0:T(8,128)(2,1)S(1)} %copy-done.14, bf16[8,128,512]{2,1,0:T(8,128)(2,1)} %copy-done.2, bf16[8,128,512]{2,1,0:T(8,128)(2,1)} %copy-done, ...), custom_call_target="tpu_custom_call" | custom-call | flops 18790481920 | bytes 3145728 | tf_op jit(solution)/shard_map/agent_stage/pallas_call | solution.py:106
  192.2 1.5 collective-permute-start.19
  193.7 1.4 collective-permute-done.17.refs_13_
  195.1 11.7 %agent_stage.7 = (f32[4,128,512]{2,1,0:T(8,128)}, bf16[4,128,512]{2,1,0:T(8,128)(2,1)}) custom-call(s32[32]{0:T(128)S(1)} %copy-done.13, bf16[16,128,512]{2,1,0:T(8,128)(2,1)S(1)} %copy-done.14, bf16[16,128,512]{2,1,0:T(8,128)(2,1)S(1)} %copy-done.14, bf16[8,128,512]{2,1,0:T(8,128)(2,1)} %copy-done.2, bf16[8,128,512]{2,1,0:T(8,128)(2,1)} %copy-done, ...), custom_call_target="tpu_custom_call" | custom-call | flops 18790481920 | bytes 3145728 | tf_op jit(solution)/shard_map/agent_stage/pallas_call | solution.py:106
  206.8 1.3 collective-permute-start.20
  208.2 1.7 collective-permute-done.20.refs_5_
  211.1 18.9 %time_stage.3 = (f32[16,128]{1,0:T(8,128)}, f32[2,128]{1,0:T(2,128)S(1)}) custom-call(s32[1]{0:T(128)} %bitcast.11.offset_ref, f32[8,128,512]{2,1,0:T(8,128)} %get-tuple-element.79.refs_12_.refs_14_.refs_0_, f32[4,128,512]{2,1,0:T(8,128)S(1)} %copy-done.7, f32[4,128,512]{2,1,0:T(8,128)S(1)} %copy-done.8, ...), custom_call_target="tpu_custom_call" | custom-call | tf_op jit(solution)/shard_map/time_stage/pallas_call | solution.py:285
  230.0 1.3 collective-permute-start.21
  233.5 1.4 advantage_stage.3
  (95 shorter events, 23.2 us)
Async XLA Ops:
  19.8 28.7 %collective-permute-start.2 = (bf16[8,128,512]{2,1,0:T(8,128)(2,1)}, bf16[8,128,512]{2,1,0:T(8,128)(2,1)S(1)}, u32[]{:S(2)}, u32[]{:S(2)}) collective-permute-start(bf16[8,128,512]{2,1,0:T(8,128)(2,1)} %constant_dynamic-slice_fusion), channel_id=1, source_target_pairs={{0,4},{2,6},{4,0},{6,2},{8,12},{10,14},{12,8},{14,10},{1,5},{3,7},... | collective-permute-start | bytes 3145736 | tf_op jit(solution)/shard_map/ppermute | solution.py:579
  20.3 28.1 %collective-permute-start.3 = (bf16[8,128,512]{2,1,0:T(8,128)(2,1)}, bf16[8,128,512]{2,1,0:T(8,128)(2,1)S(1)}, u32[]{:S(2)}, u32[]{:S(2)}) collective-permute-start(bf16[8,128,512]{2,1,0:T(8,128)(2,1)} %constant_dynamic-slice_fusion), channel_id=1, source_target_pairs={{4,8},{6,10},{8,4},{10,6},{5,9},{7,11},{9,5},{11,7},{20,24},{22,26... | collective-permute-start | bytes 3145736 | tf_op jit(solution)/shard_map/ppermute | solution.py:579
  29.9 19.6 %copy-start.12 = (s32[77]{0:T(128)S(1)}, s32[77]{0:T(128)}, u32[]{:S(2)}) copy-start(s32[77]{0:T(128)} %get-tuple-element.70.table_ref) | copy-start | bytes 928
  32.5 16.0 %collective-permute-start.4 = (bf16[4,128,512]{2,1,0:T(8,128)(2,1)S(1)}, bf16[4,128,512]{2,1,0:T(8,128)(2,1)S(1)}, u32[]{:S(2)}, u32[]{:S(2)}) collective-permute-start(bf16[4,128,512]{2,1,0:T(8,128)(2,1)S(1)} %pack.6.refs_4_), channel_id=1, source_target_pairs={{0,2},{2,0},{4,6},{6,4},{8,10},{10,8},{12,14},{14,12},{1,3},{3,1},... | collective-permute-start | bytes 1572872 | tf_op jit(solution)/shard_map/ppermute | solution.py:579
  48.5 128.9 %copy-start.2 = (bf16[8,128,512]{2,1,0:T(8,128)(2,1)}, bf16[8,128,512]{2,1,0:T(8,128)(2,1)S(1)}, u32[]{:S(2)}) copy-start(bf16[8,128,512]{2,1,0:T(8,128)(2,1)S(1)} %collective-permute-done.2.refs_1_) | copy-start | bytes 3145732
  49.4 33.7 %copy-start.14 = (bf16[16,128,512]{2,1,0:T(8,128)(2,1)S(1)}, bf16[16,128,512]{2,1,0:T(8,128)(2,1)}, u32[]{:S(2)}) copy-start(bf16[16,128,512]{2,1,0:T(8,128)(2,1)} %refs_0_.17) | copy-start | bytes 6291460
  55.6 25.5 %copy-start.9 = (bf16[8,128,512]{2,1,0:T(8,128)(2,1)}, bf16[8,128,512]{2,1,0:T(8,128)(2,1)S(1)}, u32[]{:S(2)}) copy-start(bf16[8,128,512]{2,1,0:T(8,128)(2,1)S(1)} %get-tuple-element.72.refs_6_) | copy-start | bytes 3145732
  55.6 25.4 %collective-permute-start.5 = (bf16[8,128,512]{2,1,0:T(8,128)(2,1)S(1)}, bf16[8,128,512]{2,1,0:T(8,128)(2,1)S(1)}, u32[]{:S(2)}, u32[]{:S(2)}) collective-permute-start(bf16[8,128,512]{2,1,0:T(8,128)(2,1)S(1)} %get-tuple-element.71), channel_id=1, source_target_pairs={{0,4},{2,6},{4,0},{6,2},{8,12},{10,14},{12,8},{14,10},{1,5},{3,7},... | collective-permute-start | bytes 3145736 | tf_op jit(solution)/shard_map/ppermute | solution.py:579
  56.4 24.6 %collective-permute-start.7 = (bf16[8,128,512]{2,1,0:T(8,128)(2,1)S(1)}, bf16[8,128,512]{2,1,0:T(8,128)(2,1)S(1)}, u32[]{:S(2)}, u32[]{:S(2)}) collective-permute-start(bf16[8,128,512]{2,1,0:T(8,128)(2,1)S(1)} %get-tuple-element.72.refs_6_), channel_id=1, source_target_pairs={{0,2},{2,0},{4,6},{6,4},{8,10},{10,8},{12,14},{14,12},{1,3},{3,1},... | collective-permute-start | bytes 3145736 | tf_op jit(solution)/shard_map/ppermute | solution.py:579
  57.9 23.2 %collective-permute-start.6 = (bf16[8,128,512]{2,1,0:T(8,128)(2,1)S(1)}, bf16[8,128,512]{2,1,0:T(8,128)(2,1)S(1)}, u32[]{:S(2)}, u32[]{:S(2)}) collective-permute-start(bf16[8,128,512]{2,1,0:T(8,128)(2,1)S(1)} %collective-permute-done.2.refs_1_), channel_id=1, source_target_pairs={{4,8},{6,10},{8,4},{10,6},{5,9},{7,11},{9,5},{11,7},{20,24},{22,26... | collective-permute-start | bytes 3145736 | tf_op jit(solution)/shard_map/ppermute | solution.py:579
  58.6 35.7 %collective-permute-start.9 = (bf16[8,128,512]{2,1,0:T(8,128)(2,1)S(1)}, bf16[8,128,512]{2,1,0:T(8,128)(2,1)S(1)}, u32[]{:S(2)}, u32[]{:S(2)}) collective-permute-start(bf16[8,128,512]{2,1,0:T(8,128)(2,1)S(1)} %get-tuple-element.74), channel_id=1, source_target_pairs={{4,8},{6,10},{8,4},{10,6},{5,9},{7,11},{9,5},{11,7},{20,24},{22,26... | collective-permute-start | bytes 3145736 | tf_op jit(solution)/shard_map/ppermute | solution.py:579
  81.0 33.1 %copy-start = (bf16[8,128,512]{2,1,0:T(8,128)(2,1)}, bf16[8,128,512]{2,1,0:T(8,128)(2,1)S(1)}, u32[]{:S(2)}) copy-start(bf16[8,128,512]{2,1,0:T(8,128)(2,1)S(1)} %collective-permute-done.5.refs_3_.refs_2_) | copy-start | bytes 3145732
  87.2 26.9 %copy-start.10 = (bf16[8,128,512]{2,1,0:T(8,128)(2,1)}, bf16[8,128,512]{2,1,0:T(8,128)(2,1)S(1)}, u32[]{:S(2)}) copy-start(bf16[8,128,512]{2,1,0:T(8,128)(2,1)S(1)} %get-tuple-element.75.refs_9_) | copy-start | bytes 3145732
  87.2 24.8 %collective-permute-start.11 = (bf16[8,128,512]{2,1,0:T(8,128)(2,1)S(1)}, bf16[8,128,512]{2,1,0:T(8,128)(2,1)S(1)}, u32[]{:S(2)}, u32[]{:S(2)}) collective-permute-start(bf16[8,128,512]{2,1,0:T(8,128)(2,1)S(1)} %get-tuple-element.75.refs_9_), channel_id=1, source_target_pairs={{0,2},{2,0},{4,6},{6,4},{8,10},{10,8},{12,14},{14,12},{1,3},{3,1},... | collective-permute-start | bytes 3145736 | tf_op jit(solution)/shard_map/ppermute | solution.py:579
  88.7 25.4 %collective-permute-start.8 = (bf16[8,128,512]{2,1,0:T(8,128)(2,1)S(1)}, bf16[8,128,512]{2,1,0:T(8,128)(2,1)S(1)}, u32[]{:S(2)}, u32[]{:S(2)}) collective-permute-start(bf16[8,128,512]{2,1,0:T(8,128)(2,1)S(1)} %get-tuple-element.73), channel_id=1, source_target_pairs={{0,4},{2,6},{4,0},{6,2},{8,12},{10,14},{12,8},{14,10},{1,5},{3,7},... | collective-permute-start | bytes 3145736 | tf_op jit(solution)/shard_map/ppermute | solution.py:579
  93.6 0.7 collective-permute-start.10
  94.3 19.8 %copy-start.17 = (bf16[8,128,512]{2,1,0:T(8,128)(2,1)}, bf16[8,128,512]{2,1,0:T(8,128)(2,1)S(1)}, u32[]{:S(2)}) copy-start(bf16[8,128,512]{2,1,0:T(8,128)(2,1)S(1)} %collective-permute-done.9.refs_6_) | copy-start | bytes 3145732
  117.2 28.1 %collective-permute-start.12 = (bf16[8,128,512]{2,1,0:T(8,128)(2,1)S(1)}, bf16[8,128,512]{2,1,0:T(8,128)(2,1)S(1)}, u32[]{:S(2)}, u32[]{:S(2)}) collective-permute-start(bf16[8,128,512]{2,1,0:T(8,128)(2,1)S(1)} %get-tuple-element.76), channel_id=1, source_target_pairs={{0,4},{2,6},{4,0},{6,2},{8,12},{10,14},{12,8},{14,10},{1,5},{3,7},... | collective-permute-start | bytes 3145736 | tf_op jit(solution)/shard_map/ppermute | solution.py:579
  124.0 20.3 %collective-permute-start.13 = (bf16[7,128,512]{2,1,0:T(8,128)(2,1)S(1)}, bf16[7,128,512]{2,1,0:T(8,128)(2,1)S(1)}, u32[]{:S(2)}, u32[]{:S(2)}) collective-permute-start(bf16[7,128,512]{2,1,0:T(8,128)(2,1)S(1)} %get-tuple-element.77.refs_11_), channel_id=1, source_target_pairs={{0,2},{2,0},{4,6},{6,4},{8,10},{10,8},{12,14},{14,12},{1,3},{3,1},... | collective-permute-start | bytes 2752520 | tf_op jit(solution)/shard_map/ppermute | solution.py:579
  125.6 27.2 %copy-start.1 = (bf16[8,128,512]{2,1,0:T(8,128)(2,1)S(1)}, bf16[8,128,512]{2,1,0:T(8,128)(2,1)}, u32[]{:S(2)}) copy-start(bf16[8,128,512]{2,1,0:T(8,128)(2,1)} %copy-done) | copy-start | bytes 3145732
  125.6 27.2 %copy-start.13 = (s32[32]{0:T(128)S(1)}, s32[32]{0:T(128)}, u32[]{:S(2)}) copy-start(s32[32]{0:T(128)} %get-tuple-element.69.table_ref) | copy-start | bytes 388
  125.6 27.2 %copy-start.33 = (bf16[512,512]{1,0:T(8,128)(2,1)S(1)}, bf16[512,512]{1,0:T(8,128)(2,1)}, u32[]{:S(2)}) copy-start(bf16[512,512]{1,0:T(8,128)(2,1)} %refs_17_.1) | copy-start | bytes 1572868
  125.6 0.8 collective-permute-start.14
  148.6 28.8 %collective-permute-start.15 = (bf16[6,128,512]{2,1,0:T(8,128)(2,1)S(1)}, bf16[6,128,512]{2,1,0:T(8,128)(2,1)S(1)}, u32[]{:S(2)}, u32[]{:S(2)}) collective-permute-start(bf16[6,128,512]{2,1,0:T(8,128)(2,1)S(1)} %get-tuple-element.80), channel_id=1, source_target_pairs={{0,4},{2,6},{4,0},{6,2},{8,12},{10,14},{12,8},{14,10},{1,5},{3,7},... | collective-permute-start | bytes 2359304 | tf_op jit(solution)/shard_map/ppermute | solution.py:579
  149.7 27.6 %collective-permute-start.16 = (bf16[6,128,512]{2,1,0:T(8,128)(2,1)S(1)}, bf16[6,128,512]{2,1,0:T(8,128)(2,1)S(1)}, u32[]{:S(2)}, u32[]{:S(2)}) collective-permute-start(bf16[6,128,512]{2,1,0:T(8,128)(2,1)S(1)} %get-tuple-element.78.refs_11_), channel_id=1, source_target_pairs={{0,2},{2,0},{4,6},{6,4},{8,10},{10,8},{12,14},{14,12},{1,3},{3,1},... | collective-permute-start | bytes 2359304 | tf_op jit(solution)/shard_map/ppermute | solution.py:579
  152.8 24.6 %copy-start.5 = (bf16[8,128,512]{2,1,0:T(8,128)(2,1)S(1)}, bf16[8,128,512]{2,1,0:T(8,128)(2,1)}, u32[]{:S(2)}) copy-start(bf16[8,128,512]{2,1,0:T(8,128)(2,1)} %copy-done.3) | copy-start | bytes 3145732
  176.0 32.1 %collective-permute-start.18 = (bf16[8,128,512]{2,1,0:T(8,128)(2,1)}, bf16[8,128,512]{2,1,0:T(8,128)(2,1)S(1)}, u32[]{:S(2)}, u32[]{:S(2)}) collective-permute-start(bf16[8,128,512]{2,1,0:T(8,128)(2,1)} %get-tuple-element.83), channel_id=1, source_target_pairs={{0,1},{2,3},{4,5},{6,7},{8,9},{10,11},{12,13},{14,15},{16,17},{18,... | collective-permute-start | bytes 3145736 | tf_op jit(solution)/shard_map/ppermute | solution.py:674
  178.8 16.3 %collective-permute-start.17 = (bf16[6,128,512]{2,1,0:T(8,128)(2,1)S(1)}, bf16[6,128,512]{2,1,0:T(8,128)(2,1)S(1)}, u32[]{:S(2)}, u32[]{:S(2)}) collective-permute-start(bf16[6,128,512]{2,1,0:T(8,128)(2,1)S(1)} %pack.11.refs_13_.refs_14_), channel_id=1, source_target_pairs={{0,2},{2,0},{4,6},{6,4},{8,10},{10,8},{12,14},{14,12},{1,3},{3,1},... | collective-permute-start | bytes 2359304 | tf_op jit(solution)/shard_map/ppermute | solution.py:579
  192.2 16.0 %collective-permute-start.19 = (bf16[4,128,512]{2,1,0:T(8,128)(2,1)}, bf16[4,128,512]{2,1,0:T(8,128)(2,1)S(1)}, u32[]{:S(2)}, u32[]{:S(2)}) collective-permute-start(bf16[4,128,512]{2,1,0:T(8,128)(2,1)} %get-tuple-element.84), channel_id=1, source_target_pairs={{0,1},{2,3},{4,5},{6,7},{8,9},{10,11},{12,13},{14,15},{16,17},{18,... | collective-permute-start | bytes 1572872 | tf_op jit(solution)/shard_map/ppermute | solution.py:674
  206.8 3.0 %collective-permute-start.20 = (bf16[4,128,512]{2,1,0:T(8,128)(2,1)}, bf16[4,128,512]{2,1,0:T(8,128)(2,1)S(1)}, u32[]{:S(2)}, u32[]{:S(2)}) collective-permute-start(bf16[4,128,512]{2,1,0:T(8,128)(2,1)} %get-tuple-element.85), channel_id=1, source_target_pairs={{0,1},{2,3},{4,5},{6,7},{8,9},{10,11},{12,13},{14,15},{16,17},{18,... | collective-permute-start | bytes 1572872 | tf_op jit(solution)/shard_map/ppermute | solution.py:674
  211.1 23.8 %copy-start.28 = (s32[1,16,2]{1,2,0:T(2,128)S(1)}, s32[1,16,2]{1,2,0:T(2,128)}, u32[]{:S(2)}) copy-start(s32[1,16,2]{1,2,0:T(2,128)} %param.13) | copy-start | bytes 388
  230.0 3.0 %collective-permute-start.21 = (f32[2,128]{1,0:T(2,128)S(1)}, f32[2,128]{1,0:T(2,128)S(1)}, u32[]{:S(2)}, u32[]{:S(2)}) collective-permute-start(f32[2,128]{1,0:T(2,128)S(1)} %get-tuple-element.87), channel_id=1, source_target_pairs={{1,0},{3,2},{5,4},{7,6},{9,8},{11,10},{13,12},{15,14},{17,16},{19,... | collective-permute-start | bytes 3080 | tf_op jit(solution)/shard_map/ppermute | solution.py:691
  (18 other events, 93.3 us)

commit v6 on v5

--- a/solution.py
+++ b/solution.py
@@ -1,4 +1,5 @@
 import functools
+import math
 
 import jax
 import jax.numpy as jnp
@@ -34,7 +35,7 @@
 
 def attend(queries, keys, values, head_size, bias):
     rows, width = queries.shape
-    scale = head_size ** (-0.5)
+    scale = head_size ** (-0.5) * math.log2(math.e)
     pair = 2 * head_size
     lane = lax.broadcasted_iota(jnp.int32, (rows, pair), 1)
     first = lane < head_size
@@ -46,10 +47,10 @@
         stacked = jnp.concatenate(
             [jnp.where(first, both, none), jnp.where(first, none, both)], axis=0
         )
-        scores = dot_t(stacked, keys[:, at : at + pair]) * scale
+        scores = dot_t(stacked, keys[:, at : at + pair])
         if bias is not None:
             scores = scores + bias
-        weights = jnp.exp(scores - jnp.max(scores, axis=-1, keepdims=True)).astype(bf16)
+        weights = jnp.exp2((scores - jnp.max(scores, axis=-1, keepdims=True)) * scale).astype(bf16)
         summed = dot(weights, jnp.concatenate([values[:, at : at + pair], ones], axis=1))
         result = summed[:, :pair] / summed[:, pair:]
         mixed.append(jnp.where(first, result[:rows], result[rows:]).astype(bf16))
@@ -64,17 +65,20 @@
             pltpu.make_async_copy(ref.at[entry % SPAN], target, sem).start()
 
 
-def agent_kernel(list_length, first_step, codes, idle, head_size, table_ref, own_ref, *refs):
+def agent_kernel(
+    list_length, first_step, codes, idle, head_size, table_ref, own_ref, *refs
+):
     arrays = dict(zip(codes, refs))
     proj_ref, merge_ref, residual_ref, normed_ref, held_ref, sems = refs[len(codes) + idle :]
-    width = own_ref.shape[-1]
+    together, agents, width = own_ref.shape
     turn = pl.program_id(0)
-
-    def begin(step):
-        for j in range(list_length):
-            slot = step % 2
-            entry = table_ref[(first_step + step) * list_length + j]
-            fetch(entry, arrays, held_ref.at[slot, j], sems.at[slot, j])
+    pieces = [(s, j) for s in range(together) for j in range(list_length)]
+
+    def begin(turn):
+        slot = turn % 2
+        for n, (s, j) in enumerate(pieces):
+            entry = table_ref[(first_step + turn * together + s) * list_length + j]
+            fetch(entry, arrays, held_ref.at[slot, n], sems.at[slot, n])
 
     @pl.when(turn == 0)
     def _():
@@ -84,23 +88,33 @@
     def _():
         begin(turn + 1)
 
-    own = own_ref[0].astype(f32)
-    rows = [rms(own).astype(bf16)]
-    queries = dot(rows[0], proj_ref[:, :width]).astype(bf16)
     slot = turn % 2
-    for j in range(list_length):
-        pltpu.make_async_copy(refs[0].at[0], held_ref.at[slot, j], sems.at[slot, j]).wait()
-        rows.append(rms(held_ref[slot, j].astype(f32)).astype(bf16))
-    keyvals = dot(jnp.concatenate(rows, axis=0), proj_ref[:, width:]).astype(bf16)
-    mixed = attend(queries, keyvals[:, :width], keyvals[:, width:], head_size, None)
-    residual = own + dot(mixed, merge_ref[...])
-    residual_ref[0] = residual
-    normed_ref[0] = rms(residual).astype(bf16)
+    for n in range(len(pieces)):
+        pltpu.make_async_copy(refs[0].at[0], held_ref.at[slot, n], sems.at[slot, n]).wait()
+    own = own_ref[...].astype(f32).reshape(together * agents, width)
+    listed = held_ref[slot].astype(f32).reshape(len(pieces) * agents, width)
+    mine = rms(own).astype(bf16)
+    theirs = rms(listed).astype(bf16)
+    queries = dot(mine, proj_ref[:, :width]).astype(bf16)
+    near = dot(mine, proj_ref[:, width:]).astype(bf16)
+    away = dot(theirs, proj_ref[:, width:]).astype(bf16)
+    mixed = []
+    for s in range(together):
+        here = slice(s * agents, (s + 1) * agents)
+        there = slice(s * list_length * agents, (s + 1) * list_length * agents)
+        keyvals = jnp.concatenate([near[here], away[there]], axis=0)
+        mixed.append(
+            attend(queries[here], keyvals[:, :width], keyvals[:, width:], head_size, None)
+        )
+    residual = own + dot(jnp.concatenate(mixed, axis=0), merge_ref[...])
+    residual_ref[...] = residual.reshape(together, agents, width)
+    normed_ref[...] = rms(residual).astype(bf16).reshape(together, agents, width)
 
 
 def agent_stage(embedded, arrays, table, first_step, steps, list_length, proj, merge, after=()):
     _, agents, width = embedded.shape
-    piece = (1, agents, width)
+    together = math.gcd(steps, math.gcd(first_step, 2))
+    piece = (together, agents, width)
     whole = lambda i, w: (0, 0)
     flops = 2 * steps * agents * width * width * (4 + 2 * list_length + 2 * (1 + list_length))
     return pl.pallas_call(
@@ -109,14 +123,14 @@
         ),
         grid_spec=pltpu.PrefetchScalarGridSpec(
             num_scalar_prefetch=1,
-            grid=(steps,),
-            in_specs=[pl.BlockSpec(piece, lambda i, w: (first_step + i, 0, 0))]
-            + [pl.BlockSpec(memory_space=pl.ANY)] * (len(arrays) + len(after))
+            grid=(steps // together,),
+            in_specs=[pl.BlockSpec(piece, lambda i, w: (first_step // together + i, 0, 0))]
+            + [pl.BlockSpec(memory_space=pltpu.HBM)] * (len(arrays) + len(after))
             + [pl.BlockSpec(proj.shape, whole), pl.BlockSpec(merge.shape, whole)],
             out_specs=[pl.BlockSpec(piece, lambda i, w: (i, 0, 0))] * 2,
             scratch_shapes=[
-                pltpu.VMEM((2, list_length, agents, width), bf16),
-                pltpu.SemaphoreType.DMA((2, list_length)),
+                pltpu.VMEM((2, together * list_length, agents, width), bf16),
+                pltpu.SemaphoreType.DMA((2, together * list_length)),
             ],
         ),
         out_shape=[
@@ -171,8 +185,8 @@
     return pl.pallas_call(
         functools.partial(pack_kernel, tuple(arrays), tuple(parts), len(after)),
         in_specs=[pl.BlockSpec(memory_space=pltpu.SMEM)]
-        + [pl.BlockSpec(memory_space=pl.ANY)] * (len(arrays) + len(after)),
-        out_specs=[pl.BlockSpec(memory_space=pl.ANY)] * len(parts),
+        + [pl.BlockSpec(memory_space=pltpu.HBM)] * (len(arrays) + len(after)),
+        out_specs=[pl.BlockSpec(memory_space=pltpu.HBM)] * len(parts),
         out_shape=[jax.ShapeDtypeStruct((count,) + piece, bf16) for _, count, _ in parts],
         scratch_shapes=[
             pltpu.VMEM((slots,) + piece, bf16),
@@ -395,7 +409,7 @@
     e_base = [sum(outward[:b]) for b in range(len(outward))]
     y_base = [sum(outward) + sum(across[:b]) for b in range(len(across))]
     block = lambda c, r: c * ROWS + r
-    entry = lambda b, t, j: lists_ref[(b * steps + t) * list_length + j]
+    entry = lambda c, r, t, j: lists_ref[((c * ROWS + r) * steps + t) * list_length + j]
 
     def clear(n, _):
         out_ref[n] = -1
@@ -408,10 +422,10 @@
         for n in range(outward[1]):
             out_ref[e_base[1] + n] = codes["own"] * SPAN + starts[1] + n
 
-    def named(dest, t, source):
-        hit = entry(dest, t, 0) == source
+    def named(place, r, t, source):
+        hit = entry(place, r, t, 0) == source
         for j in range(1, list_length):
-            hit = hit | (entry(dest, t, j) == source)
+            hit = hit | (entry(place, r, t, j) == source)
         return hit
 
     def choose(sizes, ready):
@@ -448,9 +462,9 @@
                 def outer_piece(n, _, u=u, k=k):
                     t = starts[k] + n
                     source = block(mirror(u), sender)
-                    need = named(block(mirror(0), 0), t, source)
+                    need = named(0, 0, t, source)
                     for r in range(1, ROWS):
-                        need = need | named(block(mirror(0), r), t, source)
+                        need = need | named(0, r, t, source)
                     batch = choose(outward, OUTWARD_READY[u][k])
                     eloc[(turn * COLUMNS + u) * steps + t] = -1
 
@@ -477,7 +491,7 @@
 
                 def row_piece(n, _, u=u, k=k):
                     t = starts[k] + n
-                    need = named(block(column, 1 - sender), t, block(mirror(u), sender))
+                    need = named(me, 1 - sender, t, block(mirror(u), sender))
                     if u == 0:
                         lies = jnp.int32(codes["own"] * SPAN) + t
                         when = jnp.int32(0)
@@ -507,7 +521,7 @@
 
         def listed_piece(n, _, k=k):
             t = starts[k] + n // list_length
-            source = entry(block(column, row), t, n % list_length)
+            source = entry(me, row, t, n % list_length)
             u = mirror(source // ROWS)
             same = source % ROWS == row
             e = eloc[u * steps + t]
@@ -535,7 +549,7 @@
         lax.fori_loop(0, count * list_length, listed_piece, 0)
 
 
-def plan(lists_all, place, steps, list_length, chunks, outward, across):
+def plan(lists_near, place, steps, list_length, chunks, outward, across):
     smem = pl.BlockSpec(memory_space=pltpu.SMEM)
     slots = sum(outward) + sum(across)
     return pl.pallas_call(
@@ -553,7 +567,7 @@
             pltpu.SMEM((max(len(outward), len(across)),), jnp.int32),
         ],
         name="plan",
-    )(place, lists_all)
+    )(place, lists_near)
 
 
 def shared(value, axes):
@@ -602,13 +616,20 @@
         arrays[rows[n]] = send(packed[0], over)
         return packed
 
-    everyone = shared(lists.reshape(-1), "agent").reshape(-1)
-    begin = jnp.minimum(everyone[0], 0)
+    mine = lists.reshape(-1)
+    beside = send(mine, over)
+    pair = jnp.stack([jnp.where(index % ROWS == r, mine, beside) for r in range(ROWS)])
+    inward = column_pairs([(0, 1), (COLUMNS - 1, COLUMNS - 2)])
+    outer_pair = send(pair, inward)
+    column = index // ROWS
+    outer = (column == 0) | (column == COLUMNS - 1)
+    near = jnp.concatenate([jnp.where(outer, pair, outer_pair), pair], axis=0).reshape(-1)
+    begin = jnp.minimum(near[0], 0)
     first = lax.dynamic_slice_in_dim(embedded, begin, chunks[0], 0)
     arrays[edge[0]] = send(first, edges)
     arrays[swapped[0]] = send(first, swap)
     out_table, in_table, flag = plan(
-        everyone, place, steps, list_length, chunks, outward, across
+        near, place, steps, list_length, chunks, outward, across
     )
     (token,) = pack(out_table, pick([own]), [across_part(0)])
     arrays[rows[0]] = send(token, over)

time: 236 us -> 223 us (0.945)
  blocking collectives: 27.4 us -> 12 us
  Pallas kernels: 91.3 us -> 82.7 us
  starting transfers between devices: 32.7 us -> 39 us
  waiting for transfers between devices: 64.5 us -> 70.5 us
    all_to_all x2 -> x1, blocking collectives: 27.4 us -> 12 us  [shared(): return lax.all_to_all(rows, axes, split_axis=0, concat_axis=0, tiled=True)]
    pallas_call x3, Pallas kernels: 46.4 us -> 36.7 us  [agent_stage(): pl.pallas_call(functools.partial(agent_kernel, list_length, first_step, t...]
    ppermute x16 -> x18, starting transfers between devices: 27.2 us -> 33.7 us  [relay(): send = lambda value, pairs: lax.ppermute(value, 'agent', pairs)]
    ppermute x16 -> x18, waiting for transfers between devices: 61.7 us -> 67.7 us  [relay(): send = lambda value, pairs: lax.ppermute(value, 'agent', pairs)]
  transfers between devices with their start and end apart: 20 -> 22, of which waited for: 9 -> 11; matrix products, arithmetic and copies ran while one was open for 1% -> 1% of each run, Pallas kernels for 26% -> 23%
where the time goes in v6:
time: 223 us; the launch traced here: 221 us
  Pallas kernels  82.7 us (37%)
  waiting for transfers between devices  70.5 us (32%)
  starting transfers between devices  39 us (17%)
  local copies, waits for them, and re-layouts  13.7 us (6%)
  blocking collectives  12 us (5%)
    ppermute x18, waiting for transfers between devices, relay(): send = lambda value, pairs: lax.ppermute(value, 'agent', pairs)  67.7 us
    pallas_call x3, Pallas kernels, agent_stage(): pl.pallas_call(functools.partial(agent_kernel, list_length, first_step, t...  36.7 us
    ppermute x18, starting transfers between devices, relay(): send = lambda value, pairs: lax.ppermute(value, 'agent', pairs)  33.7 us
    pallas_call x1, Pallas kernels, time_stage(): pl.pallas_call(functools.partial(time_kernel, len(residuals), steps, tile...  18.8 us
    pallas_call x6, Pallas kernels, pack(): pl.pallas_call(functools.partial(pack_kernel, tuple(arrays), tuple(parts)...  17.7 us
    all_to_all x1, blocking collectives, shared(): return lax.all_to_all(rows, axes, split_axis=0, concat_axis=0, tiled=True)  12 us
    unnamed x61, local copies, waits for them, and re-layouts  10.5 us
    pallas_call x1, Pallas kernels, plan(): pl.pallas_call(functools.partial(plan_kernel, steps, list_length, chunks,...  8.07 us
  transfers between devices with their start and end apart: 22, of which 11 were waited for; matrix products, arithmetic and copies ran while one was open for 1% of the time, Pallas kernels for 23%

profile of v6, /device:TPU:0, one launch (start us, length us, event | category | flops | bytes accessed | tf_op | source)
XLA Modules:
  0.0 220.9 jit_solution(2454504809273114128)
XLA Ops:
  1.5 3.0 %collective-permute-start.2 = (s32[32]{0:T(128)S(1)}, s32[32]{0:T(128)S(1)}, u32[]{:S(2)}, u32[]{:S(2)}) collective-permute-start(s32[32]{0:T(128)S(1)} %reshape_squeeze.7), channel_id=1, source_target_pairs={{0,2},{2,0},{4,6},{6,4},{8,10},{10,8},{12,14},{14,12},{1,3},{3,1},... | collective-permute-start | bytes 392 | tf_op jit(solution)/shard_map/ppermute | solution.py:593
  4.5 1.5 collective-permute-done.2
  6.0 4.0 %collective-permute-start.3 = (s32[2,32]{1,0:T(2,128)S(1)}, s32[2,32]{1,0:T(2,128)S(1)}, u32[]{:S(2)}, u32[]{:S(2)}) collective-permute-start(s32[2,32]{1,0:T(2,128)S(1)} %pad_add_fusion.1), channel_id=1, source_target_pairs={{0,4},{2,6},{12,8},{14,10},{1,5},{3,7},{13,9},{15,11},{16,20},{18,... | collective-permute-start | bytes 776 | tf_op jit(solution)/shard_map/ppermute | solution.py:593
  11.5 2.3 %constant_dynamic-slice_fusion = bf16[8,128,512]{2,1,0:T(8,128)(2,1)} fusion(bf16[16,128,512]{2,1,0:T(8,128)(2,1)} %refs_0_.17, s32[]{:T(128)S(6)} %select_n.68), kind=kLoop, calls=%fused_computation.24 | loop fusion | bytes 2097156 | tf_op jit(solution)/shard_map/dynamic_slice | solution.py:628
  13.8 2.3 %collective-permute-start.4 = (bf16[8,128,512]{2,1,0:T(8,128)(2,1)}, bf16[8,128,512]{2,1,0:T(8,128)(2,1)S(1)}, u32[]{:S(2)}, u32[]{:S(2)}) collective-permute-start(bf16[8,128,512]{2,1,0:T(8,128)(2,1)} %constant_dynamic-slice_fusion), channel_id=1, source_target_pairs={{0,4},{2,6},{4,0},{6,2},{8,12},{10,14},{12,8},{14,10},{1,5},{3,7},... | collective-permute-start | bytes 3145736 | tf_op jit(solution)/shard_map/ppermute | solution.py:593
  17.4 8.1 %plan.1 = (s32[77]{0:T(128)}, s32[32]{0:T(128)}, s32[1]{0:T(128)}) custom-call(s32[2]{0:T(128)} %pad_add_fusion.2.place_ref, s32[128]{0:T(128)} %copy-done.31), custom_call_target="tpu_custom_call" | custom-call | tf_op jit(solution)/shard_map/plan/pallas_call | solution.py:555
  26.2 2.2 pack.6.refs_4_
  28.4 1.4 collective-permute-start.6
  30.4 12.0 %all_to_all.18 = s32[32,1,1]{2,1,0:T(1,128)S(1)} all-to-all(s32[32,1,1]{2,1,0:T(1,128)S(1)} %broadcast_in_dim.5), channel_id=1, replica_groups=mesh['groups'=2,'agent'=8,'tm'=2] {'groups','agent','tm'}, dimensions={0} | all-to-all | bytes 256 | tf_op jit(solution)/shard_map/all_to_all | solution.py:576
  44.1 6.4 %pack.7 = (bf16[8,128,512]{2,1,0:T(8,128)(2,1)S(1)}, bf16[8,128,512]{2,1,0:T(8,128)(2,1)S(1)}, bf16[8,128,512]{2,1,0:T(8,128)(2,1)S(1)}) custom-call(s32[77]{0:T(128)S(1)} %copy-done.12, bf16[16,128,512]{2,1,0:T(8,128)(2,1)} %refs_0_.17, bf16[8,128,512]{2,1,0:T(8,128)(2,1)S(1)} %collective-permute-done.4.refs_1_, bf16[8,128,512]{2,1,0:T(8,128)(2,1)} %copy-done.3, ...), custom_call_target="tpu_custom_call" | custom-call | bytes 65536 | tf_op jit(solution)/shard_map/pack/pallas_call | solution.py:185
  53.5 22.1 %collective-permute-done.7.refs_3_.refs_2_ = bf16[8,128,512]{2,1,0:T(8,128)(2,1)S(1)} collective-permute-done((bf16[8,128,512]{2,1,0:T(8,128)(2,1)S(1)}, bf16[8,128,512]{2,1,0:T(8,128)(2,1)S(1)}, u32[]{:S(2)}, u32[]{:S(2)}) %collective-permute-start.7) | collective-permute-done | bytes 1048608 | tf_op jit(solution)/shard_map/ppermute | solution.py:593
  79.1 2.9 %pack.8 = (bf16[8,128,512]{2,1,0:T(8,128)(2,1)S(1)}, bf16[8,128,512]{2,1,0:T(8,128)(2,1)S(1)}) custom-call(s32[77]{0:T(128)S(1)} %copy-done.12, bf16[16,128,512]{2,1,0:T(8,128)(2,1)S(1)} %copy-done.14, bf16[8,128,512]{2,1,0:T(8,128)(2,1)S(1)} %collective-permute-done.4.refs_1_, bf16[8,128,512]{2,1,0:T(8,128)(2,1)S(1)} %copy-done.4, ...), custom_call_target="tpu_custom_call" | custom-call | bytes 65536 | tf_op jit(solution)/shard_map/pack/pallas_call | solution.py:185
  82.0 5.4 %collective-permute-start.10 = (bf16[8,128,512]{2,1,0:T(8,128)(2,1)S(1)}, bf16[8,128,512]{2,1,0:T(8,128)(2,1)S(1)}, u32[]{:S(2)}, u32[]{:S(2)}) collective-permute-start(bf16[8,128,512]{2,1,0:T(8,128)(2,1)S(1)} %get-tuple-element.73), channel_id=1, source_target_pairs={{0,4},{2,6},{4,0},{6,2},{8,12},{10,14},{12,8},{14,10},{1,5},{3,7},... | collective-permute-start | bytes 3145736 | tf_op jit(solution)/shard_map/ppermute | solution.py:593
  88.6 18.4 %collective-permute-done.10.refs_5_.refs_3_ = bf16[8,128,512]{2,1,0:T(8,128)(2,1)S(1)} collective-permute-done((bf16[8,128,512]{2,1,0:T(8,128)(2,1)S(1)}, bf16[8,128,512]{2,1,0:T(8,128)(2,1)S(1)}, u32[]{:S(2)}, u32[]{:S(2)}) %collective-permute-start.10) | collective-permute-done | bytes 1048608 | tf_op jit(solution)/shard_map/ppermute | solution.py:593
  107.0 1.5 collective-permute-done.13.refs_8_.refs_9_.refs_10_
  109.5 2.2 %pack.9 = (bf16[7,128,512]{2,1,0:T(8,128)(2,1)S(1)}, bf16[8,128,512]{2,1,0:T(8,128)(2,1)S(1)}) custom-call(s32[77]{0:T(128)S(1)} %copy-done.12, bf16[16,128,512]{2,1,0:T(8,128)(2,1)S(1)} %copy-done.14, bf16[8,128,512]{2,1,0:T(8,128)(2,1)S(1)} %collective-permute-done.4.refs_1_, bf16[8,128,512]{2,1,0:T(8,128)(2,1)S(1)} %copy-done.4, ...), custom_call_target="tpu_custom_call" | custom-call | bytes 65536 | tf_op jit(solution)/shard_map/pack/pallas_call | solution.py:185
  111.7 5.9 %collective-permute-start.14 = (bf16[8,128,512]{2,1,0:T(8,128)(2,1)S(1)}, bf16[8,128,512]{2,1,0:T(8,128)(2,1)S(1)}, u32[]{:S(2)}, u32[]{:S(2)}) collective-permute-start(bf16[8,128,512]{2,1,0:T(8,128)(2,1)S(1)} %get-tuple-element.76), channel_id=1, source_target_pairs={{0,4},{2,6},{4,0},{6,2},{8,12},{10,14},{12,8},{14,10},{1,5},{3,7},... | collective-permute-start | bytes 3145736 | tf_op jit(solution)/shard_map/ppermute | solution.py:593
  117.6 2.5 %collective-permute-start.15 = (bf16[7,128,512]{2,1,0:T(8,128)(2,1)S(1)}, bf16[7,128,512]{2,1,0:T(8,128)(2,1)S(1)}, u32[]{:S(2)}, u32[]{:S(2)}) collective-permute-start(bf16[7,128,512]{2,1,0:T(8,128)(2,1)S(1)} %get-tuple-element.77.refs_11_), channel_id=1, source_target_pairs={{0,2},{2,0},{4,6},{6,4},{8,10},{10,8},{12,14},{14,12},{1,3},{3,1},... | collective-permute-start | bytes 2752520 | tf_op jit(solution)/shard_map/ppermute | solution.py:593
  120.9 17.4 %collective-permute-done.15.refs_10_.refs_11_ = bf16[7,128,512]{2,1,0:T(8,128)(2,1)S(1)} collective-permute-done((bf16[7,128,512]{2,1,0:T(8,128)(2,1)S(1)}, bf16[7,128,512]{2,1,0:T(8,128)(2,1)S(1)}, u32[]{:S(2)}, u32[]{:S(2)}) %collective-permute-start.15) | collective-permute-done | bytes 917536 | tf_op jit(solution)/shard_map/ppermute | solution.py:593
  138.3 1.3 collective-permute-done.14.refs_8_.refs_4_
  140.6 2.1 pack.10
  142.7 2.0 collective-permute-start.17
  145.4 18.3 %agent_stage.5 = (f32[8,128,512]{2,1,0:T(8,128)}, bf16[8,128,512]{2,1,0:T(8,128)(2,1)}) custom-call(s32[32]{0:T(128)S(1)} %copy-done.13, bf16[16,128,512]{2,1,0:T(8,128)(2,1)S(1)} %copy-done.14, bf16[16,128,512]{2,1,0:T(8,128)(2,1)S(1)} %copy-done.14, bf16[8,128,512]{2,1,0:T(8,128)(2,1)S(1)} %collective-permute-done.4.refs_1_, ...), custom_call_target="tpu_custom_call" | custom-call | flops 37580963840 | bytes 6291456 | tf_op jit(solution)/shard_map/agent_stage/pallas_call | solution.py:120
  163.6 1.4 collective-permute-start.20
  165.1 1.8 pack.11.refs_13_.refs_14_
  168.0 9.0 %agent_stage.6 = (f32[4,128,512]{2,1,0:T(8,128)S(1)}, bf16[4,128,512]{2,1,0:T(8,128)(2,1)}) custom-call(s32[32]{0:T(128)S(1)} %copy-done.13, bf16[16,128,512]{2,1,0:T(8,128)(2,1)S(1)} %copy-done.14, bf16[16,128,512]{2,1,0:T(8,128)(2,1)S(1)} %copy-done.14, bf16[8,128,512]{2,1,0:T(8,128)(2,1)} %copy-done.2, bf16[8,128,512]{2,1,0:T(8,128)(2,1)} %copy-done, ...), custom_call_target="tpu_custom_call" | custom-call | flops 18790481920 | bytes 3145728 | tf_op jit(solution)/shard_map/agent_stage/pallas_call | solution.py:120
  179.3 4.0 %collective-permute-done.19.refs_13_ = bf16[6,128,512]{2,1,0:T(8,128)(2,1)S(1)} collective-permute-done((bf16[6,128,512]{2,1,0:T(8,128)(2,1)S(1)}, bf16[6,128,512]{2,1,0:T(8,128)(2,1)S(1)}, u32[]{:S(2)}, u32[]{:S(2)}) %collective-permute-start.19) | collective-permute-done | bytes 786464 | tf_op jit(solution)/shard_map/ppermute | solution.py:593
  183.4 9.4 %agent_stage.7 = (f32[4,128,512]{2,1,0:T(8,128)}, bf16[4,128,512]{2,1,0:T(8,128)(2,1)}) custom-call(s32[32]{0:T(128)S(1)} %copy-done.13, bf16[16,128,512]{2,1,0:T(8,128)(2,1)S(1)} %copy-done.14, bf16[16,128,512]{2,1,0:T(8,128)(2,1)S(1)} %copy-done.14, bf16[8,128,512]{2,1,0:T(8,128)(2,1)} %copy-done.2, bf16[8,128,512]{2,1,0:T(8,128)(2,1)} %copy-done, ...), custom_call_target="tpu_custom_call" | custom-call | flops 18790481920 | bytes 3145728 | tf_op jit(solution)/shard_map/agent_stage/pallas_call | solution.py:120
  192.8 1.3 collective-permute-start.22
  194.1 1.7 collective-permute-done.22.refs_5_
  197.1 18.8 %time_stage.3 = (f32[16,128]{1,0:T(8,128)}, f32[2,128]{1,0:T(2,128)S(1)}) custom-call(s32[1]{0:T(128)} %bitcast.13.offset_ref, f32[8,128,512]{2,1,0:T(8,128)} %get-tuple-element.79.refs_12_.refs_14_.refs_0_, f32[4,128,512]{2,1,0:T(8,128)S(1)} %copy-done.7, f32[4,128,512]{2,1,0:T(8,128)S(1)} %copy-done.8, ...), custom_call_target="tpu_custom_call" | custom-call | tf_op jit(solution)/shard_map/time_stage/pallas_call | solution.py:299
  219.5 1.4 advantage_stage.3
  (98 shorter events, 25.2 us)
Async XLA Ops:
  1.5 4.6 %collective-permute-start.2 = (s32[32]{0:T(128)S(1)}, s32[32]{0:T(128)S(1)}, u32[]{:S(2)}, u32[]{:S(2)}) collective-permute-start(s32[32]{0:T(128)S(1)} %reshape_squeeze.7), channel_id=1, source_target_pairs={{0,2},{2,0},{4,6},{6,4},{8,10},{10,8},{12,14},{14,12},{1,3},{3,1},... | collective-permute-start | bytes 392 | tf_op jit(solution)/shard_map/ppermute | solution.py:593
  6.0 5.3 %collective-permute-start.3 = (s32[2,32]{1,0:T(2,128)S(1)}, s32[2,32]{1,0:T(2,128)S(1)}, u32[]{:S(2)}, u32[]{:S(2)}) collective-permute-start(s32[2,32]{1,0:T(2,128)S(1)} %pad_add_fusion.1), channel_id=1, source_target_pairs={{0,4},{2,6},{12,8},{14,10},{1,5},{3,7},{13,9},{15,11},{16,20},{18,... | collective-permute-start | bytes 776 | tf_op jit(solution)/shard_map/ppermute | solution.py:593
  13.8 29.3 %collective-permute-start.4 = (bf16[8,128,512]{2,1,0:T(8,128)(2,1)}, bf16[8,128,512]{2,1,0:T(8,128)(2,1)S(1)}, u32[]{:S(2)}, u32[]{:S(2)}) collective-permute-start(bf16[8,128,512]{2,1,0:T(8,128)(2,1)} %constant_dynamic-slice_fusion), channel_id=1, source_target_pairs={{0,4},{2,6},{4,0},{6,2},{8,12},{10,14},{12,8},{14,10},{1,5},{3,7},... | collective-permute-start | bytes 3145736 | tf_op jit(solution)/shard_map/ppermute | solution.py:593
  16.1 27.0 %collective-permute-start.5 = (bf16[8,128,512]{2,1,0:T(8,128)(2,1)}, bf16[8,128,512]{2,1,0:T(8,128)(2,1)S(1)}, u32[]{:S(2)}, u32[]{:S(2)}) collective-permute-start(bf16[8,128,512]{2,1,0:T(8,128)(2,1)} %constant_dynamic-slice_fusion), channel_id=1, source_target_pairs={{4,8},{6,10},{8,4},{10,6},{5,9},{7,11},{9,5},{11,7},{20,24},{22,26... | collective-permute-start | bytes 3145736 | tf_op jit(solution)/shard_map/ppermute | solution.py:593
  28.4 14.7 %collective-permute-start.6 = (bf16[4,128,512]{2,1,0:T(8,128)(2,1)S(1)}, bf16[4,128,512]{2,1,0:T(8,128)(2,1)S(1)}, u32[]{:S(2)}, u32[]{:S(2)}) collective-permute-start(bf16[4,128,512]{2,1,0:T(8,128)(2,1)S(1)} %pack.6.refs_4_), channel_id=1, source_target_pairs={{0,2},{2,0},{4,6},{6,4},{8,10},{10,8},{12,14},{14,12},{1,3},{3,1},... | collective-permute-start | bytes 1572872 | tf_op jit(solution)/shard_map/ppermute | solution.py:593
  43.1 121.9 %copy-start.2 = (bf16[8,128,512]{2,1,0:T(8,128)(2,1)}, bf16[8,128,512]{2,1,0:T(8,128)(2,1)S(1)}, u32[]{:S(2)}) copy-start(bf16[8,128,512]{2,1,0:T(8,128)(2,1)S(1)} %collective-permute-done.4.refs_1_) | copy-start | bytes 3145732
  44.1 33.8 %copy-start.14 = (bf16[16,128,512]{2,1,0:T(8,128)(2,1)S(1)}, bf16[16,128,512]{2,1,0:T(8,128)(2,1)}, u32[]{:S(2)}) copy-start(bf16[16,128,512]{2,1,0:T(8,128)(2,1)} %refs_0_.17) | copy-start | bytes 6291460
  50.6 25.3 %copy-start.9 = (bf16[8,128,512]{2,1,0:T(8,128)(2,1)}, bf16[8,128,512]{2,1,0:T(8,128)(2,1)S(1)}, u32[]{:S(2)}) copy-start(bf16[8,128,512]{2,1,0:T(8,128)(2,1)S(1)} %get-tuple-element.72.refs_6_) | copy-start | bytes 3145732
  50.6 25.0 %collective-permute-start.7 = (bf16[8,128,512]{2,1,0:T(8,128)(2,1)S(1)}, bf16[8,128,512]{2,1,0:T(8,128)(2,1)S(1)}, u32[]{:S(2)}, u32[]{:S(2)}) collective-permute-start(bf16[8,128,512]{2,1,0:T(8,128)(2,1)S(1)} %get-tuple-element.71), channel_id=1, source_target_pairs={{0,4},{2,6},{4,0},{6,2},{8,12},{10,14},{12,8},{14,10},{1,5},{3,7},... | collective-permute-start | bytes 3145736 | tf_op jit(solution)/shard_map/ppermute | solution.py:593
  51.3 24.6 %collective-permute-start.9 = (bf16[8,128,512]{2,1,0:T(8,128)(2,1)S(1)}, bf16[8,128,512]{2,1,0:T(8,128)(2,1)S(1)}, u32[]{:S(2)}, u32[]{:S(2)}) collective-permute-start(bf16[8,128,512]{2,1,0:T(8,128)(2,1)S(1)} %get-tuple-element.72.refs_6_), channel_id=1, source_target_pairs={{0,2},{2,0},{4,6},{6,4},{8,10},{10,8},{12,14},{14,12},{1,3},{3,1},... | collective-permute-start | bytes 3145736 | tf_op jit(solution)/shard_map/ppermute | solution.py:593
  52.0 23.8 %collective-permute-start.8 = (bf16[8,128,512]{2,1,0:T(8,128)(2,1)S(1)}, bf16[8,128,512]{2,1,0:T(8,128)(2,1)S(1)}, u32[]{:S(2)}, u32[]{:S(2)}) collective-permute-start(bf16[8,128,512]{2,1,0:T(8,128)(2,1)S(1)} %collective-permute-done.4.refs_1_), channel_id=1, source_target_pairs={{4,8},{6,10},{8,4},{10,6},{5,9},{7,11},{9,5},{11,7},{20,24},{22,26... | collective-permute-start | bytes 3145736 | tf_op jit(solution)/shard_map/ppermute | solution.py:593
  52.8 35.8 %collective-permute-start.11 = (bf16[8,128,512]{2,1,0:T(8,128)(2,1)S(1)}, bf16[8,128,512]{2,1,0:T(8,128)(2,1)S(1)}, u32[]{:S(2)}, u32[]{:S(2)}) collective-permute-start(bf16[8,128,512]{2,1,0:T(8,128)(2,1)S(1)} %get-tuple-element.74), channel_id=1, source_target_pairs={{4,8},{6,10},{8,4},{10,6},{5,9},{7,11},{9,5},{11,7},{20,24},{22,26... | collective-permute-start | bytes 3145736 | tf_op jit(solution)/shard_map/ppermute | solution.py:593
  75.5 32.9 %copy-start = (bf16[8,128,512]{2,1,0:T(8,128)(2,1)}, bf16[8,128,512]{2,1,0:T(8,128)(2,1)S(1)}, u32[]{:S(2)}) copy-start(bf16[8,128,512]{2,1,0:T(8,128)(2,1)S(1)} %collective-permute-done.7.refs_3_.refs_2_) | copy-start | bytes 3145732
  82.0 26.5 %copy-start.10 = (bf16[8,128,512]{2,1,0:T(8,128)(2,1)}, bf16[8,128,512]{2,1,0:T(8,128)(2,1)S(1)}, u32[]{:S(2)}) copy-start(bf16[8,128,512]{2,1,0:T(8,128)(2,1)S(1)} %get-tuple-element.75.refs_9_) | copy-start | bytes 3145732
  82.0 25.0 %collective-permute-start.10 = (bf16[8,128,512]{2,1,0:T(8,128)(2,1)S(1)}, bf16[8,128,512]{2,1,0:T(8,128)(2,1)S(1)}, u32[]{:S(2)}, u32[]{:S(2)}) collective-permute-start(bf16[8,128,512]{2,1,0:T(8,128)(2,1)S(1)} %get-tuple-element.73), channel_id=1, source_target_pairs={{0,4},{2,6},{4,0},{6,2},{8,12},{10,14},{12,8},{14,10},{1,5},{3,7},... | collective-permute-start | bytes 3145736 | tf_op jit(solution)/shard_map/ppermute | solution.py:593
  87.4 21.1 %collective-permute-start.13 = (bf16[8,128,512]{2,1,0:T(8,128)(2,1)S(1)}, bf16[8,128,512]{2,1,0:T(8,128)(2,1)S(1)}, u32[]{:S(2)}, u32[]{:S(2)}) collective-permute-start(bf16[8,128,512]{2,1,0:T(8,128)(2,1)S(1)} %get-tuple-element.75.refs_9_), channel_id=1, source_target_pairs={{0,2},{2,0},{4,6},{6,4},{8,10},{10,8},{12,14},{14,12},{1,3},{3,1},... | collective-permute-start | bytes 3145736 | tf_op jit(solution)/shard_map/ppermute | solution.py:593
  87.9 0.7 collective-permute-start.12
  88.6 19.9 %copy-start.17 = (bf16[8,128,512]{2,1,0:T(8,128)(2,1)}, bf16[8,128,512]{2,1,0:T(8,128)(2,1)S(1)}, u32[]{:S(2)}) copy-start(bf16[8,128,512]{2,1,0:T(8,128)(2,1)S(1)} %collective-permute-done.11.refs_6_) | copy-start | bytes 3145732
  111.7 27.9 %collective-permute-start.14 = (bf16[8,128,512]{2,1,0:T(8,128)(2,1)S(1)}, bf16[8,128,512]{2,1,0:T(8,128)(2,1)S(1)}, u32[]{:S(2)}, u32[]{:S(2)}) collective-permute-start(bf16[8,128,512]{2,1,0:T(8,128)(2,1)S(1)} %get-tuple-element.76), channel_id=1, source_target_pairs={{0,4},{2,6},{4,0},{6,2},{8,12},{10,14},{12,8},{14,10},{1,5},{3,7},... | collective-permute-start | bytes 3145736 | tf_op jit(solution)/shard_map/ppermute | solution.py:593
  117.6 20.7 %collective-permute-start.15 = (bf16[7,128,512]{2,1,0:T(8,128)(2,1)S(1)}, bf16[7,128,512]{2,1,0:T(8,128)(2,1)S(1)}, u32[]{:S(2)}, u32[]{:S(2)}) collective-permute-start(bf16[7,128,512]{2,1,0:T(8,128)(2,1)S(1)} %get-tuple-element.77.refs_11_), channel_id=1, source_target_pairs={{0,2},{2,0},{4,6},{6,4},{8,10},{10,8},{12,14},{14,12},{1,3},{3,1},... | collective-permute-start | bytes 2752520 | tf_op jit(solution)/shard_map/ppermute | solution.py:593
  120.1 25.3 %copy-start.1 = (bf16[8,128,512]{2,1,0:T(8,128)(2,1)S(1)}, bf16[8,128,512]{2,1,0:T(8,128)(2,1)}, u32[]{:S(2)}) copy-start(bf16[8,128,512]{2,1,0:T(8,128)(2,1)} %copy-done) | copy-start | bytes 3145732
  120.1 25.3 %copy-start.13 = (s32[32]{0:T(128)S(1)}, s32[32]{0:T(128)}, u32[]{:S(2)}) copy-start(s32[32]{0:T(128)} %get-tuple-element.69.table_ref) | copy-start | bytes 388
  120.1 25.3 %copy-start.33 = (bf16[512,512]{1,0:T(8,128)(2,1)S(1)}, bf16[512,512]{1,0:T(8,128)(2,1)}, u32[]{:S(2)}) copy-start(bf16[512,512]{1,0:T(8,128)(2,1)} %refs_17_.1) | copy-start | bytes 1572868
  120.1 0.8 collective-permute-start.16
  142.7 22.3 %collective-permute-start.17 = (bf16[6,128,512]{2,1,0:T(8,128)(2,1)S(1)}, bf16[6,128,512]{2,1,0:T(8,128)(2,1)S(1)}, u32[]{:S(2)}, u32[]{:S(2)}) collective-permute-start(bf16[6,128,512]{2,1,0:T(8,128)(2,1)S(1)} %get-tuple-element.80), channel_id=1, source_target_pairs={{0,4},{2,6},{4,0},{6,2},{8,12},{10,14},{12,8},{14,10},{1,5},{3,7},... | collective-permute-start | bytes 2359304 | tf_op jit(solution)/shard_map/ppermute | solution.py:593
  144.7 20.3 %collective-permute-start.18 = (bf16[6,128,512]{2,1,0:T(8,128)(2,1)S(1)}, bf16[6,128,512]{2,1,0:T(8,128)(2,1)S(1)}, u32[]{:S(2)}, u32[]{:S(2)}) collective-permute-start(bf16[6,128,512]{2,1,0:T(8,128)(2,1)S(1)} %get-tuple-element.78.refs_11_), channel_id=1, source_target_pairs={{0,2},{2,0},{4,6},{6,4},{8,10},{10,8},{12,14},{14,12},{1,3},{3,1},... | collective-permute-start | bytes 2359304 | tf_op jit(solution)/shard_map/ppermute | solution.py:593
  163.6 30.5 %collective-permute-start.20 = (bf16[8,128,512]{2,1,0:T(8,128)(2,1)}, bf16[8,128,512]{2,1,0:T(8,128)(2,1)S(1)}, u32[]{:S(2)}, u32[]{:S(2)}) collective-permute-start(bf16[8,128,512]{2,1,0:T(8,128)(2,1)} %get-tuple-element.83), channel_id=1, source_target_pairs={{0,1},{2,3},{4,5},{6,7},{8,9},{10,11},{12,13},{14,15},{16,17},{18,... | collective-permute-start | bytes 3145736 | tf_op jit(solution)/shard_map/ppermute | solution.py:695
  166.9 16.4 %collective-permute-start.19 = (bf16[6,128,512]{2,1,0:T(8,128)(2,1)S(1)}, bf16[6,128,512]{2,1,0:T(8,128)(2,1)S(1)}, u32[]{:S(2)}, u32[]{:S(2)}) collective-permute-start(bf16[6,128,512]{2,1,0:T(8,128)(2,1)S(1)} %pack.11.refs_13_.refs_14_), channel_id=1, source_target_pairs={{0,2},{2,0},{4,6},{6,4},{8,10},{10,8},{12,14},{14,12},{1,3},{3,1},... | collective-permute-start | bytes 2359304 | tf_op jit(solution)/shard_map/ppermute | solution.py:593
  178.0 16.1 %collective-permute-start.21 = (bf16[4,128,512]{2,1,0:T(8,128)(2,1)}, bf16[4,128,512]{2,1,0:T(8,128)(2,1)S(1)}, u32[]{:S(2)}, u32[]{:S(2)}) collective-permute-start(bf16[4,128,512]{2,1,0:T(8,128)(2,1)} %get-tuple-element.84), channel_id=1, source_target_pairs={{0,1},{2,3},{4,5},{6,7},{8,9},{10,11},{12,13},{14,15},{16,17},{18,... | collective-permute-start | bytes 1572872 | tf_op jit(solution)/shard_map/ppermute | solution.py:695
  192.8 3.0 %collective-permute-start.22 = (bf16[4,128,512]{2,1,0:T(8,128)(2,1)}, bf16[4,128,512]{2,1,0:T(8,128)(2,1)S(1)}, u32[]{:S(2)}, u32[]{:S(2)}) collective-permute-start(bf16[4,128,512]{2,1,0:T(8,128)(2,1)} %get-tuple-element.85), channel_id=1, source_target_pairs={{0,1},{2,3},{4,5},{6,7},{8,9},{10,11},{12,13},{14,15},{16,17},{18,... | collective-permute-start | bytes 1572872 | tf_op jit(solution)/shard_map/ppermute | solution.py:695
  197.1 23.8 %copy-start.28 = (s32[1,16,2]{1,2,0:T(2,128)S(1)}, s32[1,16,2]{1,2,0:T(2,128)}, u32[]{:S(2)}) copy-start(s32[1,16,2]{1,2,0:T(2,128)} %param.13) | copy-start | bytes 388
  215.9 3.0 %collective-permute-start.23 = (f32[2,128]{1,0:T(2,128)S(1)}, f32[2,128]{1,0:T(2,128)S(1)}, u32[]{:S(2)}, u32[]{:S(2)}) collective-permute-start(f32[2,128]{1,0:T(2,128)S(1)} %get-tuple-element.87), channel_id=1, source_target_pairs={{1,0},{3,2},{5,4},{7,6},{9,8},{11,10},{13,12},{15,14},{17,16},{19,... | collective-permute-start | bytes 3080 | tf_op jit(solution)/shard_map/ppermute | solution.py:712
  (20 other events, 120.8 us)
